TPU v7x, 512 devices: a whole 4x8x8 slice. The times are simulated.
512 devices in a mesh: sec: 128 (over y, z, core), op: 4 (over x).
Axes of the slice: x: 4, y: 8, z: 8, core: 2. Of those that a mesh axis runs over, the one named last changes fastest.
Arguments:
- trial_state: bfloat16 [2, 8192, 8192], P(None, 'sec'), may hold values from -6 to 6
- left_operators: bfloat16 [24, 8192, 64], P('op', 'sec'), may hold values from -0.75 to 0.75
- right_operators: bfloat16 [24, 8192, 64], P('op', 'sec'), may hold values from -0.15625 to 0.15625
- left_coupling: int32 [24, 128], P('op', 'sec'), may hold values from -2 to 2
- right_coupling: int32 [24, 128], P('op', 'sec'), may hold values from -2 to 2
- left_charge: int32 [128], replicated, may hold values from 0 to 6
- right_charge: int32 [128], replicated, may hold values from 0 to 6
Outputs:
- sigma_columns: bfloat16 [2, 8192, 8192], P(None, 'sec', 'op')
All inputs are finite; a program needn't handle non-finite values.
Results may differ from a plain program's by a relative error of at most 0.0049.
Values may be sent and summed in bfloat16 or wider, within the bound.
No kernel may reach another device: no remote copies, remote signals or barrier semaphores. Data moves between devices by JAX's collectives and lax.ppermute only.
A program may use at most 128 MiB of HBM per device.

v0:
```python
import jax
import jax.numpy as jnp
from jax import lax
from jax.sharding import PartitionSpec as P

target_charge = 6


def sector_mask(own_charge, other_charges, block):
    allowed = (jnp.abs(own_charge + other_charges - target_charge) <= 1).astype(jnp.bfloat16)
    return jnp.repeat(allowed, block)


def body(
    trial_state,
    left_operators,
    right_operators,
    left_coupling,
    right_coupling,
    left_charge,
    right_charge,
):
    block = left_operators.shape[1]
    terms_here = left_operators.shape[0]
    sectors = left_charge.shape[0]
    states = block * sectors
    vectors = trial_state.shape[0]
    position = lax.axis_index("sec")
    own_left = lax.dynamic_slice_in_dim(left_charge, position, 1)
    own_right = lax.dynamic_slice_in_dim(right_charge, position, 1)
    column_mask = sector_mask(own_left, right_charge, block)
    masked = trial_state * column_mask[None, None, :]
    left_scaled = left_operators * left_coupling[:, :, None].astype(jnp.bfloat16)
    right_scaled = right_operators * right_coupling[:, :, None].astype(jnp.bfloat16)
    products = jnp.einsum(
        "tik,vkj->tjvi", left_scaled, masked, preferred_element_type=jnp.float32
    ).astype(jnp.bfloat16)
    products = products.reshape(terms_here, states, vectors * block)
    arrived = lax.all_to_all(products, "sec", split_axis=1, concat_axis=2, tiled=True)
    arrived = arrived.reshape(terms_here, block, sectors, vectors, block)
    combined = jnp.einsum(
        "tjk,tkavi->vjai", right_scaled, arrived, preferred_element_type=jnp.float32
    )
    combined = combined.reshape(vectors, block, states)
    row_mask = sector_mask(own_right, left_charge, block).astype(jnp.float32)
    combined = combined * row_mask[None, None, :]
    return lax.psum_scatter(combined, "op", scatter_dimension=2, tiled=True).astype(jnp.bfloat16)


def solution(mesh):
    return jax.shard_map(
        body,
        mesh=mesh,
        in_specs=(
            P(None, "sec", None),
            P("op", "sec", None),
            P("op", "sec", None),
            P("op", "sec"),
            P("op", "sec"),
            P(),
            P(),
        ),
        out_specs=P(None, "sec", "op"),
        check_vma=False,
    )
```

profile of v0, /device:TPU:1, one launch (start us, length us, event | category | flops | bytes accessed | tf_op | source)
XLA Modules:
  0.0 730.5 jit_solution(17220245945187173203)
XLA Ops:
  6.5 1.2 dynamic_slice.6
  7.8 1.3 compare_convert_fusion.1
  9.1 0.1 broadcast_in_dim.4
  9.2 0.1 mul.34
  9.3 0.7 convert_bitcast_fusion.1
  9.9 5.0 fusion
  15.0 5.1 copy.12
  20.1 21.1 %copy.13 = bf16[6,8192,128]{2,0,1:T(8,128)(2,1)} copy(bf16[6,8192,128]{1,2,0:T(8,128)(2,1)} %bitcast.35) | data formatting | bytes 25165824 | tf_op jit(solution)/shard_map/reshape | solution.py:38
  41.2 0.0 copy-start.1
  41.2 0.0 copy-start.2
  41.2 0.0 copy-start.3
  41.2 19.0 %all-to-all-start = ((bf16[6,8192,128]{2,0,1:T(8,128)(2,1)}), bf16[6,8192,128]{2,0,1:T(8,128)(2,1)}, u32[]{:S(2)}, u32[]{:S(2)}) async-start(bf16[6,8192,128]{2,0,1:T(8,128)(2,1)} %copy.13), calls=%async_computation | async-start | bytes 33554432 | tf_op jit(solution)/shard_map/all_to_all | solution.py:39
  60.2 0.2 reduce-scatter.2.cloned.1.call-start
  60.4 0.0 copy-done.1
  60.4 0.6 dynamic_slice.7
  61.0 0.0 copy-done.2
  61.0 0.7 fusion.10
  61.7 0.1 broadcast_in_dim.10
  61.8 0.1 convert_element_type.57
  61.8 0.0 copy-done.3
  61.9 486.2 %all-to-all-done = bf16[6,8192,128]{2,0,1:T(8,128)(2,1)} async-done(((bf16[6,8192,128]{2,0,1:T(8,128)(2,1)}), bf16[6,8192,128]{2,0,1:T(8,128)(2,1)}, u32[]{:S(2)}, u32[]{:S(2)}) %all-to-all-start) | async-done | bytes 12582944 | tf_op jit(solution)/shard_map/all_to_all | solution.py:39
  548.1 0.0 copy-start
  548.1 26.2 %copy.15 = bf16[6,64,128,128]{2,1,0,3:T(8,128)(2,1)} copy(bf16[6,64,128,128]{3,0,1,2:T(8,128)(2,1)} %bitcast.9) | data formatting | bytes 25165824 | tf_op jit(solution)/shard_map/all_to_all | solution.py:39
  574.2 0.0 copy-done
  574.2 9.0 %convolution_bitcast_fusion = f32[2,64,128,64]{2,1,3,0:T(8,128)} fusion(bf16[6,64,128,2,64]{2,1,0,4,3:T(8,128)(2,1)} %bitcast.34, bf16[6,64,64]{2,1,0:T(8,128)(2,1)S(1)} %copy-done, bf16[6]{0:T(256)(128)(2,1)S(1)} %convert_bitcast_fusion), kind=kOutput, calls=%fused_computation.2 | convolution fusion | flops 805404672 | bytes 16826380 | tf_op jit(solution)/shard_map/tjk,tkavi->vjai/dot_general | solution.py:41
  583.2 7.0 copy.16
  590.2 7.9 %reshape.36 = f32[2,64,8192]{2,1,0:T(8,128)} reshape(f32[2,64,128,64]{3,2,1,0:T(8,128)} %copy.16) | data formatting | bytes 8388608 | tf_op jit(solution)/shard_map/reshape | solution.py:44
  598.1 4.6 broadcast_multiply_fusion
  602.7 0.0 reduce-scatter.2.cloned.1.call-update
  602.7 118.8 %reduce-scatter.2.cloned.1.call-done = f32[2,64,2048]{2,1,0:T(8,128)} async-done(((f32[2,64,8192]{2,1,0:T(8,128)}), f32[2,64,2048]{2,1,0:T(8,128)}) %reduce-scatter.2.cloned.1.call-update) | async-done | bytes 1048592 | tf_op jit(solution)/shard_map/reduce_scatter | solution.py:47
  721.6 2.1 convert_element_type.58
  (1 shorter events, 0.0 us)
Async XLA Ops:
  41.2 19.3 %copy-start.1 = (s32[128]{0:T(128)S(1)}, s32[128]{0:T(128)}, u32[]{:S(2)}) copy-start(s32[128]{0:T(128)} %param.13) | copy-start | bytes 1540
  41.2 19.9 %copy-start.2 = (s32[128]{0:T(128)S(1)}, s32[128]{0:T(128)}, u32[]{:S(2)}) copy-start(s32[128]{0:T(128)} %param.12) | copy-start | bytes 1540
  41.2 20.7 %copy-start.3 = (s32[6,1]{0,1:T(1,128)S(1)}, s32[6,1]{0,1:T(1,128)}, u32[]{:S(2)}) copy-start(s32[6,1]{0,1:T(1,128)} %param.11) | copy-start | bytes 76
  41.2 506.9 %all-to-all-start = ((bf16[6,8192,128]{2,0,1:T(8,128)(2,1)}), bf16[6,8192,128]{2,0,1:T(8,128)(2,1)}, u32[]{:S(2)}, u32[]{:S(2)}) async-start(bf16[6,8192,128]{2,0,1:T(8,128)(2,1)} %copy.13), calls=%async_computation | async-start | bytes 33554432 | tf_op jit(solution)/shard_map/all_to_all | solution.py:39
  60.2 661.4 %reduce-scatter.2.cloned.1.call-start = ((), (), s32[]{:S(2)}) async-start(), calls=%async_computation.2 | async-start | bytes 5242880 | tf_op jit(solution)/shard_map/reduce_scatter | solution.py:47
  548.1 26.2 %copy-start = (bf16[6,64,64]{2,1,0:T(8,128)(2,1)S(1)}, bf16[6,64,64]{2,1,0:T(8,128)(2,1)}, u32[]{:S(2)}) copy-start(bf16[6,64,64]{2,1,0:T(8,128)(2,1)} %param.9) | copy-start | bytes 147460
Sparse Core Ops, SparseCore 0:
  602.8 118.6 reduce-scatter.1
where the time goes:
time: 732 us; the launch traced here: 730 us
  waiting for transfers between devices  605 us (83%)
  local copies, waits for them, and re-layouts  69.4 us (9%)
  starting transfers between devices  19.2 us (3%)
  matrix products  14 us (2%)
  between operations  13.5 us (2%)
  other arithmetic  9.28 us (1%)
    all_to_all x1, waiting for transfers between devices, body(): lax.all_to_all(products, 'sec', split_axis=1, concat_axis=2, tiled=True)  486 us
    reduce_scatter x1, waiting for transfers between devices, body(): lax.psum_scatter(combined, 'op', scatter_dimension=2, tiled=True)  119 us
    all_to_all x1, local copies, waits for them, and re-layouts, body(): lax.all_to_all(products, 'sec', split_axis=1, concat_axis=2, tiled=True)  26.2 us
    reshape x1, local copies, waits for them, and re-layouts, body(): products = products.reshape(terms_here, states, vectors * block)  21.1 us
    all_to_all x1, starting transfers between devices, body(): lax.all_to_all(products, 'sec', split_axis=1, concat_axis=2, tiled=True)  19 us
  transfers between devices with their start and end apart: 2, of which 2 were waited for; matrix products, arithmetic and copies ran while one was open for 0% of the time, Pallas kernels for 0%

commit v1 on v0

v1 whole, which is shorter than its diff:
```python
import jax
import jax.numpy as jnp
import numpy as np
from jax import lax
from jax.experimental import pallas as pl
from jax.experimental.pallas import tpu as pltpu
from jax.sharding import Mesh, PartitionSpec as P

target_charge = 6
XDIM, YH, YL, ZH, ZL, CORE = 4, 4, 2, 4, 2, 2
SEC = ("yh", "yl", "zh", "zl", "core")
FAR = ("yh", "yl", "zh")
NEAR = ("zl", "core")
NT = (((1,), (1,)), ((), ()))
VMEM = 48 * 1024 * 1024


def same_block(rows, lanes, block):
    row = lax.broadcasted_iota(jnp.int32, (rows, lanes), 0) // block
    lane = lax.broadcasted_iota(jnp.int32, (rows, lanes), 1) // block
    return row == lane


def block_diagonal(piece, mask):
    copies = mask.shape[0] // piece.shape[0]
    stacked = jnp.concatenate([piece] * copies, axis=0)
    return jnp.where(mask, stacked, jnp.zeros_like(stacked))


def right_kernel(block, terms, recv_ref, half_ref):
    v, g = pl.program_id(0), pl.program_id(1)
    half = block // 2
    group = 4 * block
    rows = []
    for a in range(4):
        for h in range(2):
            start = pl.multiple_of((g * 4 + a) * half, half)
            rows.append(recv_ref[v * 2 + h, pl.ds(start, half), :])
    state = jnp.concatenate(rows, axis=0)
    mask = same_block(group, group, block)
    per = terms // XDIM
    for t in range(terms):
        at = 8 * half + (t % per) * block
        right = block_diagonal(recv_ref[t // per, at:at + block, :], mask)
        out = lax.dot_general(right, state, NT, preferred_element_type=jnp.float32)
        half_ref[0, 0, :, t * group:(t + 1) * group] = out.astype(half_ref.dtype)


def left_kernel(block, terms, half_ref, left_ref, out_ref, diag_ref):
    group = 4 * block
    per = terms // XDIM

    @pl.when(pl.program_id(1) == 0)
    def _():
        mask = same_block(group, group, block)
        for t in range(terms):
            at = (t % per) * block
            diag_ref[:, t * group:(t + 1) * group] = block_diagonal(
                left_ref[t // per, 0, at:at + block, :], mask
            )

    out = lax.dot_general(half_ref[0, 0], diag_ref[...], NT, preferred_element_type=jnp.float32)
    out_ref[...] = out.reshape(4, 1, block, group).astype(out_ref.dtype)


def merge_kernel(block, in_ref, out_ref):
    wide = 2 * block
    for m in range(in_ref.shape[3] // wide):
        for s in range(2):
            low = in_ref[2 * s, 0, :, m * wide:(m + 1) * wide]
            high = in_ref[2 * s + 1, 0, :, m * wide:(m + 1) * wide]
            even = jnp.concatenate([low[:, :block], high[:, :block]], axis=1)
            odd = jnp.concatenate([low[:, block:], high[:, block:]], axis=1)
            at = (2 * m * 2 + s) * wide
            out_ref[0, :, at:at + wide] = even
            at = ((2 * m + 1) * 2 + s) * wide
            out_ref[0, :, at:at + wide] = odd


def body(
    trial_state,
    left_operators,
    right_operators,
    left_coupling,
    right_coupling,
    left_charge,
    right_charge,
):
    vectors, block, states = trial_state.shape
    here = left_operators.shape[0]
    terms = here * XDIM
    group = 4 * block
    half = block // 2
    plane = lax.axis_index("op")
    position = lax.axis_index(SEC)

    left = left_operators * left_coupling[:, :, None].astype(jnp.bfloat16)
    left = left.reshape(here // 2, 2, block, block).transpose(0, 2, 1, 3)
    left = left.reshape(here // 2 * block, 2 * block)
    swap = [(q * XDIM + x, x * XDIM + q) for q in range(YH) for x in range(XDIM)]
    left = lax.ppermute(left, ("yh", "op"), swap)
    left = jnp.broadcast_to(left[None], (ZH,) + left.shape)
    left = lax.all_to_all(left, "zh", 0, 0, tiled=True)
    left = left.reshape(ZH, here // 2, block, 2, block).transpose(1, 3, 2, 0, 4)
    left = left.reshape(here * block, group)
    left = lax.all_gather(left, ("yh", "yl"), tiled=True)
    left = left.reshape(YH, YL, here * block, group)

    right = right_operators * right_coupling[:, :, None].astype(jnp.bfloat16)
    other = lax.ppermute(right, "core", [(0, 1), (1, 0)])
    first = lax.axis_index("core") == 0
    right = jnp.concatenate(
        [jnp.where(first, right, other), jnp.where(first, other, right)], axis=2
    ).reshape(here * block, 2 * block)
    other = lax.ppermute(right, "zl", [(0, 1), (1, 0)])
    first = lax.axis_index("zl") == 0
    right = jnp.concatenate(
        [jnp.where(first, right, other), jnp.where(first, other, right)], axis=1
    )

    own = lax.dynamic_slice_in_dim(left_charge, position, 1)
    allowed = (jnp.abs(own + right_charge - target_charge) <= 1).astype(jnp.bfloat16)
    quarter = lax.dynamic_slice(
        trial_state, (plane // 2, (plane % 2) * half, 0), (1, half, states)
    )[0]
    quarter = quarter * jnp.repeat(allowed, block)[None, :]
    quarter = quarter.reshape(half, states // group, group).transpose(1, 0, 2)
    quarter = lax.all_to_all(quarter, FAR, 0, 0, tiled=True)
    quarter = quarter.reshape(YH, YL * ZH * half, group)
    packed = jnp.concatenate(
        [quarter, jnp.broadcast_to(right[None], (XDIM,) + right.shape)], axis=1
    )
    packed = lax.all_to_all(packed, "op", 0, 0, tiled=True)

    half_done = pl.pallas_call(
        lambda *refs: right_kernel(block, terms, *refs),
        grid=(vectors, YL),
        in_specs=[pl.BlockSpec(packed.shape, lambda v, g: (0, 0, 0))],
        out_specs=pl.BlockSpec((1, 1, group, terms * group), lambda v, g: (v, g, 0, 0)),
        out_shape=jax.ShapeDtypeStruct((vectors, YL, group, terms * group), jnp.bfloat16),
        compiler_params=pltpu.CompilerParams(vmem_limit_bytes=VMEM),
        name="right_products",
    )(packed)

    partial = pl.pallas_call(
        lambda *refs: left_kernel(block, terms, *refs),
        grid=(YL, vectors),
        in_specs=[
            pl.BlockSpec((1, 1, group, terms * group), lambda g, v: (v, g, 0, 0)),
            pl.BlockSpec((YH, 1, here * block, group), lambda g, v: (0, g, 0, 0)),
        ],
        out_specs=pl.BlockSpec((4, 1, block, group), lambda g, v: (0, v, 0, g)),
        out_shape=jax.ShapeDtypeStruct((4, vectors, block, YL * group), jnp.bfloat16),
        scratch_shapes=[pltpu.VMEM((group, terms * group), jnp.bfloat16)],
        compiler_params=pltpu.CompilerParams(vmem_limit_bytes=VMEM),
        name="left_products",
    )(half_done, left)

    partial = lax.all_to_all(partial, NEAR, 0, 0, tiled=True)
    return pl.pallas_call(
        lambda *refs: merge_kernel(block, *refs),
        grid=(vectors,),
        in_specs=[pl.BlockSpec((4, 1, block, YL * group), lambda v: (0, v, 0, 0))],
        out_specs=pl.BlockSpec((1, block, 4 * YL * group), lambda v: (v, 0, 0)),
        out_shape=jax.ShapeDtypeStruct((vectors, block, 4 * YL * group), jnp.bfloat16),
        name="merge_sectors",
    )(partial)


def solution(mesh):
    fine = Mesh(mesh.devices.reshape(YH, YL, ZH, ZL, CORE, XDIM), SEC + ("op",))
    return jax.shard_map(
        body,
        mesh=fine,
        in_specs=(
            P(None, SEC, None),
            P("op", SEC, None),
            P("op", SEC, None),
            P("op", SEC),
            P("op", SEC),
            P(),
            P(),
        ),
        out_specs=P(None, SEC, "op"),
        check_vma=False,
    )
```

time: 732 us -> 127 us (0.17)
  waiting for transfers between devices: 605 us -> 16.6 us
  local copies, waits for them, and re-layouts: 69.4 us -> 5.95 us
  blocking collectives: 0 us -> 33 us
  starting transfers between devices: 19.2 us -> 38.6 us
  Pallas kernels: 0 us -> 16 us
  matrix products: 14 us -> 0 us
    all_to_all x1 -> x2, waiting for transfers between devices: 486 us -> 9.13 us  [the longest x1 7.05 us: body(): left = lax.all_to_all(left, 'zh', 0, 0, tiled=True)]
    reduce_scatter x1 -> x0, waiting for transfers between devices: 119 us -> none  [body(): lax.psum_scatter(combined, 'op', scatter_dimension=2, tiled=True)]
    all_to_all x0 -> x2, blocking collectives: none -> 33 us  [the longest x1 19.4 us: body(): partial = lax.all_to_all(partial, NEAR, 0, 0, tiled=True)]
    reshape x2 -> x4, local copies, waits for them, and re-layouts: 29 us -> 1.35 us  [the longest x1 0.96 us: body(): left = left.reshape(here * block, group)]
    all_to_all x1 -> x0, local copies, waits for them, and re-layouts: 26.2 us -> none  [body(): lax.all_to_all(products, 'sec', split_axis=1, concat_axis=2, tiled=True)]
    pallas_call x0 -> x3, Pallas kernels: none -> 16 us  [the longest x1 7.67 us: body(): pl.pallas_call(lambda *refs: left_kernel(block, terms, *refs), grid=(YL,...]
    dot_general x2 -> x0, matrix products: 14 us -> none  [the longest x1 9 us: body(): jnp.einsum('tjk,tkavi->vjai', right_scaled, arrived, preferred_element_ty...]
    all_to_all x1 -> x2, starting transfers between devices: 19 us -> 29.4 us  [the longest x1 18.6 us: body(): quarter = lax.all_to_all(quarter, FAR, 0, 0, tiled=True)]
  transfers between devices with their start and end apart: 2 -> 6, of which waited for: 2 -> 4; matrix products, arithmetic and copies ran while one was open for 0% -> 3% of each run, Pallas kernels for 0% -> 5%
where the time goes in v1:
time: 127 us
  starting transfers between devices  38.6 us (30%)
  blocking collectives  33 us (26%)
  waiting for transfers between devices  16.6 us (13%)
  Pallas kernels  16 us (13%)
  between operations  13.7 us (11%)
  local copies, waits for them, and re-layouts  5.95 us (5%)
  other arithmetic  2.8 us (2%)
    all_to_all x1, blocking collectives, body(): partial = lax.all_to_all(partial, NEAR, 0, 0, tiled=True)  19.4 us
    all_to_all x1, starting transfers between devices, body(): quarter = lax.all_to_all(quarter, FAR, 0, 0, tiled=True)  18.6 us
    all_to_all x1, blocking collectives, body(): packed = lax.all_to_all(packed, 'op', 0, 0, tiled=True)  13.6 us
    all_to_all x1, starting transfers between devices, body(): left = lax.all_to_all(left, 'zh', 0, 0, tiled=True)  10.8 us
    pallas_call x1, Pallas kernels, body(): pl.pallas_call(lambda *refs: left_kernel(block, terms, *refs), grid=(YL,...  7.67 us
    all_to_all x1, waiting for transfers between devices, body(): left = lax.all_to_all(left, 'zh', 0, 0, tiled=True)  7.05 us
    ppermute x1, waiting for transfers between devices, body(): other = lax.ppermute(right, 'zl', [(0, 1), (1, 0)])  6.5 us
    pallas_call x1, Pallas kernels, body(): pl.pallas_call(lambda *refs: right_kernel(block, terms, *refs), grid=(vec...  6.42 us
  transfers between devices with their start and end apart: 6, of which 4 were waited for; matrix products, arithmetic and copies ran while one was open for 3% of the time, Pallas kernels for 5%

profile of v1, /device:TPU:1, one launch (start us, length us, event | category | flops | bytes accessed | tf_op | source)
XLA Modules:
  0.0 126.6 jit_solution(10362971225137442295)
XLA Ops:
  6.5 0.0 copy-start
  6.5 0.0 copy-start.3
  6.5 0.8 convert_bitcast_fusion
  7.3 1.0 broadcast_multiply_fusion
  8.3 0.1 copy.18
  8.4 0.0 copy-start.4
  8.4 0.1 reshape.53
  8.5 0.7 collective-permute-start.2
  9.2 0.0 collective-permute-done.2
  9.3 0.7 broadcast_in_dim.28
  10.0 10.8 %all-to-all-start.2 = ((bf16[4,192,128]{2,1,0:T(8,128)(2,1)}), bf16[4,192,128]{2,1,0:T(8,128)(2,1)S(1)}, u32[]{:S(2)}, u32[]{:S(2)}) async-start(bf16[4,192,128]{2,1,0:T(8,128)(2,1)} %broadcast_in_dim.28), calls=%async_computation.2 | async-start | bytes 393216 | tf_op jit(solution)/shard_map/all_to_all | solution.py:103
  20.8 0.0 all-gather.2.cloned.1.call-start
  20.8 0.0 copy-done
  20.9 0.0 copy-done.3
  20.9 0.6 dynamic_slice.7
  21.4 7.1 %all-to-all-done.2 = bf16[4,192,128]{2,1,0:T(8,128)(2,1)S(1)} async-done(((bf16[4,192,128]{2,1,0:T(8,128)(2,1)}), bf16[4,192,128]{2,1,0:T(8,128)(2,1)S(1)}, u32[]{:S(2)}, u32[]{:S(2)}) %all-to-all-start.2) | async-done | bytes 196640 | tf_op jit(solution)/shard_map/all_to_all | solution.py:103
  28.5 0.2 reshape.54
  28.7 0.3 copy.15
  29.0 1.0 reshape.55
  30.0 0.0 all-gather.2.cloned.1.call-update
  30.0 0.0 copy-done.4
  30.0 0.6 compare_convert_fusion
  30.6 0.0 copy-start.5
  30.6 0.0 copy-start.2
  30.6 0.1 copy.16
  30.7 0.1 reshape.57
  30.8 0.1 broadcast_in_dim.25
  30.9 0.1 broadcast_in_dim.26
  31.0 0.1 bitcast_multiply_fusion
  31.1 1.1 copy.13
  32.2 18.6 %all-to-all-start = ((bf16[32,32,256]{2,1,0:T(8,128)(2,1)}), bf16[32,32,256]{2,1,0:T(8,128)(2,1)S(1)}, u32[]{:S(2)}, u32[]{:S(2)}) async-start(bf16[32,32,256]{2,1,0:T(8,128)(2,1)} %copy.13), calls=%async_computation | async-start | bytes 1048576 | tf_op jit(solution)/shard_map/all_to_all | solution.py:128
  50.8 0.0 copy-done.5
  50.8 0.0 copy-done.2
  50.8 0.1 broadcast_multiply_fusion.1
  50.9 5.9 %collective-permute-start = (bf16[6,64,64]{2,1,0:T(8,128)(2,1)S(1)}, bf16[6,64,64]{2,1,0:T(8,128)(2,1)S(1)}, u32[]{:S(2)}, u32[]{:S(2)}) collective-permute-start(bf16[6,64,64]{2,1,0:T(8,128)(2,1)S(1)} %broadcast_multiply_fusion.1), channel_id=1, source_target_pairs={{0,4},{4,0},{1,5},{5,1},{2,6},{6,2},{3,7},{7,3},{8,12},{12,8},{9,1... | collective-permute-start | bytes 147464 | tf_op jit(solution)/shard_map/ppermute | solution.py:110
  56.8 0.9 collective-permute-done
  57.7 0.1 broadcast_select_fusion.1
  57.8 0.1 pad_maximum_fusion.2
  57.9 2.6 %collective-permute-start.1 = (bf16[384,128]{1,0:T(8,128)(2,1)S(1)}, bf16[384,128]{1,0:T(8,128)(2,1)S(1)}, u32[]{:S(2)}, u32[]{:S(2)}) collective-permute-start(bf16[384,128]{1,0:T(8,128)(2,1)S(1)} %bitcast.27), channel_id=1, source_target_pairs={{0,8},{8,0},{1,9},{9,1},{2,10},{10,2},{3,11},{11,3},{4,12},{12,4},... | collective-permute-start | bytes 294920 | tf_op jit(solution)/shard_map/ppermute | solution.py:115
  60.6 6.5 %collective-permute-done.1 = bf16[384,128]{1,0:T(8,128)(2,1)S(1)} collective-permute-done((bf16[384,128]{1,0:T(8,128)(2,1)S(1)}, bf16[384,128]{1,0:T(8,128)(2,1)S(1)}, u32[]{:S(2)}, u32[]{:S(2)}) %collective-permute-start.1) | collective-permute-done | bytes 98336 | tf_op jit(solution)/shard_map/ppermute | solution.py:115
  67.1 2.1 %all-to-all-done = bf16[32,32,256]{2,1,0:T(8,128)(2,1)S(1)} async-done(((bf16[32,32,256]{2,1,0:T(8,128)(2,1)}), bf16[32,32,256]{2,1,0:T(8,128)(2,1)S(1)}, u32[]{:S(2)}, u32[]{:S(2)}) %all-to-all-start) | async-done | bytes 524320 | tf_op jit(solution)/shard_map/all_to_all | solution.py:128
  69.2 0.1 broadcast_in_dim.27
  69.2 0.1 pad_maximum_fusion
  69.3 13.6 %all_to_all.20.refs_0_ = bf16[4,640,256]{2,1,0:T(8,128)(2,1)S(1)} all-to-all(bf16[4,640,256]{2,1,0:T(8,128)(2,1)S(1)} %pad_maximum_fusion), channel_id=1, replica_groups=mesh['yh'=4,'yl'=2,'zh'=4,'zl'=2,'core'=2,'op'=4] {'op'}, dimensions={0} | all-to-all | bytes 2621440 | tf_op jit(solution)/shard_map/all_to_all | solution.py:133
  82.9 6.4 %right_products.1.refs_0_ = bf16[2,2,256,6144]{3,2,1,0:T(8,128)(2,1)} custom-call(bf16[4,640,256]{2,1,0:T(8,128)(2,1)S(1)} %all_to_all.20.refs_0_), custom_call_target="tpu_custom_call" | custom-call | tf_op jit(solution)/shard_map/right_products/pallas_call | solution.py:135
  89.3 0.0 all-gather.2.cloned.1.call-done
  89.3 0.0 copy-start.1
  89.3 1.4 %copy-done.1 = bf16[3072,256]{1,0:T(8,128)(2,1)S(1)} copy-done((bf16[3072,256]{1,0:T(8,128)(2,1)S(1)}, bf16[3072,256]{1,0:T(8,128)(2,1)}, u32[]{:S(2)}) %copy-start.1) | copy-done | bytes 1572888
  90.8 7.7 %left_products.1 = bf16[4,2,64,512]{3,2,1,0:T(8,128)(2,1)S(1)} custom-call(bf16[2,2,256,6144]{3,2,1,0:T(8,128)(2,1)} %right_products.1.refs_0_, bf16[4,2,384,256]{3,2,1,0:T(8,128)(2,1)S(1)} %bitcast.20), custom_call_target="tpu_custom_call" | custom-call | tf_op jit(solution)/shard_map/left_products/pallas_call | solution.py:145
  98.4 19.4 %all_to_all.21.refs_0_ = bf16[4,2,64,512]{3,2,1,0:T(8,128)(2,1)} all-to-all(bf16[4,2,64,512]{3,2,1,0:T(8,128)(2,1)S(1)} %left_products.1), channel_id=1, replica_groups=mesh['yh'=4,'yl'=2,'zh'=4,'zl'=2,'core'=2,'op'=4] {'zl','core'}, dimensions={0} | all-to-all | bytes 1048576 | tf_op jit(solution)/shard_map/all_to_all | solution.py:159
  117.9 1.9 %merge_sectors.1 = bf16[2,64,2048]{2,1,0:T(8,128)(2,1)} custom-call(bf16[4,2,64,512]{3,2,1,0:T(8,128)(2,1)} %all_to_all.21.refs_0_), custom_call_target="tpu_custom_call" | custom-call | tf_op jit(solution)/shard_map/merge_sectors/pallas_call | solution.py:160
  (4 shorter events, 0.1 us)
Async XLA Ops:
  6.5 14.3 %copy-start = (bf16[2,64,8192]{2,1,0:T(8,128)(2,1)S(1)}, bf16[2,64,8192]{2,1,0:T(8,128)(2,1)}, u32[]{:S(2)}) copy-start(bf16[2,64,8192]{2,1,0:T(8,128)(2,1)} %param.7) | copy-start | bytes 6291460
  6.5 14.3 %copy-start.3 = (s32[128]{0:T(128)S(1)}, s32[128]{0:T(128)}, u32[]{:S(2)}) copy-start(s32[128]{0:T(128)} %param.12) | copy-start | bytes 1540
  8.4 21.6 %copy-start.4 = (s32[128]{0:T(128)S(1)}, s32[128]{0:T(128)}, u32[]{:S(2)}) copy-start(s32[128]{0:T(128)} %param.13) | copy-start | bytes 1540
  8.5 0.7 collective-permute-start.2
  10.0 18.5 %all-to-all-start.2 = ((bf16[4,192,128]{2,1,0:T(8,128)(2,1)}), bf16[4,192,128]{2,1,0:T(8,128)(2,1)S(1)}, u32[]{:S(2)}, u32[]{:S(2)}) async-start(bf16[4,192,128]{2,1,0:T(8,128)(2,1)} %broadcast_in_dim.28), calls=%async_computation.2 | async-start | bytes 393216 | tf_op jit(solution)/shard_map/all_to_all | solution.py:103
  20.8 68.5 %all-gather.2.cloned.1.call-start = ((), (), s32[]{:S(2)}) async-start(), calls=%async_computation.4 | async-start | bytes 1769472 | tf_op jit(solution)/shard_map/all_gather | solution.py:106
  30.6 20.2 %copy-start.5 = (s32[6,1]{0,1:T(1,128)S(1)}, s32[6,1]{0,1:T(1,128)}, u32[]{:S(2)}) copy-start(s32[6,1]{0,1:T(1,128)} %param.11) | copy-start | bytes 76
  30.6 20.2 %copy-start.2 = (bf16[6,64,64]{2,1,0:T(8,128)(2,1)S(1)}, bf16[6,64,64]{2,1,0:T(8,128)(2,1)}, u32[]{:S(2)}) copy-start(bf16[6,64,64]{2,1,0:T(8,128)(2,1)} %param.9) | copy-start | bytes 147460
  32.2 37.0 %all-to-all-start = ((bf16[32,32,256]{2,1,0:T(8,128)(2,1)}), bf16[32,32,256]{2,1,0:T(8,128)(2,1)S(1)}, u32[]{:S(2)}, u32[]{:S(2)}) async-start(bf16[32,32,256]{2,1,0:T(8,128)(2,1)} %copy.13), calls=%async_computation | async-start | bytes 1048576 | tf_op jit(solution)/shard_map/all_to_all | solution.py:128
  50.9 6.8 %collective-permute-start = (bf16[6,64,64]{2,1,0:T(8,128)(2,1)S(1)}, bf16[6,64,64]{2,1,0:T(8,128)(2,1)S(1)}, u32[]{:S(2)}, u32[]{:S(2)}) collective-permute-start(bf16[6,64,64]{2,1,0:T(8,128)(2,1)S(1)} %broadcast_multiply_fusion.1), channel_id=1, source_target_pairs={{0,4},{4,0},{1,5},{5,1},{2,6},{6,2},{3,7},{7,3},{8,12},{12,8},{9,1... | collective-permute-start | bytes 147464 | tf_op jit(solution)/shard_map/ppermute | solution.py:110
  57.9 9.2 %collective-permute-start.1 = (bf16[384,128]{1,0:T(8,128)(2,1)S(1)}, bf16[384,128]{1,0:T(8,128)(2,1)S(1)}, u32[]{:S(2)}, u32[]{:S(2)}) collective-permute-start(bf16[384,128]{1,0:T(8,128)(2,1)S(1)} %bitcast.27), channel_id=1, source_target_pairs={{0,8},{8,0},{1,9},{9,1},{2,10},{10,2},{3,11},{11,3},{4,12},{12,4},... | collective-permute-start | bytes 294920 | tf_op jit(solution)/shard_map/ppermute | solution.py:115
  89.3 1.4 %copy-start.1 = (bf16[3072,256]{1,0:T(8,128)(2,1)S(1)}, bf16[3072,256]{1,0:T(8,128)(2,1)}, u32[]{:S(2)}) copy-start(bf16[3072,256]{1,0:T(8,128)(2,1)} %all-gather.2.cloned.1.call-done) | copy-start | bytes 4718596
Sparse Core Ops, SparseCore 0:
  30.1 54.2 all-gather.1

commit v2 on v0

v2 whole, which is shorter than its diff:
```python
import jax
import jax.numpy as jnp
from jax import lax
from jax.experimental import pallas as pl
from jax.experimental.pallas import tpu as pltpu
from jax.sharding import Mesh, PartitionSpec as P

target_charge = 6
XDIM, YH, YL, ZH, ZL, CORE = 4, 4, 2, 4, 2, 2
SEC = ("yh", "yl", "zh", "zl", "core")
FAR = ("yh", "zh", "core")
NEAR = ("yl", "zl")
NT = (((1,), (1,)), ((), ()))
BLOCK = 64
WIDE = 2 * BLOCK
HALF = BLOCK // 2
GROUP = 4 * BLOCK
TERMS = 24
HERE = TERMS // XDIM
PAIRS = HERE // 2
XROWS = 2 * HALF
LROWS = PAIRS * HALF
RROWS = PAIRS * BLOCK
FROM = ZH * CORE
VMEM = 48 * 1024 * 1024


def swap_halves(piece):
    return jnp.concatenate([piece[:, BLOCK:], piece[:, :BLOCK]], axis=1)


def placed(piece, second, to_second):
    lane = lax.broadcasted_iota(jnp.int32, piece.shape, 1)
    moved = piece if second == to_second else swap_halves(piece)
    keep = (lane >= BLOCK) if to_second else (lane < BLOCK)
    return jnp.where(keep, moved, jnp.zeros_like(moved))


def pack_kernel(lc_ref, rc_ref, left_ref, right_ref, lout_ref, rout_ref):
    for p in range(PAIRS):
        left, right = [], []
        for t in (2 * p, 2 * p + 1):
            scale = lc_ref[t, 0].astype(jnp.float32)
            left.append((left_ref[t].astype(jnp.float32) * scale).astype(jnp.bfloat16))
            scale = rc_ref[t, 0].astype(jnp.float32)
            right.append((right_ref[t].astype(jnp.float32) * scale).astype(jnp.bfloat16))
        rout_ref[p * BLOCK:(p + 1) * BLOCK, :] = jnp.concatenate(right, axis=1)
        both = jnp.concatenate(left, axis=1)
        for h in range(2):
            lout_ref[h, p * HALF:(p + 1) * HALF, :] = both[h * HALF:(h + 1) * HALF]


def send_kernel(at_ref, lcharge_ref, rcharge_ref, x_ref, out_ref):
    own = lcharge_ref[at_ref[2]] - target_charge
    lane = lax.broadcasted_iota(jnp.int32, (1, WIDE), 1)

    def allowed(sector):
        return jnp.where(jnp.abs(own + rcharge_ref[sector]) <= 1, 1.0, 0.0)

    for yh in range(YH):
        for yl in range(YL):
            for zh in range(ZH):
                at = ((yh * YL + yl) * ZH + zh) * ZL
                first = x_ref[0, :, at * WIDE:(at + 1) * WIDE]
                second = x_ref[0, :, (at + 1) * WIDE:(at + 2) * WIDE]
                for c in range(CORE):
                    lanes = slice(c * BLOCK, (c + 1) * BLOCK)
                    both = jnp.concatenate([first[:, lanes], second[:, lanes]], axis=1)
                    mask = jnp.where(
                        lane < BLOCK, allowed(at * CORE + c), allowed((at + 1) * CORE + c)
                    ).astype(jnp.bfloat16)
                    to = (yh * ZH + zh) * CORE + c
                    out_ref[to, yl * HALF:(yl + 1) * HALF, :] = both * mask


def sigma_kernel(core_ref, xr_ref, own_ref, other_ref, out_ref, right_ref, left_ref, half_ref):
    g, v = pl.program_id(0), pl.program_id(1)
    core = core_ref[0]

    @pl.when((g == 0) & (v == 0))
    def _():
        right_ref[...] = jnp.zeros_like(right_ref)
        left_ref[...] = jnp.zeros_like(left_ref)
        for x in range(XDIM):
            for p in range(PAIRS):
                for b in range(4):
                    at = FROM * XROWS + b * RROWS + p * BLOCK
                    piece = xr_ref[x, at:at + BLOCK, :]
                    for s in range(2):
                        t = x * HERE + 2 * p + s
                        right_ref[t, b * BLOCK:(b + 1) * BLOCK,
                                  (b // 2) * WIDE:(b // 2 + 1) * WIDE] = placed(piece, s, b % 2)

    @pl.when(v == 0)
    def _():
        for x in range(XDIM):
            for p in range(PAIRS):
                for a in range(4):
                    for ref, h in ((own_ref, core), (other_ref, 1 - core)):
                        piece = ref[x * FROM + g * 4 + a, p * HALF:(p + 1) * HALF, :]
                        rows = pl.ds(pl.multiple_of(a * BLOCK + h * HALF, HALF), HALF)
                        for s in range(2):
                            t = x * HERE + 2 * p + s
                            at = t * GROUP + (a // 2) * WIDE
                            left_ref[rows, at:at + WIDE] = placed(piece, s, a % 2)

    rows = []
    for a in range(4):
        for h in range(2):
            start = pl.multiple_of((g * 4 + a) * XROWS, XROWS)
            piece = xr_ref[v * 2 + h, pl.ds(start, XROWS), :]
            rows.append(jnp.concatenate([piece[:HALF], piece[HALF:]], axis=1))
    state = jnp.concatenate(rows, axis=0)
    for t in range(TERMS):
        out = lax.dot_general(right_ref[t], state, NT, preferred_element_type=jnp.float32)
        half_ref[:, t * GROUP:(t + 1) * GROUP] = out.astype(half_ref.dtype)
    out = lax.dot_general(half_ref[...], left_ref[...], NT, preferred_element_type=jnp.float32)
    out_ref[...] = out.reshape(4, 1, BLOCK, GROUP).astype(out_ref.dtype)


def merge_kernel(in_ref, out_ref):
    for yl in range(YL):
        for zh in range(ZH):
            for zl in range(ZL):
                at = ((yl * ZH + zh) * ZL + zl) * WIDE
                out_ref[0, :, at:at + WIDE] = in_ref[yl * ZL + zl, 0, :, zh * WIDE:(zh + 1) * WIDE]


def body(
    trial_state,
    left_operators,
    right_operators,
    left_coupling,
    right_coupling,
    left_charge,
    right_charge,
):
    vectors, _, states = trial_state.shape
    plane = lax.axis_index("op")
    position = lax.axis_index(SEC)
    smem = pl.BlockSpec(memory_space=pltpu.SMEM)
    vmem = pl.BlockSpec(memory_space=pltpu.VMEM)
    params = pltpu.CompilerParams(vmem_limit_bytes=VMEM)

    left, right = pl.pallas_call(
        pack_kernel,
        in_specs=[smem, smem, vmem, vmem],
        out_specs=[vmem, vmem],
        out_shape=[
            jax.ShapeDtypeStruct((2, LROWS, WIDE), jnp.bfloat16),
            jax.ShapeDtypeStruct((RROWS, WIDE), jnp.bfloat16),
        ],
        name="pack_operators",
    )(left_coupling, right_coupling, left_operators, right_operators)
    swap = [(q * XDIM + x, x * XDIM + q) for q in range(YH) for x in range(XDIM)]
    left = lax.ppermute(left, ("yh", "op"), swap)
    right = lax.all_gather(right, NEAR, tiled=True)

    at = jnp.stack([plane // 2, plane % 2, position]).astype(jnp.int32)
    quarter = pl.pallas_call(
        send_kernel,
        grid_spec=pltpu.PrefetchScalarGridSpec(
            num_scalar_prefetch=1,
            grid=(1,),
            in_specs=[smem, smem, pl.BlockSpec((1, HALF, states), lambda i, at: (at[0], at[1], 0))],
            out_specs=pl.BlockSpec((YH * FROM, XROWS, WIDE), lambda i, at: (0, 0, 0)),
        ),
        out_shape=jax.ShapeDtypeStruct((YH * FROM, XROWS, WIDE), jnp.bfloat16),
        compiler_params=params,
        name="send_trial",
    )(at, left_charge, right_charge, trial_state)

    copies = jnp.broadcast_to(left[None], (YH * ZH,) + left.shape)
    sent = jnp.concatenate([quarter, copies.reshape(YH * FROM, LROWS, WIDE)], axis=1)
    sent = lax.all_to_all(sent, FAR, 0, 0, tiled=True)
    own = sent[:, XROWS:]
    other = lax.ppermute(own, "core", [(0, 1), (1, 0)])
    quarter = sent[:, :XROWS].reshape(YH, FROM * XROWS, WIDE)
    packed = jnp.concatenate(
        [quarter, jnp.broadcast_to(right[None], (XDIM,) + right.shape)], axis=1
    )
    packed = lax.all_to_all(packed, "op", 0, 0, tiled=True)

    core = lax.axis_index("core").astype(jnp.int32).reshape(1)
    partial = pl.pallas_call(
        sigma_kernel,
        grid=(2, vectors),
        in_specs=[
            smem,
            pl.BlockSpec(packed.shape, lambda g, v: (0, 0, 0)),
            pl.BlockSpec(own.shape, lambda g, v: (0, 0, 0)),
            pl.BlockSpec(own.shape, lambda g, v: (0, 0, 0)),
        ],
        out_specs=pl.BlockSpec((4, 1, BLOCK, GROUP), lambda g, v: (0, v, 0, g)),
        out_shape=jax.ShapeDtypeStruct((4, vectors, BLOCK, 2 * GROUP), jnp.bfloat16),
        scratch_shapes=[
            pltpu.VMEM((TERMS, GROUP, GROUP), jnp.bfloat16),
            pltpu.VMEM((GROUP, TERMS * GROUP), jnp.bfloat16),
            pltpu.VMEM((GROUP, TERMS * GROUP), jnp.bfloat16),
        ],
        compiler_params=params,
        name="sigma_blocks",
    )(core, packed, own, other)

    partial = lax.all_to_all(partial, NEAR, 0, 0, tiled=True)
    return pl.pallas_call(
        merge_kernel,
        grid=(vectors,),
        in_specs=[pl.BlockSpec((4, 1, BLOCK, 2 * GROUP), lambda v: (0, v, 0, 0))],
        out_specs=pl.BlockSpec((1, BLOCK, 8 * GROUP), lambda v: (v, 0, 0)),
        out_shape=jax.ShapeDtypeStruct((vectors, BLOCK, 8 * GROUP), jnp.bfloat16),
        name="merge_sectors",
    )(partial)


def solution(mesh):
    fine = Mesh(mesh.devices.reshape(YH, YL, ZH, ZL, CORE, XDIM), SEC + ("op",))
    return jax.shard_map(
        body,
        mesh=fine,
        in_specs=(
            P(None, SEC, None),
            P("op", SEC, None),
            P("op", SEC, None),
            P("op", SEC),
            P("op", SEC),
            P(),
            P(),
        ),
        out_specs=P(None, SEC, "op"),
        check_vma=False,
    )
```

time: 732 us -> 123 us (0.17)
  waiting for transfers between devices: 605 us -> 19.8 us
  local copies, waits for them, and re-layouts: 69.4 us -> 5.9 us
  blocking collectives: 0 us -> 48.8 us
  Pallas kernels: 0 us -> 14.3 us
  matrix products: 14 us -> 0 us
  between operations: 13.5 us -> 0.09 us
  starting transfers between devices: 19.2 us -> 30.9 us
    all_to_all x1 -> x2, waiting for transfers between devices: 486 us -> 17.6 us  [the longest x1 13.7 us: body(): packed = lax.all_to_all(packed, 'op', 0, 0, tiled=True)]
    reduce_scatter x1 -> x0, waiting for transfers between devices: 119 us -> none  [body(): lax.psum_scatter(combined, 'op', scatter_dimension=2, tiled=True)]
    all_gather x0 -> x1, blocking collectives: none -> 37.8 us  [body(): right = lax.all_gather(right, NEAR, tiled=True)]
    reshape x2 -> x0, local copies, waits for them, and re-layouts: 29 us -> none  [the longest x1 21.1 us: body(): products = products.reshape(terms_here, states, vectors * block)]
    all_to_all x1 -> x0, local copies, waits for them, and re-layouts: 26.2 us -> none  [body(): lax.all_to_all(products, 'sec', split_axis=1, concat_axis=2, tiled=True)]
    pallas_call x0 -> x4, Pallas kernels: none -> 14.3 us  [the longest x1 9.42 us: body(): pl.pallas_call(sigma_kernel, grid=(2, vectors), in_specs=[smem, pl.BlockS...]
    dot_general x2 -> x0, matrix products: 14 us -> none  [the longest x1 9 us: body(): jnp.einsum('tjk,tkavi->vjai', right_scaled, arrived, preferred_element_ty...]
    all_to_all x0 -> x1, blocking collectives: none -> 11 us  [body(): partial = lax.all_to_all(partial, NEAR, 0, 0, tiled=True)]
  transfers between devices with their start and end apart: 2 -> 4, of which waited for: 2 -> 3; matrix products, arithmetic and copies ran while one was open for 0% -> 0% of each run, Pallas kernels for 0% -> 1%
where the time goes in v2:
time: 123 us; the launch traced here: 122 us
  blocking collectives  48.8 us (40%)
  starting transfers between devices  30.9 us (25%)
  waiting for transfers between devices  19.8 us (16%)
  Pallas kernels  14.3 us (12%)
  local copies, waits for them, and re-layouts  5.9 us (5%)
  other arithmetic  2.44 us (2%)
    all_gather x1, blocking collectives, body(): right = lax.all_gather(right, NEAR, tiled=True)  37.8 us
    all_to_all x1, starting transfers between devices, body(): sent = lax.all_to_all(sent, FAR, 0, 0, tiled=True)  24 us
    all_to_all x1, waiting for transfers between devices, body(): packed = lax.all_to_all(packed, 'op', 0, 0, tiled=True)  13.7 us
    all_to_all x1, blocking collectives, body(): partial = lax.all_to_all(partial, NEAR, 0, 0, tiled=True)  11 us
    pallas_call x1, Pallas kernels, body(): pl.pallas_call(sigma_kernel, grid=(2, vectors), in_specs=[smem, pl.BlockS...  9.42 us
    unnamed x10, local copies, waits for them, and re-layouts  5.55 us
    all_to_all x1, waiting for transfers between devices, body(): sent = lax.all_to_all(sent, FAR, 0, 0, tiled=True)  3.85 us
    all_to_all x1, starting transfers between devices, body(): packed = lax.all_to_all(packed, 'op', 0, 0, tiled=True)  3.54 us
  transfers between devices with their start and end apart: 4, of which 3 were waited for; matrix products, arithmetic and copies ran while one was open for 0% of the time, Pallas kernels for 1%

profile of v2, /device:TPU:1, one launch (start us, length us, event | category | flops | bytes accessed | tf_op | source)
XLA Modules:
  0.0 122.3 jit_solution(3411309152776275757)
XLA Ops:
  0.0 1.3 %copy.8.lc_ref = s32[6,1]{1,0:T(8,128)} copy(s32[6,1]{0,1:T(1,128)} %param.10) | data formatting | bytes 48 | tf_op args[3]
  1.3 1.3 %copy.9.rc_ref = s32[6,1]{1,0:T(8,128)} copy(s32[6,1]{0,1:T(1,128)} %param.11) | data formatting | bytes 48 | tf_op args[4]
  2.6 1.7 %pack_operators.1 = (bf16[2,96,128]{2,1,0:T(8,128)(2,1)}, bf16[192,128]{1,0:T(8,128)(2,1)}) custom-call(s32[6,1]{1,0:T(8,128)} %copy.8.lc_ref, s32[6,1]{1,0:T(8,128)} %copy.9.rc_ref, bf16[6,64,64]{2,1,0:T(8,128)(2,1)} %left_ref.1, bf16[6,64,64]{2,1,0:T(8,128)(2,1)} %right_ref.1), custom_call_target="tpu_custom_call" | custom-call | tf_op jit(solution)/shard_map/pack_operators/pallas_call | solution.py:145
  4.3 1.4 %collective-permute-start = (bf16[2,96,128]{2,1,0:T(8,128)(2,1)}, bf16[2,96,128]{2,1,0:T(8,128)(2,1)S(1)}, u32[]{:S(2)}, u32[]{:S(2)}) collective-permute-start(bf16[2,96,128]{2,1,0:T(8,128)(2,1)} %get-tuple-element.7), channel_id=1, source_target_pairs={{0,0},{1,128},{2,256},{3,384},{128,1},{129,129},{130,257},{131,385... | collective-permute-start | bytes 147464 | tf_op jit(solution)/shard_map/ppermute | solution.py:156
  5.8 0.1 pad_add_fusion.at_ref
  5.9 0.0 copy-start
  5.9 1.6 %copy-done = bf16[2,64,8192]{2,1,0:T(8,128)(2,1)S(1)} copy-done((bf16[2,64,8192]{2,1,0:T(8,128)(2,1)S(1)}, bf16[2,64,8192]{2,1,0:T(8,128)(2,1)}, u32[]{:S(2)}) %copy-start) | copy-done | bytes 2097176
  7.4 0.0 copy-start.1
  7.4 0.7 copy-done.1
  8.1 0.0 copy-start.2
  8.1 0.7 copy-done.2
  8.8 1.4 %send_trial.1 = bf16[32,64,128]{2,1,0:T(8,128)(2,1)S(1)} custom-call(s32[3]{0:T(128)S(1)} %pad_add_fusion.at_ref, s32[128]{0:T(128)S(1)} %copy-done.1, s32[128]{0:T(128)S(1)} %copy-done.2, bf16[2,64,8192]{2,1,0:T(8,128)(2,1)S(1)} %copy-done), custom_call_target="tpu_custom_call" | custom-call | tf_op jit(solution)/shard_map/send_trial/pallas_call | solution.py:160
  10.1 0.0 collective-permute-done
  10.2 0.1 broadcast_in_dim.4
  10.3 1.2 pad_maximum_fusion
  11.5 0.0 copy-start.3
  11.5 24.0 %all-to-all-start = ((bf16[32,160,128]{2,1,0:T(8,128)(2,1)}), bf16[32,160,128]{2,1,0:T(8,128)(2,1)S(1)}, u32[]{:S(2)}, u32[]{:S(2)}) async-start(bf16[32,160,128]{2,1,0:T(8,128)(2,1)} %pad_maximum_fusion), calls=%async_computation | async-start | bytes 2621440 | tf_op jit(solution)/shard_map/all_to_all | solution.py:175
  35.5 0.0 copy-done.3
  35.5 37.8 %all_gather.3 = bf16[768,128]{1,0:T(8,128)(2,1)S(1)} all-gather(bf16[192,128]{1,0:T(8,128)(2,1)S(1)} %copy-done.3), channel_id=1, replica_groups=mesh['yh'=4,'yl'=2,'zh'=4,'zl'=2,'core'=2,'op'=4] {'yl','zl'}, dimensions={0}, use_global_device_ids=true | all-gather | bytes 245760 | tf_op jit(solution)/shard_map/all_gather | solution.py:157
  73.3 3.8 %all-to-all-done = bf16[32,160,128]{2,1,0:T(8,128)(2,1)S(1)} async-done(((bf16[32,160,128]{2,1,0:T(8,128)(2,1)}), bf16[32,160,128]{2,1,0:T(8,128)(2,1)S(1)}, u32[]{:S(2)}, u32[]{:S(2)}) %all-to-all-start) | async-done | bytes 1310752 | tf_op jit(solution)/shard_map/all_to_all | solution.py:175
  77.2 0.1 broadcast_in_dim.5
  77.4 1.2 pad_maximum_fusion.1
  78.5 3.5 %all-to-all-start.1 = ((bf16[4,1280,128]{2,1,0:T(8,128)(2,1)}), bf16[4,1280,128]{2,1,0:T(8,128)(2,1)S(1)}, u32[]{:S(2)}, u32[]{:S(2)}) async-start(bf16[4,1280,128]{2,1,0:T(8,128)(2,1)} %pad_maximum_fusion.1), calls=%async_computation.1 | async-start | bytes 2621440 | tf_op jit(solution)/shard_map/all_to_all | solution.py:182
  82.1 0.1 slice.9.own_ref
  82.1 1.9 %collective-permute-start.1 = (bf16[32,96,128]{2,1,0:T(8,128)(2,1)S(1)}, bf16[32,96,128]{2,1,0:T(8,128)(2,1)S(1)}, u32[]{:S(2)}, u32[]{:S(2)}) collective-permute-start(bf16[32,96,128]{2,1,0:T(8,128)(2,1)S(1)} %slice.9.own_ref), channel_id=1, source_target_pairs={{0,4},{4,0},{1,5},{5,1},{2,6},{6,2},{3,7},{7,3},{8,12},{12,8},{9,1... | collective-permute-start | bytes 2359304 | tf_op jit(solution)/shard_map/ppermute | solution.py:177
  84.1 2.3 %collective-permute-done.1.other_ref = bf16[32,96,128]{2,1,0:T(8,128)(2,1)S(1)} collective-permute-done((bf16[32,96,128]{2,1,0:T(8,128)(2,1)S(1)}, bf16[32,96,128]{2,1,0:T(8,128)(2,1)S(1)}, u32[]{:S(2)}, u32[]{:S(2)}) %collective-permute-start.1) | collective-permute-done | bytes 786464 | tf_op jit(solution)/shard_map/ppermute | solution.py:177
  86.3 13.7 %all-to-all-done.1.xr_ref = bf16[4,1280,128]{2,1,0:T(8,128)(2,1)S(1)} async-done(((bf16[4,1280,128]{2,1,0:T(8,128)(2,1)}), bf16[4,1280,128]{2,1,0:T(8,128)(2,1)S(1)}, u32[]{:S(2)}, u32[]{:S(2)}) %all-to-all-start.1) | async-done | bytes 1310752 | tf_op jit(solution)/shard_map/all_to_all | solution.py:182
  100.1 9.4 %sigma_blocks.1 = bf16[4,2,64,512]{3,2,1,0:T(8,128)(2,1)S(1)} custom-call(s32[1]{0:T(128)} %bitcast.core_ref, bf16[4,1280,128]{2,1,0:T(8,128)(2,1)S(1)} %all-to-all-done.1.xr_ref, bf16[32,96,128]{2,1,0:T(8,128)(2,1)S(1)} %slice.9.own_ref, bf16[32,96,128]{2,1,0:T(8,128)(2,1)S(1)} %collective-permute-done.1.other_ref), custom_call_target="tpu_custom_call" | custom-call | tf_op jit(solution)/shard_map/sigma_blocks/pallas_call | solution.py:185
  109.5 11.0 %all_to_all.15.in_ref = bf16[4,2,64,512]{3,2,1,0:T(8,128)(2,1)} all-to-all(bf16[4,2,64,512]{3,2,1,0:T(8,128)(2,1)S(1)} %sigma_blocks.1), channel_id=1, replica_groups=mesh['yh'=4,'yl'=2,'zh'=4,'zl'=2,'core'=2,'op'=4] {'yl','zl'}, dimensions={0} | all-to-all | bytes 1048576 | tf_op jit(solution)/shard_map/all_to_all | solution.py:205
  120.5 1.8 %merge_sectors.1 = bf16[2,64,2048]{2,1,0:T(8,128)(2,1)} custom-call(bf16[4,2,64,512]{3,2,1,0:T(8,128)(2,1)} %all_to_all.15.in_ref), custom_call_target="tpu_custom_call" | custom-call | tf_op jit(solution)/shard_map/merge_sectors/pallas_call | solution.py:206
  (1 shorter events, 0.0 us)
Async XLA Ops:
  4.3 5.8 %collective-permute-start = (bf16[2,96,128]{2,1,0:T(8,128)(2,1)}, bf16[2,96,128]{2,1,0:T(8,128)(2,1)S(1)}, u32[]{:S(2)}, u32[]{:S(2)}) collective-permute-start(bf16[2,96,128]{2,1,0:T(8,128)(2,1)} %get-tuple-element.7), channel_id=1, source_target_pairs={{0,0},{1,128},{2,256},{3,384},{128,1},{129,129},{130,257},{131,385... | collective-permute-start | bytes 147464 | tf_op jit(solution)/shard_map/ppermute | solution.py:156
  5.9 1.6 %copy-start = (bf16[2,64,8192]{2,1,0:T(8,128)(2,1)S(1)}, bf16[2,64,8192]{2,1,0:T(8,128)(2,1)}, u32[]{:S(2)}) copy-start(bf16[2,64,8192]{2,1,0:T(8,128)(2,1)} %x_ref.1) | copy-start | bytes 6291460
  7.4 0.7 copy-start.1
  8.1 0.7 copy-start.2
  11.5 24.0 %copy-start.3 = (bf16[192,128]{1,0:T(8,128)(2,1)S(1)}, bf16[192,128]{1,0:T(8,128)(2,1)}, u32[]{:S(2)}) copy-start(bf16[192,128]{1,0:T(8,128)(2,1)} %get-tuple-element.8) | copy-start | bytes 147460
  11.5 65.7 %all-to-all-start = ((bf16[32,160,128]{2,1,0:T(8,128)(2,1)}), bf16[32,160,128]{2,1,0:T(8,128)(2,1)S(1)}, u32[]{:S(2)}, u32[]{:S(2)}) async-start(bf16[32,160,128]{2,1,0:T(8,128)(2,1)} %pad_maximum_fusion), calls=%async_computation | async-start | bytes 2621440 | tf_op jit(solution)/shard_map/all_to_all | solution.py:175
  78.5 21.5 %all-to-all-start.1 = ((bf16[4,1280,128]{2,1,0:T(8,128)(2,1)}), bf16[4,1280,128]{2,1,0:T(8,128)(2,1)S(1)}, u32[]{:S(2)}, u32[]{:S(2)}) async-start(bf16[4,1280,128]{2,1,0:T(8,128)(2,1)} %pad_maximum_fusion.1), calls=%async_computation.1 | async-start | bytes 2621440 | tf_op jit(solution)/shard_map/all_to_all | solution.py:182
  82.1 4.2 %collective-permute-start.1 = (bf16[32,96,128]{2,1,0:T(8,128)(2,1)S(1)}, bf16[32,96,128]{2,1,0:T(8,128)(2,1)S(1)}, u32[]{:S(2)}, u32[]{:S(2)}) collective-permute-start(bf16[32,96,128]{2,1,0:T(8,128)(2,1)S(1)} %slice.9.own_ref), channel_id=1, source_target_pairs={{0,4},{4,0},{1,5},{5,1},{2,6},{6,2},{3,7},{7,3},{8,12},{12,8},{9,1... | collective-permute-start | bytes 2359304 | tf_op jit(solution)/shard_map/ppermute | solution.py:177

commit v3 on v2

v3 whole, which is shorter than its diff:
```python
import jax
import jax.numpy as jnp
from jax import lax
from jax.experimental import pallas as pl
from jax.experimental.pallas import tpu as pltpu
from jax.sharding import Mesh, PartitionSpec as P

target_charge = 6
XDIM, YH, YL, ZH, ZL, CORE = 4, 4, 2, 4, 2, 2
SEC = ("yh", "yl", "zh", "zl", "core")
FAR = ("yh", "zh", "core")
NEAR = ("yl", "zl")
NT = (((1,), (1,)), ((), ()))
BLOCK = 64
WIDE = 2 * BLOCK
HALF = BLOCK // 2
GROUP = 4 * BLOCK
TERMS = 24
HERE = TERMS // XDIM
PAIRS = HERE // 2
XROWS = 2 * HALF
RROWS = PAIRS * BLOCK
FROM = ZH * CORE
VMEM = 48 * 1024 * 1024


def swap_halves(piece):
    return jnp.concatenate([piece[:, BLOCK:], piece[:, :BLOCK]], axis=1)


def placed(piece, second, to_second):
    lane = lax.broadcasted_iota(jnp.int32, piece.shape, 1)
    moved = piece if second == to_second else swap_halves(piece)
    keep = (lane >= BLOCK) if to_second else (lane < BLOCK)
    return jnp.where(keep, moved, jnp.zeros_like(moved))


def pack_kernel(lc_ref, rc_ref, left_ref, right_ref, lout_ref, rout_ref):
    for p in range(PAIRS):
        for c_ref, in_ref, out_ref in ((lc_ref, left_ref, lout_ref), (rc_ref, right_ref, rout_ref)):
            both = []
            for t in (2 * p, 2 * p + 1):
                scale = c_ref[0, t].astype(jnp.float32)
                both.append((in_ref[t].astype(jnp.float32) * scale).astype(jnp.bfloat16))
            out_ref[p * BLOCK:(p + 1) * BLOCK, :] = jnp.concatenate(both, axis=1)


def send_kernel(at_ref, x_ref, out_ref):
    for yh in range(YH):
        for yl in range(YL):
            for zh in range(ZH):
                at = ((yh * YL + yl) * ZH + zh) * ZL
                first = x_ref[0, :, at * WIDE:(at + 1) * WIDE]
                second = x_ref[0, :, (at + 1) * WIDE:(at + 2) * WIDE]
                for c in range(CORE):
                    lanes = slice(c * BLOCK, (c + 1) * BLOCK)
                    to = (yh * ZH + zh) * CORE + c
                    out_ref[to, yl * HALF:(yl + 1) * HALF, :] = jnp.concatenate(
                        [first[:, lanes], second[:, lanes]], axis=1
                    )


def spread_kernel(left_ref, after_ref, out_ref):
    for to in range(YH * ZH):
        out_ref[to] = left_ref[...]


def sigma_kernel(at_ref, lcharge_ref, rcharge_ref, xr_ref, own_ref, other_ref, out_ref, right_ref, left_ref, half_ref):
    g, v = pl.program_id(0), pl.program_id(1)
    x_at, yh_at, yl_at, zh_at, zl_at, core = [at_ref[n] for n in range(6)]

    @pl.when((g == 0) & (v == 0))
    def _():
        right_ref[...] = jnp.zeros_like(right_ref)
        left_ref[...] = jnp.zeros_like(left_ref)
        for x in range(XDIM):
            for p in range(PAIRS):
                for b in range(4):
                    at = FROM * XROWS + (b // 2) * 2 * RROWS + (b % 2) * RROWS + p * BLOCK
                    piece = xr_ref[x, at:at + BLOCK, :]
                    for s in range(2):
                        t = x * HERE + 2 * p + s
                        right_ref[t, b * BLOCK:(b + 1) * BLOCK,
                                  (b // 2) * WIDE:(b // 2 + 1) * WIDE] = placed(piece, s, b % 2)

    @pl.when(v == 0)
    def _():
        for x in range(XDIM):
            for p in range(PAIRS):
                for z in range(2):
                    rows = slice(p * BLOCK, (p + 1) * BLOCK)
                    mine = own_ref[x * ZH + g * 2 + z, rows, :]
                    theirs = other_ref[x * ZH + g * 2 + z, rows, :]
                    for c in range(CORE):
                        piece = jnp.where(core == c, mine, theirs)
                        a = z * CORE + c
                        for s in range(2):
                            t = x * HERE + 2 * p + s
                            at = t * GROUP + z * WIDE
                            left_ref[a * BLOCK:(a + 1) * BLOCK, at:at + WIDE] = placed(piece, s, c)

    rows = []
    for a in range(4):
        for h in range(2):
            start = pl.multiple_of((g * 4 + a) * XROWS, XROWS)
            piece = xr_ref[v * 2 + h, pl.ds(start, XROWS), :]
            rows.append(jnp.concatenate([piece[:HALF], piece[HALF:]], axis=1))
    state = jnp.concatenate(rows, axis=0)
    for t in range(TERMS):
        out = lax.dot_general(right_ref[t], state, NT, preferred_element_type=jnp.float32)
        half_ref[:, t * GROUP:(t + 1) * GROUP] = out.astype(half_ref.dtype)
    out = lax.dot_general(half_ref[...], left_ref[...], NT, preferred_element_type=jnp.float32)

    lane = lax.broadcasted_iota(jnp.int32, (1, GROUP), 1) // BLOCK
    charge = jnp.zeros((1, GROUP), jnp.int32)
    for a in range(4):
        sector = (((x_at * YL + yl_at) * ZH + g * 2 + a // 2) * ZL + zl_at) * CORE + a % 2
        charge = jnp.where(lane == a, lcharge_ref[sector], charge)
    for b in range(4):
        sector = (((yh_at * YL + b // 2) * ZH + zh_at) * ZL + b % 2) * CORE + core
        allowed = jnp.abs(charge + rcharge_ref[sector] - target_charge) <= 1
        block = out[b * BLOCK:(b + 1) * BLOCK]
        out_ref[b, 0] = jnp.where(allowed, block, jnp.zeros_like(block)).astype(out_ref.dtype)


def merge_kernel(in_ref, out_ref):
    for yl in range(YL):
        for zh in range(ZH):
            for zl in range(ZL):
                at = ((yl * ZH + zh) * ZL + zl) * WIDE
                out_ref[0, :, at:at + WIDE] = in_ref[yl * ZL + zl, 0, :, zh * WIDE:(zh + 1) * WIDE]


def body(
    trial_state,
    left_operators,
    right_operators,
    left_coupling,
    right_coupling,
    left_charge,
    right_charge,
):
    vectors, _, states = trial_state.shape
    at = jnp.stack([lax.axis_index(n) for n in ("op",) + SEC]).astype(jnp.int32)
    smem = pl.BlockSpec(memory_space=pltpu.SMEM)
    vmem = pl.BlockSpec(memory_space=pltpu.VMEM)
    params = pltpu.CompilerParams(vmem_limit_bytes=VMEM)

    operator = jax.ShapeDtypeStruct((RROWS, WIDE), jnp.bfloat16)
    left, right = pl.pallas_call(
        pack_kernel,
        in_specs=[smem, smem, vmem, vmem],
        out_specs=[vmem, vmem],
        out_shape=[operator, operator],
        name="pack_operators",
    )(left_coupling.reshape(1, HERE), right_coupling.reshape(1, HERE), left_operators, right_operators)
    swap = [(q * XDIM + x, x * XDIM + q) for q in range(YH) for x in range(XDIM)]
    left = lax.ppermute(left, ("yh", "op"), swap)

    quarter = pl.pallas_call(
        send_kernel,
        grid_spec=pltpu.PrefetchScalarGridSpec(
            num_scalar_prefetch=1,
            grid=(1,),
            in_specs=[
                pl.BlockSpec((1, HALF, states), lambda i, at: (at[0] // 2, lax.rem(at[0], 2), 0))
            ],
            out_specs=pl.BlockSpec((YH * FROM, XROWS, WIDE), lambda i, at: (0, 0, 0)),
        ),
        out_shape=jax.ShapeDtypeStruct((YH * FROM, XROWS, WIDE), jnp.bfloat16),
        compiler_params=params,
        name="send_trial",
    )(at, trial_state)
    quarter = lax.all_to_all(quarter, FAR, 0, 0, tiled=True)

    for axis in ("zl", "yl"):
        other = lax.ppermute(right, axis, [(0, 1), (1, 0)])
        first = lax.axis_index(axis) == 0
        right = jnp.concatenate(
            [jnp.where(first, right, other), jnp.where(first, other, right)], axis=0
        )

    left = pl.pallas_call(
        spread_kernel,
        in_specs=[vmem, pl.BlockSpec(memory_space=pl.ANY)],
        out_specs=vmem,
        out_shape=jax.ShapeDtypeStruct((YH * ZH, RROWS, WIDE), jnp.bfloat16),
        name="spread_left",
    )(left, quarter)
    own = lax.all_to_all(left, ("yh", "zh"), 0, 0, tiled=True)
    other = lax.ppermute(own, "core", [(0, 1), (1, 0)])

    quarter = quarter.reshape(YH, FROM * XROWS, WIDE)
    packed = jnp.concatenate(
        [quarter, jnp.broadcast_to(right[None], (XDIM,) + right.shape)], axis=1
    )
    packed = lax.all_to_all(packed, "op", 0, 0, tiled=True)

    partial = pl.pallas_call(
        sigma_kernel,
        grid=(2, vectors),
        in_specs=[
            smem,
            smem,
            smem,
            pl.BlockSpec(packed.shape, lambda g, v: (0, 0, 0)),
            pl.BlockSpec(own.shape, lambda g, v: (0, 0, 0)),
            pl.BlockSpec(own.shape, lambda g, v: (0, 0, 0)),
        ],
        out_specs=pl.BlockSpec((4, 1, BLOCK, GROUP), lambda g, v: (0, v, 0, g)),
        out_shape=jax.ShapeDtypeStruct((4, vectors, BLOCK, 2 * GROUP), jnp.bfloat16),
        scratch_shapes=[
            pltpu.VMEM((TERMS, GROUP, GROUP), jnp.bfloat16),
            pltpu.VMEM((GROUP, TERMS * GROUP), jnp.bfloat16),
            pltpu.VMEM((GROUP, TERMS * GROUP), jnp.bfloat16),
        ],
        compiler_params=params,
        name="sigma_blocks",
    )(at, left_charge, right_charge, packed, own, other)

    partial = lax.all_to_all(partial, NEAR, 0, 0, tiled=True)
    return pl.pallas_call(
        merge_kernel,
        grid=(vectors,),
        in_specs=[pl.BlockSpec((4, 1, BLOCK, 2 * GROUP), lambda v: (0, v, 0, 0))],
        out_specs=pl.BlockSpec((1, BLOCK, 8 * GROUP), lambda v: (v, 0, 0)),
        out_shape=jax.ShapeDtypeStruct((vectors, BLOCK, 8 * GROUP), jnp.bfloat16),
        name="merge_sectors",
    )(partial)


def solution(mesh):
    fine = Mesh(mesh.devices.reshape(YH, YL, ZH, ZL, CORE, XDIM), SEC + ("op",))
    return jax.shard_map(
        body,
        mesh=fine,
        in_specs=(
            P(None, SEC, None),
            P("op", SEC, None),
            P("op", SEC, None),
            P("op", SEC),
            P("op", SEC),
            P(),
            P(),
        ),
        out_specs=P(None, SEC, "op"),
        check_vma=False,
    )
```

time: 123 us -> 124 us (level)
  blocking collectives: 48.8 us -> 9.62 us
  waiting for transfers between devices: 19.8 us -> 44.2 us
  starting transfers between devices: 30.9 us -> 47.7 us
  local copies, waits for them, and re-layouts: 5.9 us -> 2.59 us
  Pallas kernels: 14.3 us -> 16.9 us
    all_gather x1 -> x0, blocking collectives: 37.8 us -> none  [body(): right = lax.all_gather(right, NEAR, tiled=True)]
    all_to_all x1 -> x2, waiting for transfers between devices: 3.85 us -> 23.6 us  [the longest x1 18.3 us: body(): quarter = lax.all_to_all(quarter, FAR, 0, 0, tiled=True)]
    ppermute x0 -> x2, starting transfers between devices: none -> 16 us  [body(): other = lax.ppermute(right, axis, [(0, 1), (1, 0)])]
    ppermute x0 -> x2, waiting for transfers between devices: none -> 6.14 us  [body(): other = lax.ppermute(right, axis, [(0, 1), (1, 0)])]
    unnamed x10 -> x14, local copies, waits for them, and re-layouts: 5.55 us -> 2.41 us
    pallas_call x1 -> x2, Pallas kernels: 9.42 us -> 11.9 us  [the longest x1 10.1 us: body(): pl.pallas_call(sigma_kernel, grid=(2, vectors), in_specs=[smem, smem, sme...]
    ppermute x1, waiting for transfers between devices: 2.25 us -> 0.01 us  [body(): other = lax.ppermute(own, 'core', [(0, 1), (1, 0)])]
    all_to_all x1, blocking collectives: 11 us -> 9.62 us  [body(): partial = lax.all_to_all(partial, NEAR, 0, 0, tiled=True)]
  transfers between devices with their start and end apart: 4 -> 7, of which waited for: 3 -> 5; matrix products, arithmetic and copies ran while one was open for 0% -> 1% of each run, Pallas kernels for 1% -> 1%
where the time goes in v3:
time: 124 us; the launch traced here: 122 us
  starting transfers between devices  47.7 us (38%)
  waiting for transfers between devices  44.2 us (36%)
  Pallas kernels  16.9 us (14%)
  blocking collectives  9.62 us (8%)
  local copies, waits for them, and re-layouts  2.59 us (2%)
  other arithmetic  1.25 us (1%)
    all_to_all x1, waiting for transfers between devices, body(): quarter = lax.all_to_all(quarter, FAR, 0, 0, tiled=True)  18.3 us
    all_to_all x1, starting transfers between devices, body(): quarter = lax.all_to_all(quarter, FAR, 0, 0, tiled=True)  17.2 us
    ppermute x2, starting transfers between devices, body(): other = lax.ppermute(right, axis, [(0, 1), (1, 0)])  16 us
    all_to_all x1, waiting for transfers between devices, body(): packed = lax.all_to_all(packed, 'op', 0, 0, tiled=True)  14.4 us
    pallas_call x1, Pallas kernels, body(): pl.pallas_call(sigma_kernel, grid=(2, vectors), in_specs=[smem, smem, sme...  10.1 us
    all_to_all x1, blocking collectives, body(): partial = lax.all_to_all(partial, NEAR, 0, 0, tiled=True)  9.62 us
    all_to_all x1, starting transfers between devices, body(): own = lax.all_to_all(left, ('yh', 'zh'), 0, 0, tiled=True)  6.69 us
    ppermute x2, waiting for transfers between devices, body(): other = lax.ppermute(right, axis, [(0, 1), (1, 0)])  6.14 us
  transfers between devices with their start and end apart: 7, of which 5 were waited for; matrix products, arithmetic and copies ran while one was open for 1% of the time, Pallas kernels for 1%

profile of v3, /device:TPU:1, one launch (start us, length us, event | category | flops | bytes accessed | tf_op | source)
XLA Modules:
  0.0 122.5 jit_solution(6720542542596256484)
XLA Ops:
  0.0 0.1 stack.27.at_ref
  0.1 0.0 copy-start
  0.1 1.6 %copy-done = bf16[2,64,8192]{2,1,0:T(8,128)(2,1)S(1)} copy-done((bf16[2,64,8192]{2,1,0:T(8,128)(2,1)S(1)}, bf16[2,64,8192]{2,1,0:T(8,128)(2,1)}, u32[]{:S(2)}) %copy-start) | copy-done | bytes 2097176
  1.7 1.6 %send_trial.1 = bf16[32,64,128]{2,1,0:T(8,128)(2,1)} custom-call(s32[6]{0:T(128)S(1)} %stack.27.at_ref, bf16[2,64,8192]{2,1,0:T(8,128)(2,1)S(1)} %copy-done), custom_call_target="tpu_custom_call" | custom-call | tf_op jit(solution)/shard_map/send_trial/pallas_call | solution.py:160
  3.2 17.2 %all-to-all-start = ((bf16[32,64,128]{2,1,0:T(8,128)(2,1)}), bf16[32,64,128]{2,1,0:T(8,128)(2,1)S(1)}, u32[]{:S(2)}, u32[]{:S(2)}) async-start(bf16[32,64,128]{2,1,0:T(8,128)(2,1)} %send_trial.1), calls=%async_computation | async-start | bytes 1048576 | tf_op jit(solution)/shard_map/all_to_all | solution.py:174
  20.5 1.7 %pack_operators.1 = (bf16[192,128]{1,0:T(8,128)(2,1)}, bf16[192,128]{1,0:T(8,128)(2,1)}) custom-call(s32[1,6]{1,0:T(1,128)} %bitcast.10, s32[1,6]{1,0:T(1,128)} %bitcast.11, bf16[6,64,64]{2,1,0:T(8,128)(2,1)} %left_ref.1, bf16[6,64,64]{2,1,0:T(8,128)(2,1)} %right_ref.1), custom_call_target="tpu_custom_call" | custom-call | tf_op jit(solution)/shard_map/pack_operators/pallas_call | solution.py:150
  22.2 0.0 copy-start.5
  22.2 1.6 %collective-permute-start.2 = (bf16[192,128]{1,0:T(8,128)(2,1)}, bf16[192,128]{1,0:T(8,128)(2,1)S(1)}, u32[]{:S(2)}, u32[]{:S(2)}) collective-permute-start(bf16[192,128]{1,0:T(8,128)(2,1)} %get-tuple-element.8), channel_id=1, source_target_pairs={{0,0},{1,128},{2,256},{3,384},{128,1},{129,129},{130,257},{131,385... | collective-permute-start | bytes 147464 | tf_op jit(solution)/shard_map/ppermute | solution.py:158
  23.7 0.0 collective-permute-done.2.left_ref
  23.7 0.0 copy-start.6
  23.7 18.3 %all-to-all-done.after_ref = bf16[32,64,128]{2,1,0:T(8,128)(2,1)S(1)} async-done(((bf16[32,64,128]{2,1,0:T(8,128)(2,1)}), bf16[32,64,128]{2,1,0:T(8,128)(2,1)S(1)}, u32[]{:S(2)}, u32[]{:S(2)}) %all-to-all-start) | async-done | bytes 524320 | tf_op jit(solution)/shard_map/all_to_all | solution.py:174
  42.1 0.0 copy-done.6
  42.1 0.0 copy-start.3
  42.1 0.8 copy-done.3
  42.9 1.8 %spread_left.1 = bf16[16,192,128]{2,1,0:T(8,128)(2,1)} custom-call(bf16[192,128]{1,0:T(8,128)(2,1)} %copy-done.6, bf16[32,64,128]{2,1,0:T(8,128)(2,1)} %copy-done.3), custom_call_target="tpu_custom_call" | custom-call | tf_op jit(solution)/shard_map/spread_left/pallas_call | solution.py:183
  44.7 6.7 %all-to-all-start.2 = ((bf16[16,192,128]{2,1,0:T(8,128)(2,1)}), bf16[16,192,128]{2,1,0:T(8,128)(2,1)S(1)}, u32[]{:S(2)}, u32[]{:S(2)}) async-start(bf16[16,192,128]{2,1,0:T(8,128)(2,1)} %spread_left.1), calls=%async_computation.2 | async-start | bytes 1572864 | tf_op jit(solution)/shard_map/all_to_all | solution.py:190
  51.4 0.0 copy-start.4
  51.4 0.0 copy-done.5
  51.4 3.2 %collective-permute-start = (bf16[192,128]{1,0:T(8,128)(2,1)S(1)}, bf16[192,128]{1,0:T(8,128)(2,1)S(1)}, u32[]{:S(2)}, u32[]{:S(2)}) collective-permute-start(bf16[192,128]{1,0:T(8,128)(2,1)S(1)} %copy-done.5), channel_id=1, source_target_pairs={{0,8},{8,0},{1,9},{9,1},{2,10},{10,2},{3,11},{11,3},{4,12},{12,4},... | collective-permute-start | bytes 147464 | tf_op jit(solution)/shard_map/ppermute | solution.py:177
  54.6 3.9 %collective-permute-done = bf16[192,128]{1,0:T(8,128)(2,1)S(1)} collective-permute-done((bf16[192,128]{1,0:T(8,128)(2,1)S(1)}, bf16[192,128]{1,0:T(8,128)(2,1)S(1)}, u32[]{:S(2)}, u32[]{:S(2)}) %collective-permute-start) | collective-permute-done | bytes 49184 | tf_op jit(solution)/shard_map/ppermute | solution.py:177
  58.5 12.7 %collective-permute-start.1 = (bf16[384,128]{1,0:T(8,128)(2,1)S(1)}, bf16[384,128]{1,0:T(8,128)(2,1)S(1)}, u32[]{:S(2)}, u32[]{:S(2)}) collective-permute-start(bf16[384,128]{1,0:T(8,128)(2,1)S(1)} %pad_maximum_fusion.2), channel_id=1, source_target_pairs={{0,64},{64,0},{1,65},{65,1},{2,66},{66,2},{3,67},{67,3},{4,68},{68... | collective-permute-start | bytes 294920 | tf_op jit(solution)/shard_map/ppermute | solution.py:177
  71.3 2.3 %collective-permute-done.1 = bf16[384,128]{1,0:T(8,128)(2,1)S(1)} collective-permute-done((bf16[384,128]{1,0:T(8,128)(2,1)S(1)}, bf16[384,128]{1,0:T(8,128)(2,1)S(1)}, u32[]{:S(2)}, u32[]{:S(2)}) %collective-permute-start.1) | collective-permute-done | bytes 98336 | tf_op jit(solution)/shard_map/ppermute | solution.py:177
  73.6 0.1 broadcast_in_dim.2
  73.7 0.0 copy-done.4
  73.7 1.2 pad_maximum_fusion
  74.9 0.0 copy-start.1
  74.9 0.0 copy-start.2
  74.9 5.3 %all-to-all-done.2.own_ref = bf16[16,192,128]{2,1,0:T(8,128)(2,1)S(1)} async-done(((bf16[16,192,128]{2,1,0:T(8,128)(2,1)}), bf16[16,192,128]{2,1,0:T(8,128)(2,1)S(1)}, u32[]{:S(2)}, u32[]{:S(2)}) %all-to-all-start.2) | async-done | bytes 786464 | tf_op jit(solution)/shard_map/all_to_all | solution.py:190
  80.3 3.5 %all-to-all-start.1 = ((bf16[4,1280,128]{2,1,0:T(8,128)(2,1)}), bf16[4,1280,128]{2,1,0:T(8,128)(2,1)S(1)}, u32[]{:S(2)}, u32[]{:S(2)}) async-start(bf16[4,1280,128]{2,1,0:T(8,128)(2,1)} %pad_maximum_fusion), calls=%async_computation.1 | async-start | bytes 2621440 | tf_op jit(solution)/shard_map/all_to_all | solution.py:197
  83.8 2.7 %collective-permute-start.3 = (bf16[16,192,128]{2,1,0:T(8,128)(2,1)S(1)}, bf16[16,192,128]{2,1,0:T(8,128)(2,1)S(1)}, u32[]{:S(2)}, u32[]{:S(2)}) collective-permute-start(bf16[16,192,128]{2,1,0:T(8,128)(2,1)S(1)} %all-to-all-done.2.own_ref), channel_id=1, source_target_pairs={{0,4},{4,0},{1,5},{5,1},{2,6},{6,2},{3,7},{7,3},{8,12},{12,8},{9,1... | collective-permute-start | bytes 2359304 | tf_op jit(solution)/shard_map/ppermute | solution.py:191
  86.5 14.4 %all-to-all-done.1.xr_ref = bf16[4,1280,128]{2,1,0:T(8,128)(2,1)S(1)} async-done(((bf16[4,1280,128]{2,1,0:T(8,128)(2,1)}), bf16[4,1280,128]{2,1,0:T(8,128)(2,1)S(1)}, u32[]{:S(2)}, u32[]{:S(2)}) %all-to-all-start.1) | async-done | bytes 1310752 | tf_op jit(solution)/shard_map/all_to_all | solution.py:197
  100.9 0.0 collective-permute-done.3.other_ref
  100.9 0.0 copy-done.1
  100.9 0.0 copy-done.2
  101.0 10.1 %sigma_blocks.1 = bf16[4,2,64,512]{3,2,1,0:T(8,128)(2,1)S(1)} custom-call(s32[6]{0:T(128)S(1)} %stack.27.at_ref, s32[128]{0:T(128)S(1)} %copy-done.1, s32[128]{0:T(128)S(1)} %copy-done.2, bf16[4,1280,128]{2,1,0:T(8,128)(2,1)S(1)} %all-to-all-done.1.xr_ref, bf16[16,192,128]{2,1,0:T(8,128)(2,1)S(1)} %all-to-all-done.2.own_ref, ...), custom_call_target="tpu_custom_call" | custom-call | tf_op jit(solution)/shard_map/sigma_blocks/pallas_call | solution.py:199
  111.1 9.6 %all_to_all.20.in_ref = bf16[4,2,64,512]{3,2,1,0:T(8,128)(2,1)} all-to-all(bf16[4,2,64,512]{3,2,1,0:T(8,128)(2,1)S(1)} %sigma_blocks.1), channel_id=1, replica_groups=mesh['yh'=4,'yl'=2,'zh'=4,'zl'=2,'core'=2,'op'=4] {'yl','zl'}, dimensions={0} | all-to-all | bytes 1048576 | tf_op jit(solution)/shard_map/all_to_all | solution.py:221
  120.7 1.8 %merge_sectors.1 = bf16[2,64,2048]{2,1,0:T(8,128)(2,1)} custom-call(bf16[4,2,64,512]{3,2,1,0:T(8,128)(2,1)} %all_to_all.20.in_ref), custom_call_target="tpu_custom_call" | custom-call | tf_op jit(solution)/shard_map/merge_sectors/pallas_call | solution.py:222
  (4 shorter events, 0.1 us)
Async XLA Ops:
  0.1 1.6 %copy-start = (bf16[2,64,8192]{2,1,0:T(8,128)(2,1)S(1)}, bf16[2,64,8192]{2,1,0:T(8,128)(2,1)}, u32[]{:S(2)}) copy-start(bf16[2,64,8192]{2,1,0:T(8,128)(2,1)} %x_ref.1) | copy-start | bytes 6291460
  3.2 38.8 %all-to-all-start = ((bf16[32,64,128]{2,1,0:T(8,128)(2,1)}), bf16[32,64,128]{2,1,0:T(8,128)(2,1)S(1)}, u32[]{:S(2)}, u32[]{:S(2)}) async-start(bf16[32,64,128]{2,1,0:T(8,128)(2,1)} %send_trial.1), calls=%async_computation | async-start | bytes 1048576 | tf_op jit(solution)/shard_map/all_to_all | solution.py:174
  22.2 29.2 %copy-start.5 = (bf16[192,128]{1,0:T(8,128)(2,1)S(1)}, bf16[192,128]{1,0:T(8,128)(2,1)}, u32[]{:S(2)}) copy-start(bf16[192,128]{1,0:T(8,128)(2,1)} %get-tuple-element.7) | copy-start | bytes 147460
  22.2 1.6 %collective-permute-start.2 = (bf16[192,128]{1,0:T(8,128)(2,1)}, bf16[192,128]{1,0:T(8,128)(2,1)S(1)}, u32[]{:S(2)}, u32[]{:S(2)}) collective-permute-start(bf16[192,128]{1,0:T(8,128)(2,1)} %get-tuple-element.8), channel_id=1, source_target_pairs={{0,0},{1,128},{2,256},{3,384},{128,1},{129,129},{130,257},{131,385... | collective-permute-start | bytes 147464 | tf_op jit(solution)/shard_map/ppermute | solution.py:158
  23.7 18.3 %copy-start.6 = (bf16[192,128]{1,0:T(8,128)(2,1)}, bf16[192,128]{1,0:T(8,128)(2,1)S(1)}, u32[]{:S(2)}) copy-start(bf16[192,128]{1,0:T(8,128)(2,1)S(1)} %collective-permute-done.2.left_ref) | copy-start | bytes 147460
  42.1 0.8 copy-start.3
  44.7 35.6 %all-to-all-start.2 = ((bf16[16,192,128]{2,1,0:T(8,128)(2,1)}), bf16[16,192,128]{2,1,0:T(8,128)(2,1)S(1)}, u32[]{:S(2)}, u32[]{:S(2)}) async-start(bf16[16,192,128]{2,1,0:T(8,128)(2,1)} %spread_left.1), calls=%async_computation.2 | async-start | bytes 1572864 | tf_op jit(solution)/shard_map/all_to_all | solution.py:190
  51.4 22.4 %copy-start.4 = (bf16[32,64,128]{2,1,0:T(8,128)(2,1)S(1)}, bf16[32,64,128]{2,1,0:T(8,128)(2,1)}, u32[]{:S(2)}) copy-start(bf16[32,64,128]{2,1,0:T(8,128)(2,1)} %copy-done.3) | copy-start | bytes 1572868
  51.4 7.1 %collective-permute-start = (bf16[192,128]{1,0:T(8,128)(2,1)S(1)}, bf16[192,128]{1,0:T(8,128)(2,1)S(1)}, u32[]{:S(2)}, u32[]{:S(2)}) collective-permute-start(bf16[192,128]{1,0:T(8,128)(2,1)S(1)} %copy-done.5), channel_id=1, source_target_pairs={{0,8},{8,0},{1,9},{9,1},{2,10},{10,2},{3,11},{11,3},{4,12},{12,4},... | collective-permute-start | bytes 147464 | tf_op jit(solution)/shard_map/ppermute | solution.py:177
  58.5 15.0 %collective-permute-start.1 = (bf16[384,128]{1,0:T(8,128)(2,1)S(1)}, bf16[384,128]{1,0:T(8,128)(2,1)S(1)}, u32[]{:S(2)}, u32[]{:S(2)}) collective-permute-start(bf16[384,128]{1,0:T(8,128)(2,1)S(1)} %pad_maximum_fusion.2), channel_id=1, source_target_pairs={{0,64},{64,0},{1,65},{65,1},{2,66},{66,2},{3,67},{67,3},{4,68},{68... | collective-permute-start | bytes 294920 | tf_op jit(solution)/shard_map/ppermute | solution.py:177
  74.9 26.0 %copy-start.1 = (s32[128]{0:T(128)S(1)}, s32[128]{0:T(128)}, u32[]{:S(2)}) copy-start(s32[128]{0:T(128)} %lcharge_ref.1) | copy-start | bytes 1540
  74.9 26.0 %copy-start.2 = (s32[128]{0:T(128)S(1)}, s32[128]{0:T(128)}, u32[]{:S(2)}) copy-start(s32[128]{0:T(128)} %rcharge_ref.1) | copy-start | bytes 1540
  80.3 20.7 %all-to-all-start.1 = ((bf16[4,1280,128]{2,1,0:T(8,128)(2,1)}), bf16[4,1280,128]{2,1,0:T(8,128)(2,1)S(1)}, u32[]{:S(2)}, u32[]{:S(2)}) async-start(bf16[4,1280,128]{2,1,0:T(8,128)(2,1)} %pad_maximum_fusion), calls=%async_computation.1 | async-start | bytes 2621440 | tf_op jit(solution)/shard_map/all_to_all | solution.py:197
  83.8 17.1 %collective-permute-start.3 = (bf16[16,192,128]{2,1,0:T(8,128)(2,1)S(1)}, bf16[16,192,128]{2,1,0:T(8,128)(2,1)S(1)}, u32[]{:S(2)}, u32[]{:S(2)}) collective-permute-start(bf16[16,192,128]{2,1,0:T(8,128)(2,1)S(1)} %all-to-all-done.2.own_ref), channel_id=1, source_target_pairs={{0,4},{4,0},{1,5},{5,1},{2,6},{6,2},{3,7},{7,3},{8,12},{12,8},{9,1... | collective-permute-start | bytes 2359304 | tf_op jit(solution)/shard_map/ppermute | solution.py:191

commit v4 on v3

v4 whole, which is shorter than its diff:
```python
import jax
import jax.numpy as jnp
from jax import lax
from jax.experimental import pallas as pl
from jax.experimental.pallas import tpu as pltpu
from jax.sharding import Mesh, PartitionSpec as P

target_charge = 6
XDIM, YH, YL, ZH, ZL, CORE = 4, 4, 2, 4, 2, 2
SEC = ("yh", "yl", "zh", "zl", "core")
FAR = ("yh", "zh")
NEAR = ("yl", "zl")
NT = (((1,), (1,)), ((), ()))
BLOCK = 64
WIDE = 2 * BLOCK
HALF = BLOCK // 2
GROUP = 4 * BLOCK
TERMS = 24
HERE = TERMS // XDIM
PAIRS = HERE // 2
XROWS = 2 * HALF
RROWS = PAIRS * BLOCK
FROM = ZH * CORE
VMEM = 24 * 1024 * 1024
SMALL = 8 * 1024 * 1024


def swap_halves(piece):
    return jnp.concatenate([piece[:, BLOCK:], piece[:, :BLOCK]], axis=1)


def placed(piece, second, to_second):
    lane = lax.broadcasted_iota(jnp.int32, piece.shape, 1)
    moved = piece if second == to_second else swap_halves(piece)
    keep = (lane >= BLOCK) if to_second else (lane < BLOCK)
    return jnp.where(keep, moved, jnp.zeros_like(moved))


def prepare_kernel(at_ref, lc_ref, rc_ref, left_ref, right_ref, x_ref, sent_ref, rout_ref):
    wide = CORE * XROWS
    for p in range(PAIRS):
        pairs = []
        for c_ref, in_ref in ((lc_ref, left_ref), (rc_ref, right_ref)):
            both = []
            for t in (2 * p, 2 * p + 1):
                scale = c_ref[0, t].astype(jnp.float32)
                both.append((in_ref[t].astype(jnp.float32) * scale).astype(jnp.bfloat16))
            pairs.append(jnp.concatenate(both, axis=1))
        rout_ref[p * BLOCK:(p + 1) * BLOCK, :] = pairs[1]
        for to in range(YH * ZH):
            sent_ref[to, wide + p * BLOCK:wide + (p + 1) * BLOCK, :] = pairs[0]
    for yh in range(YH):
        for yl in range(YL):
            for zh in range(ZH):
                at = ((yh * YL + yl) * ZH + zh) * ZL
                first = x_ref[0, :, at * WIDE:(at + 1) * WIDE]
                second = x_ref[0, :, (at + 1) * WIDE:(at + 2) * WIDE]
                for c in range(CORE):
                    lanes = slice(c * BLOCK, (c + 1) * BLOCK)
                    rows = slice(c * XROWS + yl * HALF, c * XROWS + (yl + 1) * HALF)
                    sent_ref[yh * ZH + zh, rows, :] = jnp.concatenate(
                        [first[:, lanes], second[:, lanes]], axis=1
                    )


def plane_kernel(got_ref, r0_ref, r1_ref, r2_ref, r3_ref, out_ref, right_ref):
    wide = CORE * XROWS
    for at in range(YH * ZH):
        q, z = at // ZH, at % ZH
        out_ref[q, z * wide:(z + 1) * wide, :] = got_ref[at, :wide, :]
        rows = slice(ZH * wide + z * RROWS, ZH * wide + (z + 1) * RROWS)
        out_ref[q, rows, :] = got_ref[at, wide:, :]
    for d, ref in enumerate((r0_ref, r1_ref, r2_ref, r3_ref)):
        right_ref[d * RROWS:(d + 1) * RROWS, :] = ref[...]


def core_kernel(at_ref, got_ref, r0_ref, r1_ref, r2_ref, r3_ref, own_ref, give_ref, near_ref):
    core = at_ref[5]
    for e, ref in enumerate((r0_ref, r1_ref, r2_ref, r3_ref)):
        near_ref[jnp.bitwise_xor(at_ref[2] * ZL + at_ref[4], e)] = ref[...]
    for x in range(XDIM):
        for z in range(ZH):
            rows = slice(z * XROWS, (z + 1) * XROWS)
            for to_ref, c in ((own_ref, core), (give_ref, 1 - core)):
                at = pl.multiple_of((z * CORE + c) * XROWS, XROWS)
                to_ref[x, rows, :] = got_ref[x, pl.ds(at, XROWS), :]
        left = got_ref[x, FROM * XROWS:, :]
        own_ref[x, ZH * XROWS:, :] = left
        give_ref[x, ZH * XROWS:, :] = left


def sigma_kernel(c, at_ref, lcharge_ref, rcharge_ref, got_ref, near_ref, *refs):
    out_ref, right_ref, left_ref, half_ref = refs[-4:]
    v = pl.program_id(0)
    x_at, yh_at, yl_at, zh_at, zl_at, core = [at_ref[n] for n in range(6)]

    @pl.when(v == 0)
    def _():
        right_ref[...] = jnp.zeros_like(right_ref)
        left_ref[...] = jnp.zeros_like(left_ref)
        for b in range(4):
            for d in range(XDIM):
                first = jnp.bitwise_xor(x_at, d) * HERE
                for p in range(PAIRS):
                    at = d * RROWS + p * BLOCK
                    piece = near_ref[b, at:at + BLOCK, :]
                    for s in range(2):
                        right_ref[first + 2 * p + s, b * BLOCK:(b + 1) * BLOCK,
                                  (b // 2) * WIDE:(b // 2 + 1) * WIDE] = placed(piece, s, b % 2)
        for x in range(XDIM):
            for z in range(ZH):
                for p in range(PAIRS):
                    at = ZH * XROWS + z * RROWS + p * BLOCK
                    piece = got_ref[x, at:at + BLOCK, :]
                    for s in range(2):
                        at = (x * HERE + 2 * p + s) * GROUP + (z // 2) * WIDE
                        left_ref[z * BLOCK:(z + 1) * BLOCK, at:at + WIDE] = placed(piece, s, z % 2)

    rows = []
    for z in range(ZH):
        for h in range(2):
            piece = got_ref[v * 2 + h, z * XROWS:(z + 1) * XROWS, :]
            rows.append(jnp.concatenate([piece[:HALF], piece[HALF:]], axis=1))
    state = jnp.concatenate(rows, axis=0)
    for t in range(TERMS):
        out = lax.dot_general(right_ref[t], state, NT, preferred_element_type=jnp.float32)
        half_ref[:, t * GROUP:(t + 1) * GROUP] = out.astype(half_ref.dtype)
    out = lax.dot_general(half_ref[...], left_ref[...], NT, preferred_element_type=jnp.float32)

    lane = lax.broadcasted_iota(jnp.int32, (1, GROUP), 1) // BLOCK
    charge = jnp.zeros((1, GROUP), jnp.int32)
    for z in range(ZH):
        sector = (((x_at * YL + yl_at) * ZH + z) * ZL + zl_at) * CORE + jnp.bitwise_xor(core, c)
        charge = jnp.where(lane == z, lcharge_ref[sector], charge)
    for b in range(4):
        sector = (((yh_at * YL + b // 2) * ZH + zh_at) * ZL + b % 2) * CORE + core
        allowed = jnp.abs(charge + rcharge_ref[sector] - target_charge) <= 1
        block = out[b * BLOCK:(b + 1) * BLOCK]
        out_ref[b, 0, 0] = jnp.where(allowed, block, jnp.zeros_like(block)).astype(out_ref.dtype)


def merge_kernel(at_ref, in_ref, out_ref):
    core = at_ref[5]
    for yl in range(YL):
        for zl in range(ZL):
            for m in range(ZH // 2):
                low = in_ref[yl * ZL + zl, core, 0, :, m * WIDE:(m + 1) * WIDE]
                high = in_ref[yl * ZL + zl, 1 - core, 0, :, m * WIDE:(m + 1) * WIDE]
                for h in range(2):
                    lanes = slice(h * BLOCK, (h + 1) * BLOCK)
                    at = ((yl * ZH + 2 * m + h) * ZL + zl) * WIDE
                    out_ref[0, :, at:at + WIDE] = jnp.concatenate(
                        [low[:, lanes], high[:, lanes]], axis=1
                    )


def body(
    trial_state,
    left_operators,
    right_operators,
    left_coupling,
    right_coupling,
    left_charge,
    right_charge,
):
    vectors, _, states = trial_state.shape
    at = jnp.stack([lax.axis_index(n) for n in ("op",) + SEC]).astype(jnp.int32)
    smem = pl.BlockSpec(memory_space=pltpu.SMEM)
    vmem = pl.BlockSpec(memory_space=pltpu.VMEM)
    params = pltpu.CompilerParams(vmem_limit_bytes=VMEM)
    small = pltpu.CompilerParams(vmem_limit_bytes=SMALL)

    wide = CORE * XROWS
    message = jax.ShapeDtypeStruct((YH * ZH, wide + RROWS, WIDE), jnp.bfloat16)
    operator = jax.ShapeDtypeStruct((RROWS, WIDE), jnp.bfloat16)

    def whole(shape):
        return pl.BlockSpec(shape, lambda i, at: (0,) * len(shape))

    sent, right = pl.pallas_call(
        prepare_kernel,
        grid_spec=pltpu.PrefetchScalarGridSpec(
            num_scalar_prefetch=1,
            grid=(1,),
            in_specs=[
                smem,
                smem,
                whole(left_operators.shape),
                whole(right_operators.shape),
                pl.BlockSpec((1, HALF, states), lambda i, at: (at[0] // 2, lax.rem(at[0], 2), 0)),
            ],
            out_specs=[whole(message.shape), whole(operator.shape)],
        ),
        out_shape=[message, operator],
        name="prepare_parts",
    )(
        at,
        left_coupling.reshape(1, HERE),
        right_coupling.reshape(1, HERE),
        left_operators,
        right_operators,
        trial_state,
    )
    got = lax.all_to_all(sent, FAR, 0, 0, tiled=True)

    rights = [right] + [
        lax.ppermute(right, "op", [(n, n ^ d) for n in range(XDIM)]) for d in (1, 2, 3)
    ]

    plane = jax.ShapeDtypeStruct((XDIM, ZH * message.shape[1], WIDE), jnp.bfloat16)
    got, right = pl.pallas_call(
        plane_kernel,
        in_specs=[vmem] * 5,
        out_specs=[vmem] * 2,
        out_shape=[plane, jax.ShapeDtypeStruct((XDIM * RROWS, WIDE), jnp.bfloat16)],
        compiler_params=small,
        name="sort_planes",
    )(got, *rights)
    got = lax.all_to_all(got, "op", 0, 0, tiled=True)

    rights = [right] + [
        lax.ppermute(right, NEAR, [(n, n ^ d) for n in range(YL * ZL)]) for d in (1, 2, 3)
    ]

    mine = jax.ShapeDtypeStruct((XDIM, ZH * (XROWS + RROWS), WIDE), jnp.bfloat16)
    near = jax.ShapeDtypeStruct((YL * ZL,) + right.shape, jnp.bfloat16)
    own, give, right = pl.pallas_call(
        core_kernel,
        in_specs=[smem] + [vmem] * 5,
        out_specs=[vmem] * 3,
        out_shape=[mine, mine, near],
        compiler_params=small,
        name="sort_cores",
    )(at, got, *rights)
    other = lax.ppermute(give, "core", [(0, 1), (1, 0)])

    partial = None
    for c, got in enumerate((own, other)):
        before = [] if partial is None else [partial]
        partial = pl.pallas_call(
            lambda *refs, c=c: sigma_kernel(c, *refs),
            grid=(vectors,),
            in_specs=[smem] * 3
            + [pl.BlockSpec(mine.shape, lambda v: (0, 0, 0))]
            + [pl.BlockSpec(near.shape, lambda v: (0, 0, 0))]
            + [pl.BlockSpec(memory_space=pl.ANY) for _ in before],
            out_specs=pl.BlockSpec((4, 1, 1, BLOCK, GROUP), lambda v, c=c: (0, c, v, 0, 0)),
            out_shape=jax.ShapeDtypeStruct((4, CORE, vectors, BLOCK, GROUP), jnp.bfloat16),
            scratch_shapes=[
                pltpu.VMEM((TERMS, GROUP, GROUP), jnp.bfloat16),
                pltpu.VMEM((GROUP, TERMS * GROUP), jnp.bfloat16),
                pltpu.VMEM((GROUP, TERMS * GROUP), jnp.bfloat16),
            ],
            input_output_aliases={5: 0} if before else {},
            compiler_params=params,
            name="sigma_blocks",
        )(at, left_charge, right_charge, got, right, *before)

    partial = lax.all_to_all(partial, NEAR, 0, 0, tiled=True)
    return pl.pallas_call(
        merge_kernel,
        grid=(vectors,),
        in_specs=[
            smem,
            pl.BlockSpec((4, CORE, 1, BLOCK, GROUP), lambda v: (0, 0, v, 0, 0)),
        ],
        out_specs=pl.BlockSpec((1, BLOCK, 8 * GROUP), lambda v: (v, 0, 0)),
        out_shape=jax.ShapeDtypeStruct((vectors, BLOCK, 8 * GROUP), jnp.bfloat16),
        compiler_params=small,
        name="merge_sectors",
    )(at, partial)


def solution(mesh):
    fine = Mesh(mesh.devices.reshape(YH, YL, ZH, ZL, CORE, XDIM), SEC + ("op",))
    return jax.shard_map(
        body,
        mesh=fine,
        in_specs=(
            P(None, SEC, None),
            P("op", SEC, None),
            P("op", SEC, None),
            P("op", SEC),
            P("op", SEC),
            P(),
            P(),
        ),
        out_specs=P(None, SEC, "op"),
        check_vma=False,
    )
```

time: 124 us -> 112 us (0.903); the launches traced: 122 us -> 112 us
  waiting for transfers between devices: 44.2 us -> 37.8 us
  starting transfers between devices: 47.7 us -> 44.8 us
  local copies, waits for them, and re-layouts: 2.59 us -> 0.64 us
  other arithmetic: 1.25 us -> 0 us
    all_to_all x3 -> x2, waiting for transfers between devices: 38.1 us -> 29.4 us  [the longest x1 29.4 us: body(): got = lax.all_to_all(sent, FAR, 0, 0, tiled=True)]
    all_to_all x3 -> x2, starting transfers between devices: 27.5 us -> 20.5 us  [the longest x1 16.4 us: body(): got = lax.all_to_all(sent, FAR, 0, 0, tiled=True)]
    ppermute x4 -> x7, starting transfers between devices: 20.3 us -> 24.3 us  [the longest x3 8.98 us: body(): lax.ppermute(right, 'op', [(n, n ^ d) for n in range(XDIM)])]
    unnamed x14 -> x8, local copies, waits for them, and re-layouts: 2.41 us -> 0.01 us
    ppermute x4 -> x7, waiting for transfers between devices: 6.14 us -> 8.39 us  [the longest x3 5.44 us: body(): lax.ppermute(right, NEAR, [(n, n ^ d) for n in range(YL * ZL)])]
    pallas_call x5 -> x6, Pallas kernels: 16.9 us -> 18.1 us  [the longest x2 11.3 us: body(): pl.pallas_call(lambda *refs, c=c: sigma_kernel(c, *refs), grid=(vectors,)...]
  transfers between devices with their start and end apart: 7 -> 9, of which waited for: 5 -> 5; matrix products, arithmetic and copies ran while one was open for 1% -> 0% of each run, Pallas kernels for 1% -> 5%
where the time goes in v4:
time: 112 us
  starting transfers between devices  44.8 us (40%)
  waiting for transfers between devices  37.8 us (34%)
  Pallas kernels  18.1 us (16%)
  blocking collectives  10.4 us (9%)
    all_to_all x1, waiting for transfers between devices, body(): got = lax.all_to_all(sent, FAR, 0, 0, tiled=True)  29.4 us
    all_to_all x1, starting transfers between devices, body(): got = lax.all_to_all(sent, FAR, 0, 0, tiled=True)  16.4 us
    pallas_call x2, Pallas kernels, body(): pl.pallas_call(lambda *refs, c=c: sigma_kernel(c, *refs), grid=(vectors,)...  11.3 us
    all_to_all x1, blocking collectives, body(): partial = lax.all_to_all(partial, NEAR, 0, 0, tiled=True)  10.4 us
    ppermute x3, starting transfers between devices, body(): lax.ppermute(right, 'op', [(n, n ^ d) for n in range(XDIM)])  8.98 us
    ppermute x3, starting transfers between devices, body(): lax.ppermute(right, NEAR, [(n, n ^ d) for n in range(YL * ZL)])  8.49 us
    ppermute x1, starting transfers between devices, body(): other = lax.ppermute(give, 'core', [(0, 1), (1, 0)])  6.8 us
    ppermute x3, waiting for transfers between devices, body(): lax.ppermute(right, NEAR, [(n, n ^ d) for n in range(YL * ZL)])  5.44 us
  transfers between devices with their start and end apart: 9, of which 5 were waited for; matrix products, arithmetic and copies ran while one was open for 0% of the time, Pallas kernels for 5%

profile of v4, /device:TPU:1, one launch (start us, length us, event | category | flops | bytes accessed | tf_op | source)
XLA Modules:
  0.0 111.9 jit_solution(13140201450841020402)
XLA Ops:
  0.0 0.6 stack.27.at_ref.refs_0_
  0.6 3.2 %prepare_parts.1 = (bf16[16,320,128]{2,1,0:T(8,128)(2,1)}, bf16[192,128]{1,0:T(8,128)(2,1)}) custom-call(s32[6]{0:T(128)} %stack.27.at_ref.refs_0_, s32[1,6]{1,0:T(1,128)} %bitcast.8, s32[1,6]{1,0:T(1,128)} %bitcast.9, bf16[6,64,64]{2,1,0:T(8,128)(2,1)} %left_ref.1, bf16[6,64,64]{2,1,0:T(8,128)(2,1)} %right_ref.1, bf16[2,64,8192]{2,1,0:T(8,128)(2,1)} %x_ref.1), custom_call_target="tpu_custom_call" | custom-call | tf_op jit(solution)/shard_map/prepare_parts/pallas_call | solution.py:180
  3.8 0.0 copy-start
  3.8 16.4 %all-to-all-start = ((bf16[16,320,128]{2,1,0:T(8,128)(2,1)}), bf16[16,320,128]{2,1,0:T(8,128)(2,1)S(1)}, u32[]{:S(2)}, u32[]{:S(2)}) async-start(bf16[16,320,128]{2,1,0:T(8,128)(2,1)} %get-tuple-element.12), calls=%async_computation | async-start | bytes 2621440 | tf_op jit(solution)/shard_map/all_to_all | solution.py:204
  20.2 0.0 copy-done
  20.2 4.4 %collective-permute-start.2 = (bf16[192,128]{1,0:T(8,128)(2,1)S(1)}, bf16[192,128]{1,0:T(8,128)(2,1)S(1)}, u32[]{:S(2)}, u32[]{:S(2)}) collective-permute-start(bf16[192,128]{1,0:T(8,128)(2,1)S(1)} %copy-done), channel_id=1, source_target_pairs={{0,3},{1,2},{2,1},{3,0},{4,7},{5,6},{6,5},{7,4},{8,11},{9,10},{10,... | collective-permute-start | bytes 147464 | tf_op jit(solution)/shard_map/ppermute | solution.py:207
  24.6 2.4 %collective-permute-start.1 = (bf16[192,128]{1,0:T(8,128)(2,1)S(1)}, bf16[192,128]{1,0:T(8,128)(2,1)S(1)}, u32[]{:S(2)}, u32[]{:S(2)}) collective-permute-start(bf16[192,128]{1,0:T(8,128)(2,1)S(1)} %copy-done), channel_id=1, source_target_pairs={{0,2},{1,3},{2,0},{3,1},{4,6},{5,7},{6,4},{7,5},{8,10},{9,11},{10,... | collective-permute-start | bytes 147464 | tf_op jit(solution)/shard_map/ppermute | solution.py:207
  27.0 2.2 %collective-permute-start = (bf16[192,128]{1,0:T(8,128)(2,1)S(1)}, bf16[192,128]{1,0:T(8,128)(2,1)S(1)}, u32[]{:S(2)}, u32[]{:S(2)}) collective-permute-start(bf16[192,128]{1,0:T(8,128)(2,1)S(1)} %copy-done), channel_id=1, source_target_pairs={{0,1},{1,0},{2,3},{3,2},{4,5},{5,4},{6,7},{7,6},{8,9},{9,8},{10,11... | collective-permute-start | bytes 147464 | tf_op jit(solution)/shard_map/ppermute | solution.py:207
  29.2 0.0 collective-permute-done.2.r3_ref
  29.2 2.0 %collective-permute-done.1.r2_ref = bf16[192,128]{1,0:T(8,128)(2,1)S(1)} collective-permute-done((bf16[192,128]{1,0:T(8,128)(2,1)S(1)}, bf16[192,128]{1,0:T(8,128)(2,1)S(1)}, u32[]{:S(2)}, u32[]{:S(2)}) %collective-permute-start.1) | collective-permute-done | bytes 49184 | tf_op jit(solution)/shard_map/ppermute | solution.py:207
  31.2 0.9 collective-permute-done.r1_ref
  32.2 29.4 %all-to-all-done.got_ref = bf16[16,320,128]{2,1,0:T(8,128)(2,1)S(1)} async-done(((bf16[16,320,128]{2,1,0:T(8,128)(2,1)}), bf16[16,320,128]{2,1,0:T(8,128)(2,1)S(1)}, u32[]{:S(2)}, u32[]{:S(2)}) %all-to-all-start) | async-done | bytes 1310752 | tf_op jit(solution)/shard_map/all_to_all | solution.py:204
  61.6 1.2 %sort_planes.1 = (bf16[4,1280,128]{2,1,0:T(8,128)(2,1)}, bf16[768,128]{1,0:T(8,128)(2,1)S(1)}) custom-call(bf16[16,320,128]{2,1,0:T(8,128)(2,1)S(1)} %all-to-all-done.got_ref, bf16[192,128]{1,0:T(8,128)(2,1)S(1)} %copy-done, bf16[192,128]{1,0:T(8,128)(2,1)S(1)} %collective-permute-done.r1_ref, bf16[192,128]{1,0:T(8,128)(2,1)S(1)} %collective-permute-done.1.r2_ref, ...), custom_call_target="tpu_custom_call" | custom-call | tf_op jit(solution)/shard_map/sort_planes/pallas_call | solution.py:211
  62.8 0.0 copy-start.1
  62.8 4.1 %all-to-all-start.1 = ((bf16[4,1280,128]{2,1,0:T(8,128)(2,1)}), bf16[4,1280,128]{2,1,0:T(8,128)(2,1)S(1)}, u32[]{:S(2)}, u32[]{:S(2)}) async-start(bf16[4,1280,128]{2,1,0:T(8,128)(2,1)} %get-tuple-element.14), calls=%async_computation.1 | async-start | bytes 2621440 | tf_op jit(solution)/shard_map/all_to_all | solution.py:219
  66.9 0.0 copy-start.2
  66.9 0.0 copy-start.3
  66.9 2.0 %collective-permute-start.5 = (bf16[768,128]{1,0:T(8,128)(2,1)S(1)}, bf16[768,128]{1,0:T(8,128)(2,1)S(1)}, u32[]{:S(2)}, u32[]{:S(2)}) collective-permute-start(bf16[768,128]{1,0:T(8,128)(2,1)S(1)} %get-tuple-element.15.r0_ref), channel_id=1, source_target_pairs={{0,72},{8,64},{64,8},{72,0},{1,73},{9,65},{65,9},{73,1},{2,74},{10... | collective-permute-start | bytes 589832 | tf_op jit(solution)/shard_map/ppermute | solution.py:222
  69.0 1.9 %collective-permute-start.4 = (bf16[768,128]{1,0:T(8,128)(2,1)S(1)}, bf16[768,128]{1,0:T(8,128)(2,1)S(1)}, u32[]{:S(2)}, u32[]{:S(2)}) collective-permute-start(bf16[768,128]{1,0:T(8,128)(2,1)S(1)} %get-tuple-element.15.r0_ref), channel_id=1, source_target_pairs={{0,64},{8,72},{64,0},{72,8},{1,65},{9,73},{65,1},{73,9},{2,66},{10... | collective-permute-start | bytes 589832 | tf_op jit(solution)/shard_map/ppermute | solution.py:222
  70.9 4.5 %collective-permute-start.3 = (bf16[768,128]{1,0:T(8,128)(2,1)S(1)}, bf16[768,128]{1,0:T(8,128)(2,1)S(1)}, u32[]{:S(2)}, u32[]{:S(2)}) collective-permute-start(bf16[768,128]{1,0:T(8,128)(2,1)S(1)} %get-tuple-element.15.r0_ref), channel_id=1, source_target_pairs={{0,8},{8,0},{64,72},{72,64},{1,9},{9,1},{65,73},{73,65},{2,10},{10... | collective-permute-start | bytes 589832 | tf_op jit(solution)/shard_map/ppermute | solution.py:222
  75.4 0.0 collective-permute-done.5.r3_ref
  75.4 1.4 %collective-permute-done.4.r2_ref = bf16[768,128]{1,0:T(8,128)(2,1)S(1)} collective-permute-done((bf16[768,128]{1,0:T(8,128)(2,1)S(1)}, bf16[768,128]{1,0:T(8,128)(2,1)S(1)}, u32[]{:S(2)}, u32[]{:S(2)}) %collective-permute-start.4) | collective-permute-done | bytes 196640 | tf_op jit(solution)/shard_map/ppermute | solution.py:222
  76.8 4.1 %collective-permute-done.3.r1_ref = bf16[768,128]{1,0:T(8,128)(2,1)S(1)} collective-permute-done((bf16[768,128]{1,0:T(8,128)(2,1)S(1)}, bf16[768,128]{1,0:T(8,128)(2,1)S(1)}, u32[]{:S(2)}, u32[]{:S(2)}) %collective-permute-start.3) | collective-permute-done | bytes 196640 | tf_op jit(solution)/shard_map/ppermute | solution.py:222
  80.9 0.0 all-to-all-done.1.got_ref
  80.9 0.0 copy-done.1
  80.9 0.8 sort_cores.1
  81.7 6.8 %collective-permute-start.6 = (bf16[4,1024,128]{2,1,0:T(8,128)(2,1)S(1)}, bf16[4,1024,128]{2,1,0:T(8,128)(2,1)S(1)}, u32[]{:S(2)}, u32[]{:S(2)}) collective-permute-start(bf16[4,1024,128]{2,1,0:T(8,128)(2,1)S(1)} %get-tuple-element.16), channel_id=1, source_target_pairs={{0,4},{4,0},{1,5},{5,1},{2,6},{6,2},{3,7},{7,3},{8,12},{12,8},{9,1... | collective-permute-start | bytes 3145736 | tf_op jit(solution)/shard_map/ppermute | solution.py:235
  88.5 0.0 copy-done.2
  88.5 0.0 copy-done.3
  88.5 5.7 %sigma_blocks.2.refs_5_ = bf16[4,2,2,64,256]{4,3,2,1,0:T(8,128)(2,1)S(1)} custom-call(s32[6]{0:T(128)S(1)} %copy-done.1, s32[128]{0:T(128)S(1)} %copy-done.2, s32[128]{0:T(128)S(1)} %copy-done.3, bf16[4,1024,128]{2,1,0:T(8,128)(2,1)S(1)} %get-tuple-element.18.refs_3_, bf16[4,768,128]{2,1,0:T(8,128)(2,1)S(1)} %get-tuple-element.17.refs_4_), custom_call_target="tpu_custom_call" | custom-call | tf_op jit(solution)/shard_map/sigma_blocks/pallas_call | solution.py:240
  94.2 0.0 collective-permute-done.6.refs_3_
  94.2 5.7 %sigma_blocks.3 = bf16[4,2,2,64,256]{4,3,2,1,0:T(8,128)(2,1)S(1)} custom-call(s32[6]{0:T(128)S(1)} %copy-done.1, s32[128]{0:T(128)S(1)} %copy-done.2, s32[128]{0:T(128)S(1)} %copy-done.3, bf16[4,1024,128]{2,1,0:T(8,128)(2,1)S(1)} %collective-permute-done.6.refs_3_, ...), custom_call_target="tpu_custom_call", output_to_operand_aliasing={{}: (5, {})} | custom-call | tf_op jit(solution)/shard_map/sigma_blocks/pallas_call | solution.py:240
  99.9 10.4 %all_to_all.15.in_ref = bf16[4,2,2,64,256]{4,3,2,1,0:T(8,128)(2,1)S(1)} all-to-all(bf16[4,2,2,64,256]{4,3,2,1,0:T(8,128)(2,1)S(1)} %sigma_blocks.3), channel_id=1, replica_groups=mesh['yh'=4,'yl'=2,'zh'=4,'zl'=2,'core'=2,'op'=4] {'yl','zl'}, dimensions={0} | all-to-all | bytes 1048576 | tf_op jit(solution)/shard_map/all_to_all | solution.py:259
  110.3 1.6 %merge_sectors.1 = bf16[2,64,2048]{2,1,0:T(8,128)(2,1)} custom-call(s32[6]{0:T(128)S(1)} %copy-done.1, bf16[4,2,2,64,256]{4,3,2,1,0:T(8,128)(2,1)S(1)} %all_to_all.15.in_ref), custom_call_target="tpu_custom_call" | custom-call | tf_op jit(solution)/shard_map/merge_sectors/pallas_call | solution.py:260
Async XLA Ops:
  3.8 16.4 %copy-start = (bf16[192,128]{1,0:T(8,128)(2,1)S(1)}, bf16[192,128]{1,0:T(8,128)(2,1)}, u32[]{:S(2)}) copy-start(bf16[192,128]{1,0:T(8,128)(2,1)} %get-tuple-element.13.r0_ref) | copy-start | bytes 147460
  3.8 57.7 %all-to-all-start = ((bf16[16,320,128]{2,1,0:T(8,128)(2,1)}), bf16[16,320,128]{2,1,0:T(8,128)(2,1)S(1)}, u32[]{:S(2)}, u32[]{:S(2)}) async-start(bf16[16,320,128]{2,1,0:T(8,128)(2,1)} %get-tuple-element.12), calls=%async_computation | async-start | bytes 2621440 | tf_op jit(solution)/shard_map/all_to_all | solution.py:204
  20.2 9.0 %collective-permute-start.2 = (bf16[192,128]{1,0:T(8,128)(2,1)S(1)}, bf16[192,128]{1,0:T(8,128)(2,1)S(1)}, u32[]{:S(2)}, u32[]{:S(2)}) collective-permute-start(bf16[192,128]{1,0:T(8,128)(2,1)S(1)} %copy-done), channel_id=1, source_target_pairs={{0,3},{1,2},{2,1},{3,0},{4,7},{5,6},{6,5},{7,4},{8,11},{9,10},{10,... | collective-permute-start | bytes 147464 | tf_op jit(solution)/shard_map/ppermute | solution.py:207
  24.6 6.6 %collective-permute-start.1 = (bf16[192,128]{1,0:T(8,128)(2,1)S(1)}, bf16[192,128]{1,0:T(8,128)(2,1)S(1)}, u32[]{:S(2)}, u32[]{:S(2)}) collective-permute-start(bf16[192,128]{1,0:T(8,128)(2,1)S(1)} %copy-done), channel_id=1, source_target_pairs={{0,2},{1,3},{2,0},{3,1},{4,6},{5,7},{6,4},{7,5},{8,10},{9,11},{10,... | collective-permute-start | bytes 147464 | tf_op jit(solution)/shard_map/ppermute | solution.py:207
  27.0 5.1 %collective-permute-start = (bf16[192,128]{1,0:T(8,128)(2,1)S(1)}, bf16[192,128]{1,0:T(8,128)(2,1)S(1)}, u32[]{:S(2)}, u32[]{:S(2)}) collective-permute-start(bf16[192,128]{1,0:T(8,128)(2,1)S(1)} %copy-done), channel_id=1, source_target_pairs={{0,1},{1,0},{2,3},{3,2},{4,5},{5,4},{6,7},{7,6},{8,9},{9,8},{10,11... | collective-permute-start | bytes 147464 | tf_op jit(solution)/shard_map/ppermute | solution.py:207
  62.8 18.1 %copy-start.1 = (s32[6]{0:T(128)S(1)}, s32[6]{0:T(128)}, u32[]{:S(2)}) copy-start(s32[6]{0:T(128)} %stack.27.at_ref.refs_0_) | copy-start | bytes 76
  62.8 18.1 %all-to-all-start.1 = ((bf16[4,1280,128]{2,1,0:T(8,128)(2,1)}), bf16[4,1280,128]{2,1,0:T(8,128)(2,1)S(1)}, u32[]{:S(2)}, u32[]{:S(2)}) async-start(bf16[4,1280,128]{2,1,0:T(8,128)(2,1)} %get-tuple-element.14), calls=%async_computation.1 | async-start | bytes 2621440 | tf_op jit(solution)/shard_map/all_to_all | solution.py:219
  66.9 21.6 %copy-start.2 = (s32[128]{0:T(128)S(1)}, s32[128]{0:T(128)}, u32[]{:S(2)}) copy-start(s32[128]{0:T(128)} %refs_1_.3) | copy-start | bytes 1540
  66.9 21.6 %copy-start.3 = (s32[128]{0:T(128)S(1)}, s32[128]{0:T(128)}, u32[]{:S(2)}) copy-start(s32[128]{0:T(128)} %refs_2_.3) | copy-start | bytes 1540
  66.9 8.5 %collective-permute-start.5 = (bf16[768,128]{1,0:T(8,128)(2,1)S(1)}, bf16[768,128]{1,0:T(8,128)(2,1)S(1)}, u32[]{:S(2)}, u32[]{:S(2)}) collective-permute-start(bf16[768,128]{1,0:T(8,128)(2,1)S(1)} %get-tuple-element.15.r0_ref), channel_id=1, source_target_pairs={{0,72},{8,64},{64,8},{72,0},{1,73},{9,65},{65,9},{73,1},{2,74},{10... | collective-permute-start | bytes 589832 | tf_op jit(solution)/shard_map/ppermute | solution.py:222
  69.0 7.8 %collective-permute-start.4 = (bf16[768,128]{1,0:T(8,128)(2,1)S(1)}, bf16[768,128]{1,0:T(8,128)(2,1)S(1)}, u32[]{:S(2)}, u32[]{:S(2)}) collective-permute-start(bf16[768,128]{1,0:T(8,128)(2,1)S(1)} %get-tuple-element.15.r0_ref), channel_id=1, source_target_pairs={{0,64},{8,72},{64,0},{72,8},{1,65},{9,73},{65,1},{73,9},{2,66},{10... | collective-permute-start | bytes 589832 | tf_op jit(solution)/shard_map/ppermute | solution.py:222
  70.9 10.0 %collective-permute-start.3 = (bf16[768,128]{1,0:T(8,128)(2,1)S(1)}, bf16[768,128]{1,0:T(8,128)(2,1)S(1)}, u32[]{:S(2)}, u32[]{:S(2)}) collective-permute-start(bf16[768,128]{1,0:T(8,128)(2,1)S(1)} %get-tuple-element.15.r0_ref), channel_id=1, source_target_pairs={{0,8},{8,0},{64,72},{72,64},{1,9},{9,1},{65,73},{73,65},{2,10},{10... | collective-permute-start | bytes 589832 | tf_op jit(solution)/shard_map/ppermute | solution.py:222
  81.7 12.5 %collective-permute-start.6 = (bf16[4,1024,128]{2,1,0:T(8,128)(2,1)S(1)}, bf16[4,1024,128]{2,1,0:T(8,128)(2,1)S(1)}, u32[]{:S(2)}, u32[]{:S(2)}) collective-permute-start(bf16[4,1024,128]{2,1,0:T(8,128)(2,1)S(1)} %get-tuple-element.16), channel_id=1, source_target_pairs={{0,4},{4,0},{1,5},{5,1},{2,6},{6,2},{3,7},{7,3},{8,12},{12,8},{9,1... | collective-permute-start | bytes 3145736 | tf_op jit(solution)/shard_map/ppermute | solution.py:235

commit v5 on v4

v5 whole, which is shorter than its diff:
```python
import jax
import jax.numpy as jnp
from jax import lax
from jax.experimental import pallas as pl
from jax.experimental.pallas import tpu as pltpu
from jax.sharding import Mesh, PartitionSpec as P

target_charge = 6
XDIM, YH, YL, ZH, ZL, CORE = 4, 4, 2, 4, 2, 2
SEC = ("yh", "yl", "zh", "zl", "core")
FAR = ("yh", "zh")
NEAR = ("yl", "zl")
NT = (((1,), (1,)), ((), ()))
BLOCK = 64
WIDE = 2 * BLOCK
HALF = BLOCK // 2
GROUP = 4 * BLOCK
TERMS = 24
HERE = TERMS // XDIM
PAIRS = HERE // 2
XROWS = 2 * HALF
RROWS = PAIRS * BLOCK
FROM = ZH * CORE
VMEM = 24 * 1024 * 1024
SMALL = 8 * 1024 * 1024


def swap_halves(piece):
    return jnp.concatenate([piece[:, BLOCK:], piece[:, :BLOCK]], axis=1)


def placed(piece, second, to_second):
    lane = lax.broadcasted_iota(jnp.int32, piece.shape, 1)
    moved = piece if second == to_second else swap_halves(piece)
    keep = (lane >= BLOCK) if to_second else (lane < BLOCK)
    return jnp.where(keep, moved, jnp.zeros_like(moved))


def place():
    return [lax.axis_index(n).astype(jnp.int32) for n in ("op",) + SEC]


def prepare_kernel(
    lc_ref, rc_ref, left_in, right_in, x_ref, out_ref, rout_ref,
    sent_ref, left_ref, right_ref, rows_ref, sems,
):
    operators = [
        pltpu.make_async_copy(source, ref, sems.at[YH + n])
        for n, (source, ref) in enumerate(((left_in, left_ref), (right_in, right_ref)))
    ]
    for copy in operators:
        copy.start()
    plane = lax.axis_index("op").astype(jnp.int32)
    lanes_of = rows_ref.shape[2]
    copies = []
    for yh in range(YH):
        source = x_ref.at[
            plane // 2,
            pl.ds(pl.multiple_of(lax.rem(plane, 2) * HALF, HALF), HALF),
            pl.ds(yh * lanes_of, lanes_of),
        ]
        copies.append(pltpu.make_async_copy(source, rows_ref.at[yh], sems.at[yh]))
        copies[-1].start()
    for copy in operators:
        copy.wait()
    wide = CORE * XROWS
    for p in range(PAIRS):
        pairs = []
        for c_ref, in_ref in ((lc_ref, left_ref), (rc_ref, right_ref)):
            both = []
            for t in (2 * p, 2 * p + 1):
                scale = c_ref[0, t].astype(jnp.float32)
                both.append((in_ref[t].astype(jnp.float32) * scale).astype(jnp.bfloat16))
            pairs.append(jnp.concatenate(both, axis=1))
        rout_ref[p * BLOCK:(p + 1) * BLOCK, :] = pairs[1]
        for to in range(YH * ZH):
            sent_ref[to, wide + p * BLOCK:wide + (p + 1) * BLOCK, :] = pairs[0]
    for yh in range(YH):
        copies[yh].wait()
        for yl in range(YL):
            for zh in range(ZH):
                at = (yl * ZH + zh) * ZL
                first = rows_ref[yh, :, at * WIDE:(at + 1) * WIDE]
                second = rows_ref[yh, :, (at + 1) * WIDE:(at + 2) * WIDE]
                for c in range(CORE):
                    lanes = slice(c * BLOCK, (c + 1) * BLOCK)
                    rows = slice(c * XROWS + yl * HALF, c * XROWS + (yl + 1) * HALF)
                    sent_ref[yh * ZH + zh, rows, :] = jnp.concatenate(
                        [first[:, lanes], second[:, lanes]], axis=1
                    )
        done = pl.ds(yh * ZH, ZH)
        copies.append(
            pltpu.make_async_copy(sent_ref.at[done], out_ref.at[done], sems.at[YH + 2 + yh])
        )
        copies[-1].start()
    for copy in copies[YH:]:
        copy.wait()


def stack_kernel(got_ref, r0_ref, r1_ref, r2_ref, r3_ref, same_ref, right_ref):
    for d, ref in enumerate((r0_ref, r1_ref, r2_ref, r3_ref)):
        right_ref[d * RROWS:(d + 1) * RROWS, :] = ref[...]


def core_kernel(got_ref, r0_ref, r1_ref, r2_ref, r3_ref, own_ref, give_ref, near_ref):
    _, _, yl_at, _, zl_at, core = place()
    for e, ref in enumerate((r0_ref, r1_ref, r2_ref, r3_ref)):
        near_ref[jnp.bitwise_xor(yl_at * ZL + zl_at, e)] = ref[...]
    step = CORE * XROWS + RROWS
    for x in range(XDIM):
        for z in range(ZH):
            rows = slice(z * XROWS, (z + 1) * XROWS)
            for to_ref, c in ((own_ref, core), (give_ref, 1 - core)):
                at = pl.multiple_of(z * step + c * XROWS, XROWS)
                to_ref[x, rows, :] = got_ref[x, pl.ds(at, XROWS), :]
            left = got_ref[x, z * step + CORE * XROWS:(z + 1) * step, :]
            rows = slice(ZH * XROWS + z * RROWS, ZH * XROWS + (z + 1) * RROWS)
            own_ref[x, rows, :] = left
            give_ref[x, rows, :] = left


def build_right(x_at, near_ref, right_ref):
    zeros = jnp.zeros((BLOCK, WIDE), jnp.bfloat16)
    for b in range(4):
        rows = slice(b * BLOCK, (b + 1) * BLOCK)
        used = slice((b // 2) * WIDE, (b // 2 + 1) * WIDE)
        unused = slice((1 - b // 2) * WIDE, (2 - b // 2) * WIDE)
        for d in range(XDIM):
            first = jnp.bitwise_xor(x_at, d) * HERE
            for p in range(PAIRS):
                at = d * RROWS + p * BLOCK
                piece = near_ref[b, at:at + BLOCK, :]
                for s in range(2):
                    right_ref[first + 2 * p + s, rows, used] = placed(piece, s, b % 2)
                    right_ref[first + 2 * p + s, rows, unused] = zeros


def build_left(got_ref, left_ref):
    zeros = jnp.zeros((BLOCK, WIDE), jnp.bfloat16)
    for x in range(XDIM):
        for z in range(ZH):
            rows = slice(z * BLOCK, (z + 1) * BLOCK)
            for p in range(PAIRS):
                at = ZH * XROWS + z * RROWS + p * BLOCK
                piece = got_ref[x, at:at + BLOCK, :]
                for s in range(2):
                    at = (x * HERE + 2 * p + s) * GROUP
                    used, unused = at + (z // 2) * WIDE, at + (1 - z // 2) * WIDE
                    left_ref[rows, used:used + WIDE] = placed(piece, s, z % 2)
                    left_ref[rows, unused:unused + WIDE] = zeros


def sigma_kernel(c, lcharge_ref, rcharge_ref, got_ref, near_ref, *refs):
    if c == 0:
        out_ref, right_ref, left_ref, half_ref = refs
    else:
        right_ref, _, out_ref, left_ref, half_ref = refs
    x_at, yh_at, yl_at, zh_at, zl_at, core = place()
    if c == 0:
        build_right(x_at, near_ref, right_ref)
    vectors = half_ref.shape[0] // GROUP
    for v in range(vectors):
        rows = []
        for z in range(ZH):
            for h in range(2):
                piece = got_ref[v * 2 + h, z * XROWS:(z + 1) * XROWS, :]
                rows.append(jnp.concatenate([piece[:HALF], piece[HALF:]], axis=1))
        state = jnp.concatenate(rows, axis=0)
        for t in range(TERMS):
            out = lax.dot_general(right_ref[t], state, NT, preferred_element_type=jnp.float32)
            half_ref[v * GROUP:(v + 1) * GROUP, t * GROUP:(t + 1) * GROUP] = out.astype(
                half_ref.dtype
            )
    build_left(got_ref, left_ref)
    out = lax.dot_general(half_ref[...], left_ref[...], NT, preferred_element_type=jnp.float32)

    lane = lax.broadcasted_iota(jnp.int32, (1, GROUP), 1) // BLOCK
    charge = jnp.zeros((1, GROUP), jnp.int32)
    for z in range(ZH):
        sector = (((x_at * YL + yl_at) * ZH + z) * ZL + zl_at) * CORE + jnp.bitwise_xor(core, c)
        charge = jnp.where(lane == z, lcharge_ref[sector], charge)
    for b in range(4):
        sector = (((yh_at * YL + b // 2) * ZH + zh_at) * ZL + b % 2) * CORE + core
        allowed = jnp.abs(charge + rcharge_ref[sector] - target_charge) <= 1
        for v in range(vectors):
            at = v * GROUP + b * BLOCK
            block = out[at:at + BLOCK]
            out_ref[b, 0, v] = jnp.where(allowed, block, jnp.zeros_like(block)).astype(
                out_ref.dtype
            )


def merge_kernel(in_ref, out_ref):
    core = lax.axis_index("core").astype(jnp.int32)
    for yl in range(YL):
        for zl in range(ZL):
            for m in range(ZH // 2):
                low = in_ref[yl * ZL + zl, core, 0, :, m * WIDE:(m + 1) * WIDE]
                high = in_ref[yl * ZL + zl, 1 - core, 0, :, m * WIDE:(m + 1) * WIDE]
                for h in range(2):
                    lanes = slice(h * BLOCK, (h + 1) * BLOCK)
                    at = ((yl * ZH + 2 * m + h) * ZL + zl) * WIDE
                    out_ref[0, :, at:at + WIDE] = jnp.concatenate(
                        [low[:, lanes], high[:, lanes]], axis=1
                    )


def body(
    trial_state,
    left_operators,
    right_operators,
    left_coupling,
    right_coupling,
    left_charge,
    right_charge,
):
    vectors, _, states = trial_state.shape
    smem = pl.BlockSpec(memory_space=pltpu.SMEM)
    vmem = pl.BlockSpec(memory_space=pltpu.VMEM)
    anywhere = pl.BlockSpec(memory_space=pl.ANY)
    params = pltpu.CompilerParams(vmem_limit_bytes=VMEM)
    small = pltpu.CompilerParams(vmem_limit_bytes=SMALL)

    wide = CORE * XROWS
    message = jax.ShapeDtypeStruct((YH * ZH, wide + RROWS, WIDE), jnp.bfloat16)
    operator = jax.ShapeDtypeStruct((RROWS, WIDE), jnp.bfloat16)

    sent, right = pl.pallas_call(
        prepare_kernel,
        in_specs=[smem, smem] + [pl.BlockSpec(memory_space=pltpu.HBM)] * 3,
        out_specs=[anywhere, vmem],
        out_shape=[message, operator],
        scratch_shapes=[
            pltpu.VMEM(message.shape, jnp.bfloat16),
            pltpu.VMEM(left_operators.shape, jnp.bfloat16),
            pltpu.VMEM(right_operators.shape, jnp.bfloat16),
            pltpu.VMEM((YH, HALF, states // YH), jnp.bfloat16),
            pltpu.SemaphoreType.DMA((2 * YH + 2,)),
        ],
        name="prepare_parts",
    )(
        left_coupling.reshape(1, HERE),
        right_coupling.reshape(1, HERE),
        left_operators,
        right_operators,
        trial_state,
    )
    got = lax.all_to_all(sent, FAR, 0, 0, tiled=True)

    rights = [right] + [
        lax.ppermute(right, "op", [(n, n ^ d) for n in range(XDIM)]) for d in (1, 2, 3)
    ]

    got, right = pl.pallas_call(
        stack_kernel,
        in_specs=[anywhere] + [vmem] * 4,
        out_specs=[anywhere, vmem],
        out_shape=[message, jax.ShapeDtypeStruct((XDIM * RROWS, WIDE), jnp.bfloat16)],
        input_output_aliases={0: 0},
        compiler_params=small,
        name="stack_right",
    )(got, *rights)

    got = got.reshape(XDIM, ZH * message.shape[1], WIDE)
    got = lax.all_to_all(got, "op", 0, 0, tiled=True)

    rights = [right] + [
        lax.ppermute(right, NEAR, [(n, n ^ d) for n in range(YL * ZL)]) for d in (1, 2, 3)
    ]

    mine = jax.ShapeDtypeStruct((XDIM, ZH * (XROWS + RROWS), WIDE), jnp.bfloat16)
    near = jax.ShapeDtypeStruct((YL * ZL,) + right.shape, jnp.bfloat16)
    own, give, right = pl.pallas_call(
        core_kernel,
        in_specs=[vmem] * 5,
        out_specs=[vmem] * 3,
        out_shape=[mine, mine, near],
        compiler_params=small,
        name="sort_cores",
    )(got, *rights)
    other = lax.ppermute(give, "core", [(0, 1), (1, 0)])

    shared = [
        jax.ShapeDtypeStruct((TERMS, GROUP, GROUP), jnp.bfloat16),
        jax.ShapeDtypeStruct((4, CORE, vectors, BLOCK, GROUP), jnp.bfloat16),
    ]
    blocks = [
        pl.BlockSpec((4, 1, vectors, BLOCK, GROUP), lambda i, c=c: (0, c, 0, 0, 0))
        for c in range(CORE)
    ]
    keep = pl.BlockSpec(shared[0].shape, lambda v: (0, 0, 0))
    scratch = [
        pltpu.VMEM((GROUP, TERMS * GROUP), jnp.bfloat16),
        pltpu.VMEM((vectors * GROUP, TERMS * GROUP), jnp.bfloat16),
    ]
    inputs = [smem, smem] + [
        pl.BlockSpec(shape.shape, lambda v: (0, 0, 0)) for shape in (mine, near)
    ]
    partial, diagonal = pl.pallas_call(
        lambda *refs: sigma_kernel(0, *refs),
        grid=(1,),
        in_specs=inputs,
        out_specs=[blocks[0], keep],
        out_shape=shared[::-1],
        scratch_shapes=scratch,
        compiler_params=params,
        name="sigma_own",
    )(left_charge, right_charge, own, right)
    partial = pl.pallas_call(
        lambda lc, rc, got, *refs: sigma_kernel(1, lc, rc, got, None, *refs),
        grid=(1,),
        in_specs=inputs[:3] + [keep, anywhere],
        out_specs=blocks[1],
        out_shape=shared[1],
        scratch_shapes=scratch,
        input_output_aliases={4: 0},
        compiler_params=params,
        name="sigma_other",
    )(left_charge, right_charge, other, diagonal, partial)

    partial = lax.all_to_all(partial, NEAR, 0, 0, tiled=True)
    return pl.pallas_call(
        merge_kernel,
        grid=(vectors,),
        in_specs=[pl.BlockSpec((4, CORE, 1, BLOCK, GROUP), lambda v: (0, 0, v, 0, 0))],
        out_specs=pl.BlockSpec((1, BLOCK, 8 * GROUP), lambda v: (v, 0, 0)),
        out_shape=jax.ShapeDtypeStruct((vectors, BLOCK, 8 * GROUP), jnp.bfloat16),
        compiler_params=small,
        name="merge_sectors",
    )(partial)


def solution(mesh):
    fine = Mesh(mesh.devices.reshape(YH, YL, ZH, ZL, CORE, XDIM), SEC + ("op",))
    return jax.shard_map(
        body,
        mesh=fine,
        in_specs=(
            P(None, SEC, None),
            P("op", SEC, None),
            P("op", SEC, None),
            P("op", SEC),
            P("op", SEC),
            P(),
            P(),
        ),
        out_specs=P(None, SEC, "op"),
        check_vma=False,
    )
```

time: 112 us -> 108 us (0.964)
  Pallas kernels: 18.1 us -> 14.1 us
    pallas_call x6, Pallas kernels: 18.1 us -> 14.1 us  [the longest x1 4.72 us: body(): pl.pallas_call(lambda *refs: sigma_kernel(0, *refs), grid=(1,), in_specs=...]
  transfers between devices with their start and end apart: 9 -> 9, of which waited for: 5 -> 5; matrix products, arithmetic and copies ran while one was open for 0% -> 0% of each run, Pallas kernels for 5% -> 4%
where the time goes in v5:
time: 108 us; the launch traced here: 107 us
  starting transfers between devices  44.7 us (41%)
  waiting for transfers between devices  37.9 us (35%)
  Pallas kernels  14.1 us (13%)
  blocking collectives  10.4 us (10%)
    all_to_all x1, waiting for transfers between devices, body(): got = lax.all_to_all(sent, FAR, 0, 0, tiled=True)  29.4 us
    all_to_all x1, starting transfers between devices, body(): got = lax.all_to_all(sent, FAR, 0, 0, tiled=True)  16.4 us
    all_to_all x1, blocking collectives, body(): partial = lax.all_to_all(partial, NEAR, 0, 0, tiled=True)  10.4 us
    ppermute x3, starting transfers between devices, body(): lax.ppermute(right, 'op', [(n, n ^ d) for n in range(XDIM)])  8.98 us
    ppermute x3, starting transfers between devices, body(): lax.ppermute(right, NEAR, [(n, n ^ d) for n in range(YL * ZL)])  8.49 us
    ppermute x1, starting transfers between devices, body(): other = lax.ppermute(give, 'core', [(0, 1), (1, 0)])  6.77 us
    ppermute x3, waiting for transfers between devices, body(): lax.ppermute(right, NEAR, [(n, n ^ d) for n in range(YL * ZL)])  5.44 us
    pallas_call x1, Pallas kernels, body(): pl.pallas_call(lambda *refs: sigma_kernel(0, *refs), grid=(1,), in_specs=...  4.72 us
  transfers between devices with their start and end apart: 9, of which 5 were waited for; matrix products, arithmetic and copies ran while one was open for 0% of the time, Pallas kernels for 4%

profile of v5, /device:TPU:1, one launch (start us, length us, event | category | flops | bytes accessed | tf_op | source)
XLA Modules:
  0.0 107.3 jit_solution(11279994888992935227)
XLA Ops:
  0.0 3.7 %prepare_parts.1 = (bf16[16,320,128]{2,1,0:T(8,128)(2,1)}, bf16[192,128]{1,0:T(8,128)(2,1)}) custom-call(s32[1,6]{1,0:T(1,128)} %bitcast.3, s32[1,6]{1,0:T(1,128)} %bitcast.4, bf16[6,64,64]{2,1,0:T(8,128)(2,1)} %left_in.1, bf16[6,64,64]{2,1,0:T(8,128)(2,1)} %right_in.1, bf16[2,64,8192]{2,1,0:T(8,128)(2,1)} %x_ref.1), custom_call_target="tpu_custom_call" | custom-call | tf_op jit(solution)/shard_map/prepare_parts/pallas_call | solution.py:228
  3.7 0.0 copy-start
  3.7 16.4 %all-to-all-start = ((bf16[16,320,128]{2,1,0:T(8,128)(2,1)}), bf16[16,320,128]{2,1,0:T(8,128)(2,1)}, u32[]{:S(2)}, u32[]{:S(2)}) async-start(bf16[16,320,128]{2,1,0:T(8,128)(2,1)} %get-tuple-element.14), calls=%async_computation | async-start | bytes 2621440 | tf_op jit(solution)/shard_map/all_to_all | solution.py:248
  20.1 0.0 copy-done
  20.1 4.4 %collective-permute-start.2 = (bf16[192,128]{1,0:T(8,128)(2,1)S(1)}, bf16[192,128]{1,0:T(8,128)(2,1)S(1)}, u32[]{:S(2)}, u32[]{:S(2)}) collective-permute-start(bf16[192,128]{1,0:T(8,128)(2,1)S(1)} %copy-done), channel_id=1, source_target_pairs={{0,3},{1,2},{2,1},{3,0},{4,7},{5,6},{6,5},{7,4},{8,11},{9,10},{10,... | collective-permute-start | bytes 147464 | tf_op jit(solution)/shard_map/ppermute | solution.py:251
  24.5 2.4 %collective-permute-start.1 = (bf16[192,128]{1,0:T(8,128)(2,1)S(1)}, bf16[192,128]{1,0:T(8,128)(2,1)S(1)}, u32[]{:S(2)}, u32[]{:S(2)}) collective-permute-start(bf16[192,128]{1,0:T(8,128)(2,1)S(1)} %copy-done), channel_id=1, source_target_pairs={{0,2},{1,3},{2,0},{3,1},{4,6},{5,7},{6,4},{7,5},{8,10},{9,11},{10,... | collective-permute-start | bytes 147464 | tf_op jit(solution)/shard_map/ppermute | solution.py:251
  27.0 2.2 %collective-permute-start = (bf16[192,128]{1,0:T(8,128)(2,1)S(1)}, bf16[192,128]{1,0:T(8,128)(2,1)S(1)}, u32[]{:S(2)}, u32[]{:S(2)}) collective-permute-start(bf16[192,128]{1,0:T(8,128)(2,1)S(1)} %copy-done), channel_id=1, source_target_pairs={{0,1},{1,0},{2,3},{3,2},{4,5},{5,4},{6,7},{7,6},{8,9},{9,8},{10,11... | collective-permute-start | bytes 147464 | tf_op jit(solution)/shard_map/ppermute | solution.py:251
  29.1 0.0 collective-permute-done.2.r3_ref
  29.1 2.1 %collective-permute-done.1.r2_ref = bf16[192,128]{1,0:T(8,128)(2,1)S(1)} collective-permute-done((bf16[192,128]{1,0:T(8,128)(2,1)S(1)}, bf16[192,128]{1,0:T(8,128)(2,1)S(1)}, u32[]{:S(2)}, u32[]{:S(2)}) %collective-permute-start.1) | collective-permute-done | bytes 49184 | tf_op jit(solution)/shard_map/ppermute | solution.py:251
  31.3 0.9 collective-permute-done.r1_ref
  32.2 29.4 %all-to-all-done.got_ref = bf16[16,320,128]{2,1,0:T(8,128)(2,1)} async-done(((bf16[16,320,128]{2,1,0:T(8,128)(2,1)}), bf16[16,320,128]{2,1,0:T(8,128)(2,1)}, u32[]{:S(2)}, u32[]{:S(2)}) %all-to-all-start) | async-done | bytes 1310752 | tf_op jit(solution)/shard_map/all_to_all | solution.py:248
  61.6 4.0 %all-to-all-start.1 = ((bf16[4,1280,128]{2,1,0:T(8,128)(2,1)}), bf16[4,1280,128]{2,1,0:T(8,128)(2,1)S(1)}, u32[]{:S(2)}, u32[]{:S(2)}) async-start(bf16[4,1280,128]{2,1,0:T(8,128)(2,1)} %bitcast.2), calls=%async_computation.1 | async-start | bytes 2621440 | tf_op jit(solution)/shard_map/all_to_all | solution.py:265
  65.7 0.0 copy-start.1
  65.7 0.0 copy-start.2
  65.7 2.0 %collective-permute-start.5 = (bf16[768,128]{1,0:T(8,128)(2,1)S(1)}, bf16[768,128]{1,0:T(8,128)(2,1)S(1)}, u32[]{:S(2)}, u32[]{:S(2)}) collective-permute-start(bf16[768,128]{1,0:T(8,128)(2,1)S(1)} %get-tuple-element.17.r0_ref), channel_id=1, source_target_pairs={{0,72},{8,64},{64,8},{72,0},{1,73},{9,65},{65,9},{73,1},{2,74},{10... | collective-permute-start | bytes 589832 | tf_op jit(solution)/shard_map/ppermute | solution.py:268
  67.7 1.9 %collective-permute-start.4 = (bf16[768,128]{1,0:T(8,128)(2,1)S(1)}, bf16[768,128]{1,0:T(8,128)(2,1)S(1)}, u32[]{:S(2)}, u32[]{:S(2)}) collective-permute-start(bf16[768,128]{1,0:T(8,128)(2,1)S(1)} %get-tuple-element.17.r0_ref), channel_id=1, source_target_pairs={{0,64},{8,72},{64,0},{72,8},{1,65},{9,73},{65,1},{73,9},{2,66},{10... | collective-permute-start | bytes 589832 | tf_op jit(solution)/shard_map/ppermute | solution.py:268
  69.6 4.5 %collective-permute-start.3 = (bf16[768,128]{1,0:T(8,128)(2,1)S(1)}, bf16[768,128]{1,0:T(8,128)(2,1)S(1)}, u32[]{:S(2)}, u32[]{:S(2)}) collective-permute-start(bf16[768,128]{1,0:T(8,128)(2,1)S(1)} %get-tuple-element.17.r0_ref), channel_id=1, source_target_pairs={{0,8},{8,0},{64,72},{72,64},{1,9},{9,1},{65,73},{73,65},{2,10},{10... | collective-permute-start | bytes 589832 | tf_op jit(solution)/shard_map/ppermute | solution.py:268
  74.2 0.0 collective-permute-done.5.r3_ref
  74.2 1.3 %collective-permute-done.4.r2_ref = bf16[768,128]{1,0:T(8,128)(2,1)S(1)} collective-permute-done((bf16[768,128]{1,0:T(8,128)(2,1)S(1)}, bf16[768,128]{1,0:T(8,128)(2,1)S(1)}, u32[]{:S(2)}, u32[]{:S(2)}) %collective-permute-start.4) | collective-permute-done | bytes 196640 | tf_op jit(solution)/shard_map/ppermute | solution.py:268
  75.5 4.1 %collective-permute-done.3.r1_ref = bf16[768,128]{1,0:T(8,128)(2,1)S(1)} collective-permute-done((bf16[768,128]{1,0:T(8,128)(2,1)S(1)}, bf16[768,128]{1,0:T(8,128)(2,1)S(1)}, u32[]{:S(2)}, u32[]{:S(2)}) %collective-permute-start.3) | collective-permute-done | bytes 196640 | tf_op jit(solution)/shard_map/ppermute | solution.py:268
  79.6 0.0 all-to-all-done.1.got_ref
  79.7 0.3 sort_cores.1
  80.0 6.8 %collective-permute-start.6 = (bf16[4,1024,128]{2,1,0:T(8,128)(2,1)S(1)}, bf16[4,1024,128]{2,1,0:T(8,128)(2,1)S(1)}, u32[]{:S(2)}, u32[]{:S(2)}) collective-permute-start(bf16[4,1024,128]{2,1,0:T(8,128)(2,1)S(1)} %get-tuple-element.18), channel_id=1, source_target_pairs={{0,4},{4,0},{1,5},{5,1},{2,6},{6,2},{3,7},{7,3},{8,12},{12,8},{9,1... | collective-permute-start | bytes 3145736 | tf_op jit(solution)/shard_map/ppermute | solution.py:281
  86.7 0.0 copy-done.1
  86.7 0.0 copy-done.2
  86.8 4.7 %sigma_own.1 = (bf16[4,2,2,64,256]{4,3,2,1,0:T(8,128)(2,1)S(1)}, bf16[24,256,256]{2,1,0:T(8,128)(2,1)S(1)}) custom-call(s32[128]{0:T(128)S(1)} %copy-done.1, s32[128]{0:T(128)S(1)} %copy-done.2, bf16[4,1024,128]{2,1,0:T(8,128)(2,1)S(1)} %get-tuple-element.19.refs_2_, bf16[4,768,128]{2,1,0:T(8,128)(2,1)S(1)} %get-tuple-element.20.refs_3_), custom_call_target="tpu_custom_call" | custom-call | tf_op jit(solution)/shard_map/sigma_own/pallas_call | solution.py:299
  91.5 0.0 collective-permute-done.6.got
  91.5 4.3 %sigma_other.1 = bf16[4,2,2,64,256]{4,3,2,1,0:T(8,128)(2,1)S(1)} custom-call(s32[128]{0:T(128)S(1)} %copy-done.1, s32[128]{0:T(128)S(1)} %copy-done.2, bf16[4,1024,128]{2,1,0:T(8,128)(2,1)S(1)} %collective-permute-done.6.got, bf16[24,256,256]{2,1,0:T(8,128)(2,1)S(1)} %get-tuple-element.21.refs_0_, ...), custom_call_target="tpu_custom_call", output_to_operand_aliasing={{}: (4, {})} | custom-call | tf_op jit(solution)/shard_map/sigma_other/pallas_call | solution.py:309
  95.8 10.4 %all_to_all.15.in_ref = bf16[4,2,2,64,256]{4,3,2,1,0:T(8,128)(2,1)S(1)} all-to-all(bf16[4,2,2,64,256]{4,3,2,1,0:T(8,128)(2,1)S(1)} %sigma_other.1), channel_id=1, replica_groups=mesh['yh'=4,'yl'=2,'zh'=4,'zl'=2,'core'=2,'op'=4] {'yl','zl'}, dimensions={0} | all-to-all | bytes 1048576 | tf_op jit(solution)/shard_map/all_to_all | solution.py:321
  106.2 1.1 merge_sectors.1
  (1 shorter events, 0.0 us)
Async XLA Ops:
  3.7 16.4 %copy-start = (bf16[192,128]{1,0:T(8,128)(2,1)S(1)}, bf16[192,128]{1,0:T(8,128)(2,1)}, u32[]{:S(2)}) copy-start(bf16[192,128]{1,0:T(8,128)(2,1)} %get-tuple-element.15.r0_ref) | copy-start | bytes 147460
  3.7 57.9 %all-to-all-start = ((bf16[16,320,128]{2,1,0:T(8,128)(2,1)}), bf16[16,320,128]{2,1,0:T(8,128)(2,1)}, u32[]{:S(2)}, u32[]{:S(2)}) async-start(bf16[16,320,128]{2,1,0:T(8,128)(2,1)} %get-tuple-element.14), calls=%async_computation | async-start | bytes 2621440 | tf_op jit(solution)/shard_map/all_to_all | solution.py:248
  20.1 9.0 %collective-permute-start.2 = (bf16[192,128]{1,0:T(8,128)(2,1)S(1)}, bf16[192,128]{1,0:T(8,128)(2,1)S(1)}, u32[]{:S(2)}, u32[]{:S(2)}) collective-permute-start(bf16[192,128]{1,0:T(8,128)(2,1)S(1)} %copy-done), channel_id=1, source_target_pairs={{0,3},{1,2},{2,1},{3,0},{4,7},{5,6},{6,5},{7,4},{8,11},{9,10},{10,... | collective-permute-start | bytes 147464 | tf_op jit(solution)/shard_map/ppermute | solution.py:251
  24.5 6.7 %collective-permute-start.1 = (bf16[192,128]{1,0:T(8,128)(2,1)S(1)}, bf16[192,128]{1,0:T(8,128)(2,1)S(1)}, u32[]{:S(2)}, u32[]{:S(2)}) collective-permute-start(bf16[192,128]{1,0:T(8,128)(2,1)S(1)} %copy-done), channel_id=1, source_target_pairs={{0,2},{1,3},{2,0},{3,1},{4,6},{5,7},{6,4},{7,5},{8,10},{9,11},{10,... | collective-permute-start | bytes 147464 | tf_op jit(solution)/shard_map/ppermute | solution.py:251
  27.0 5.2 %collective-permute-start = (bf16[192,128]{1,0:T(8,128)(2,1)S(1)}, bf16[192,128]{1,0:T(8,128)(2,1)S(1)}, u32[]{:S(2)}, u32[]{:S(2)}) collective-permute-start(bf16[192,128]{1,0:T(8,128)(2,1)S(1)} %copy-done), channel_id=1, source_target_pairs={{0,1},{1,0},{2,3},{3,2},{4,5},{5,4},{6,7},{7,6},{8,9},{9,8},{10,11... | collective-permute-start | bytes 147464 | tf_op jit(solution)/shard_map/ppermute | solution.py:251
  61.6 18.0 %all-to-all-start.1 = ((bf16[4,1280,128]{2,1,0:T(8,128)(2,1)}), bf16[4,1280,128]{2,1,0:T(8,128)(2,1)S(1)}, u32[]{:S(2)}, u32[]{:S(2)}) async-start(bf16[4,1280,128]{2,1,0:T(8,128)(2,1)} %bitcast.2), calls=%async_computation.1 | async-start | bytes 2621440 | tf_op jit(solution)/shard_map/all_to_all | solution.py:265
  65.7 21.1 %copy-start.1 = (s32[128]{0:T(128)S(1)}, s32[128]{0:T(128)}, u32[]{:S(2)}) copy-start(s32[128]{0:T(128)} %lc.1) | copy-start | bytes 1540
  65.7 21.1 %copy-start.2 = (s32[128]{0:T(128)S(1)}, s32[128]{0:T(128)}, u32[]{:S(2)}) copy-start(s32[128]{0:T(128)} %rc.1) | copy-start | bytes 1540
  65.7 8.5 %collective-permute-start.5 = (bf16[768,128]{1,0:T(8,128)(2,1)S(1)}, bf16[768,128]{1,0:T(8,128)(2,1)S(1)}, u32[]{:S(2)}, u32[]{:S(2)}) collective-permute-start(bf16[768,128]{1,0:T(8,128)(2,1)S(1)} %get-tuple-element.17.r0_ref), channel_id=1, source_target_pairs={{0,72},{8,64},{64,8},{72,0},{1,73},{9,65},{65,9},{73,1},{2,74},{10... | collective-permute-start | bytes 589832 | tf_op jit(solution)/shard_map/ppermute | solution.py:268
  67.7 7.8 %collective-permute-start.4 = (bf16[768,128]{1,0:T(8,128)(2,1)S(1)}, bf16[768,128]{1,0:T(8,128)(2,1)S(1)}, u32[]{:S(2)}, u32[]{:S(2)}) collective-permute-start(bf16[768,128]{1,0:T(8,128)(2,1)S(1)} %get-tuple-element.17.r0_ref), channel_id=1, source_target_pairs={{0,64},{8,72},{64,0},{72,8},{1,65},{9,73},{65,1},{73,9},{2,66},{10... | collective-permute-start | bytes 589832 | tf_op jit(solution)/shard_map/ppermute | solution.py:268
  69.6 10.0 %collective-permute-start.3 = (bf16[768,128]{1,0:T(8,128)(2,1)S(1)}, bf16[768,128]{1,0:T(8,128)(2,1)S(1)}, u32[]{:S(2)}, u32[]{:S(2)}) collective-permute-start(bf16[768,128]{1,0:T(8,128)(2,1)S(1)} %get-tuple-element.17.r0_ref), channel_id=1, source_target_pairs={{0,8},{8,0},{64,72},{72,64},{1,9},{9,1},{65,73},{73,65},{2,10},{10... | collective-permute-start | bytes 589832 | tf_op jit(solution)/shard_map/ppermute | solution.py:268
  80.0 11.5 %collective-permute-start.6 = (bf16[4,1024,128]{2,1,0:T(8,128)(2,1)S(1)}, bf16[4,1024,128]{2,1,0:T(8,128)(2,1)S(1)}, u32[]{:S(2)}, u32[]{:S(2)}) collective-permute-start(bf16[4,1024,128]{2,1,0:T(8,128)(2,1)S(1)} %get-tuple-element.18), channel_id=1, source_target_pairs={{0,4},{4,0},{1,5},{5,1},{2,6},{6,2},{3,7},{7,3},{8,12},{12,8},{9,1... | collective-permute-start | bytes 3145736 | tf_op jit(solution)/shard_map/ppermute | solution.py:281

commit v6 on v5

--- a/solution.py
+++ b/solution.py
@@ -41,40 +41,28 @@
 
 
 def prepare_kernel(
-    lc_ref, rc_ref, left_in, right_in, x_ref, out_ref, rout_ref,
-    sent_ref, left_ref, right_ref, rows_ref, sems,
+    lc_in, rc_in, left_in, right_in, x_ref, out_ref, lout_ref, rout_ref,
+    sent_ref, lc_ref, rc_ref, left_ref, right_ref, rows_ref, sems,
 ):
-    operators = [
-        pltpu.make_async_copy(source, ref, sems.at[YH + n])
-        for n, (source, ref) in enumerate(((left_in, left_ref), (right_in, right_ref)))
-    ]
-    for copy in operators:
-        copy.start()
     plane = lax.axis_index("op").astype(jnp.int32)
     lanes_of = rows_ref.shape[2]
     copies = []
+
+    def copy(source, to):
+        copies.append(pltpu.make_async_copy(source, to, sems.at[len(copies)]))
+        copies[-1].start()
+
     for yh in range(YH):
         source = x_ref.at[
             plane // 2,
             pl.ds(pl.multiple_of(lax.rem(plane, 2) * HALF, HALF), HALF),
             pl.ds(yh * lanes_of, lanes_of),
         ]
-        copies.append(pltpu.make_async_copy(source, rows_ref.at[yh], sems.at[yh]))
-        copies[-1].start()
-    for copy in operators:
-        copy.wait()
-    wide = CORE * XROWS
-    for p in range(PAIRS):
-        pairs = []
-        for c_ref, in_ref in ((lc_ref, left_ref), (rc_ref, right_ref)):
-            both = []
-            for t in (2 * p, 2 * p + 1):
-                scale = c_ref[0, t].astype(jnp.float32)
-                both.append((in_ref[t].astype(jnp.float32) * scale).astype(jnp.bfloat16))
-            pairs.append(jnp.concatenate(both, axis=1))
-        rout_ref[p * BLOCK:(p + 1) * BLOCK, :] = pairs[1]
-        for to in range(YH * ZH):
-            sent_ref[to, wide + p * BLOCK:wide + (p + 1) * BLOCK, :] = pairs[0]
+        copy(source, rows_ref.at[yh])
+    copy(left_in, left_ref)
+    copy(right_in, right_ref)
+    copy(lc_in, lc_ref)
+    copy(rc_in, rc_ref)
     for yh in range(YH):
         copies[yh].wait()
         for yl in range(YL):
@@ -88,33 +76,58 @@
                     sent_ref[yh * ZH + zh, rows, :] = jnp.concatenate(
                         [first[:, lanes], second[:, lanes]], axis=1
                     )
-        done = pl.ds(yh * ZH, ZH)
-        copies.append(
-            pltpu.make_async_copy(sent_ref.at[done], out_ref.at[done], sems.at[YH + 2 + yh])
-        )
-        copies[-1].start()
-    for copy in copies[YH:]:
-        copy.wait()
-
-
-def stack_kernel(got_ref, r0_ref, r1_ref, r2_ref, r3_ref, same_ref, right_ref):
+        places = pl.ds(yh * ZH, ZH)
+        copy(sent_ref.at[places], out_ref.at[places])
+    for n, (c_ref, in_ref, to_ref) in enumerate(
+        ((lc_ref, left_ref, lout_ref), (rc_ref, right_ref, rout_ref))
+    ):
+        copies[YH + n].wait()
+        copies[YH + 2 + n].wait()
+        scale = c_ref[...].astype(jnp.float32)
+        for p in range(PAIRS):
+            both = []
+            for t in (2 * p, 2 * p + 1):
+                scaled = in_ref[t].astype(jnp.float32) * scale[:, t:t + 1]
+                both.append(scaled.astype(jnp.bfloat16))
+            to_ref[p * BLOCK:(p + 1) * BLOCK, :] = jnp.concatenate(both, axis=1)
+    for done in copies[YH + 4:]:
+        done.wait()
+
+
+def spread_kernel(
+    got_ref, left_ref, r0_ref, r1_ref, r2_ref, r3_ref,
+    x0_ref, x1_ref, x2_ref, x3_ref, sent_ref, right_ref,
+):
+    plane = lax.axis_index("op").astype(jnp.int32)
+    wide = CORE * XROWS
+    for d, ref in enumerate((x0_ref, x1_ref, x2_ref, x3_ref)):
+        to = jnp.bitwise_xor(plane, d)
+        for z in range(ZH):
+            ref[z * wide:(z + 1) * wide, :] = got_ref[to * ZH + z]
+    for to in range(YH * ZH):
+        sent_ref[to] = left_ref[...]
     for d, ref in enumerate((r0_ref, r1_ref, r2_ref, r3_ref)):
         right_ref[d * RROWS:(d + 1) * RROWS, :] = ref[...]
 
 
-def core_kernel(got_ref, r0_ref, r1_ref, r2_ref, r3_ref, own_ref, give_ref, near_ref):
-    _, _, yl_at, _, zl_at, core = place()
+def core_kernel(
+    left_ref, x0_ref, x1_ref, x2_ref, x3_ref, r0_ref, r1_ref, r2_ref, r3_ref,
+    own_ref, give_ref, near_ref,
+):
+    x_at, _, yl_at, _, zl_at, core = place()
     for e, ref in enumerate((r0_ref, r1_ref, r2_ref, r3_ref)):
         near_ref[jnp.bitwise_xor(yl_at * ZL + zl_at, e)] = ref[...]
-    step = CORE * XROWS + RROWS
-    for x in range(XDIM):
+    for d, ref in enumerate((x0_ref, x1_ref, x2_ref, x3_ref)):
+        x = jnp.bitwise_xor(x_at, d)
         for z in range(ZH):
             rows = slice(z * XROWS, (z + 1) * XROWS)
             for to_ref, c in ((own_ref, core), (give_ref, 1 - core)):
-                at = pl.multiple_of(z * step + c * XROWS, XROWS)
-                to_ref[x, rows, :] = got_ref[x, pl.ds(at, XROWS), :]
-            left = got_ref[x, z * step + CORE * XROWS:(z + 1) * step, :]
+                at = pl.multiple_of((z * CORE + c) * XROWS, XROWS)
+                to_ref[x, rows, :] = ref[pl.ds(at, XROWS), :]
+    for x in range(XDIM):
+        for z in range(ZH):
             rows = slice(ZH * XROWS + z * RROWS, ZH * XROWS + (z + 1) * RROWS)
+            left = left_ref[x * ZH + z]
             own_ref[x, rows, :] = left
             give_ref[x, rows, :] = left
 
@@ -222,20 +235,22 @@
     small = pltpu.CompilerParams(vmem_limit_bytes=SMALL)
 
     wide = CORE * XROWS
-    message = jax.ShapeDtypeStruct((YH * ZH, wide + RROWS, WIDE), jnp.bfloat16)
+    message = jax.ShapeDtypeStruct((YH * ZH, wide, WIDE), jnp.bfloat16)
     operator = jax.ShapeDtypeStruct((RROWS, WIDE), jnp.bfloat16)
 
-    sent, right = pl.pallas_call(
+    sent, left, right = pl.pallas_call(
         prepare_kernel,
-        in_specs=[smem, smem] + [pl.BlockSpec(memory_space=pltpu.HBM)] * 3,
-        out_specs=[anywhere, vmem],
-        out_shape=[message, operator],
+        in_specs=[pl.BlockSpec(memory_space=pltpu.HBM)] * 5,
+        out_specs=[anywhere, vmem, vmem],
+        out_shape=[message, operator, operator],
         scratch_shapes=[
-            pltpu.VMEM(message.shape, jnp.bfloat16),
+            pltpu.VMEM((YH * ZH, wide, WIDE), jnp.bfloat16),
+            pltpu.VMEM((1, HERE), jnp.int32),
+            pltpu.VMEM((1, HERE), jnp.int32),
             pltpu.VMEM(left_operators.shape, jnp.bfloat16),
             pltpu.VMEM(right_operators.shape, jnp.bfloat16),
             pltpu.VMEM((YH, HALF, states // YH), jnp.bfloat16),
-            pltpu.SemaphoreType.DMA((2 * YH + 2,)),
+            pltpu.SemaphoreType.DMA((2 * YH + 4,)),
         ],
         name="prepare_parts",
     )(
@@ -247,22 +262,27 @@
     )
     got = lax.all_to_all(sent, FAR, 0, 0, tiled=True)
 
-    rights = [right] + [
-        lax.ppermute(right, "op", [(n, n ^ d) for n in range(XDIM)]) for d in (1, 2, 3)
-    ]
-
-    got, right = pl.pallas_call(
-        stack_kernel,
-        in_specs=[anywhere] + [vmem] * 4,
-        out_specs=[anywhere, vmem],
-        out_shape=[message, jax.ShapeDtypeStruct((XDIM * RROWS, WIDE), jnp.bfloat16)],
-        input_output_aliases={0: 0},
+    swap = [(q * XDIM + x, x * XDIM + q) for q in range(YH) for x in range(XDIM)]
+    left = lax.ppermute(left, ("yh", "op"), swap)
+
+    across = [[(n, n ^ d) for n in range(XDIM)] for d in range(XDIM)]
+    rights = [right] + [lax.ppermute(right, "op", across[d]) for d in (1, 2, 3)]
+
+    plane = jax.ShapeDtypeStruct((ZH * wide, WIDE), jnp.bfloat16)
+    *parts, left, right = pl.pallas_call(
+        spread_kernel,
+        in_specs=[vmem] * 6,
+        out_specs=[vmem] * 6,
+        out_shape=[plane] * XDIM
+        + [
+            jax.ShapeDtypeStruct((YH * ZH, RROWS, WIDE), jnp.bfloat16),
+            jax.ShapeDtypeStruct((XDIM * RROWS, WIDE), jnp.bfloat16),
+        ],
         compiler_params=small,
-        name="stack_right",
-    )(got, *rights)
-
-    got = got.reshape(XDIM, ZH * message.shape[1], WIDE)
-    got = lax.all_to_all(got, "op", 0, 0, tiled=True)
+        name="spread_parts",
+    )(got, left, *rights)
+    left = lax.all_to_all(left, FAR, 0, 0, tiled=True)
+    parts = parts[:1] + [lax.ppermute(parts[d], "op", across[d]) for d in (1, 2, 3)]
 
     rights = [right] + [
         lax.ppermute(right, NEAR, [(n, n ^ d) for n in range(YL * ZL)]) for d in (1, 2, 3)
@@ -272,12 +292,12 @@
     near = jax.ShapeDtypeStruct((YL * ZL,) + right.shape, jnp.bfloat16)
     own, give, right = pl.pallas_call(
         core_kernel,
-        in_specs=[vmem] * 5,
+        in_specs=[vmem] * 9,
         out_specs=[vmem] * 3,
         out_shape=[mine, mine, near],
         compiler_params=small,
         name="sort_cores",
-    )(got, *rights)
+    )(left, *parts, *rights)
     other = lax.ppermute(give, "core", [(0, 1), (1, 0)])
 
     shared = [

time: 108 us -> 104 us (0.963)
  waiting for transfers between devices: 37.9 us -> 17.9 us
  starting transfers between devices: 44.7 us -> 60 us
    all_to_all x1, waiting for transfers between devices: 29.4 us -> 0.99 us  [body(): got = lax.all_to_all(sent, FAR, 0, 0, tiled=True)]
    ppermute x3 -> x7, starting transfers between devices: 8.98 us -> 25.2 us  [the longest x3 14.2 us: body(): rights = [right] + [lax.ppermute(right, 'op', across[d]) for d in (1, 2, 3)]]
    ppermute x3 -> x7, waiting for transfers between devices: 3.05 us -> 9.79 us  [the longest x3 6.39 us: body(): lax.ppermute(parts[d], 'op', across[d])]
    ppermute x1, starting transfers between devices: 6.77 us -> 2.43 us  [body(): other = lax.ppermute(give, 'core', [(0, 1), (1, 0)])]
    all_to_all x1, starting transfers between devices: 4.02 us -> 7.75 us  [body(): left = lax.all_to_all(left, FAR, 0, 0, tiled=True)]
    ppermute x3, waiting for transfers between devices: 5.44 us -> 7.13 us  [body(): lax.ppermute(right, NEAR, [(n, n ^ d) for n in range(YL * ZL)])]
  transfers between devices with their start and end apart: 9 -> 13, of which waited for: 5 -> 8; matrix products, arithmetic and copies ran while one was open for 0% -> 0% of each run, Pallas kernels for 4% -> 5%
where the time goes in v6:
time: 104 us
  starting transfers between devices  60 us (58%)
  waiting for transfers between devices  17.9 us (17%)
  Pallas kernels  14.2 us (14%)
  blocking collectives  10.4 us (10%)
    all_to_all x1, starting transfers between devices, body(): got = lax.all_to_all(sent, FAR, 0, 0, tiled=True)  16.2 us
    ppermute x3, starting transfers between devices, body(): rights = [right] + [lax.ppermute(right, 'op', across[d]) for d in (1, 2, 3)]  14.2 us
    all_to_all x1, blocking collectives, body(): partial = lax.all_to_all(partial, NEAR, 0, 0, tiled=True)  10.4 us
    ppermute x3, starting transfers between devices, body(): lax.ppermute(parts[d], 'op', across[d])  9.58 us
    ppermute x3, starting transfers between devices, body(): lax.ppermute(right, NEAR, [(n, n ^ d) for n in range(YL * ZL)])  8.37 us
    all_to_all x1, starting transfers between devices, body(): left = lax.all_to_all(left, FAR, 0, 0, tiled=True)  7.75 us
    ppermute x3, waiting for transfers between devices, body(): lax.ppermute(right, NEAR, [(n, n ^ d) for n in range(YL * ZL)])  7.13 us
    ppermute x3, waiting for transfers between devices, body(): lax.ppermute(parts[d], 'op', across[d])  6.39 us
  transfers between devices with their start and end apart: 13, of which 8 were waited for; matrix products, arithmetic and copies ran while one was open for 0% of the time, Pallas kernels for 5%

profile of v6, /device:TPU:1, one launch (start us, length us, event | category | flops | bytes accessed | tf_op | source)
XLA Modules:
  0.0 103.5 jit_solution(9761110147661714370)
XLA Ops:
  0.0 2.7 %prepare_parts.1 = (bf16[16,128,128]{2,1,0:T(8,128)(2,1)}, bf16[192,128]{1,0:T(8,128)(2,1)}, bf16[192,128]{1,0:T(8,128)(2,1)}) custom-call(s32[1,6]{1,0:T(1,128)} %bitcast.2, s32[1,6]{1,0:T(1,128)} %bitcast.3, bf16[6,64,64]{2,1,0:T(8,128)(2,1)} %left_in.1, bf16[6,64,64]{2,1,0:T(8,128)(2,1)} %right_in.1, bf16[2,64,8192]{2,1,0:T(8,128)(2,1)} %x_ref.1), custom_call_target="tpu_custom_call" | custom-call | tf_op jit(solution)/shard_map/prepare_parts/pallas_call | solution.py:241
  2.7 0.0 copy-start.1
  2.7 0.0 copy-start.2
  2.8 16.2 %all-to-all-start = ((bf16[16,128,128]{2,1,0:T(8,128)(2,1)}), bf16[16,128,128]{2,1,0:T(8,128)(2,1)S(1)}, u32[]{:S(2)}, u32[]{:S(2)}) async-start(bf16[16,128,128]{2,1,0:T(8,128)(2,1)} %get-tuple-element.19), calls=%async_computation | async-start | bytes 1048576 | tf_op jit(solution)/shard_map/all_to_all | solution.py:263
  19.0 1.5 %collective-permute-start = (bf16[192,128]{1,0:T(8,128)(2,1)}, bf16[192,128]{1,0:T(8,128)(2,1)S(1)}, u32[]{:S(2)}, u32[]{:S(2)}) collective-permute-start(bf16[192,128]{1,0:T(8,128)(2,1)} %get-tuple-element.20), channel_id=1, source_target_pairs={{0,0},{1,128},{2,256},{3,384},{128,1},{129,129},{130,257},{131,385... | collective-permute-start | bytes 147464 | tf_op jit(solution)/shard_map/ppermute | solution.py:266
  20.5 8.2 %collective-permute-start.3 = (bf16[192,128]{1,0:T(8,128)(2,1)}, bf16[192,128]{1,0:T(8,128)(2,1)S(1)}, u32[]{:S(2)}, u32[]{:S(2)}) collective-permute-start(bf16[192,128]{1,0:T(8,128)(2,1)} %get-tuple-element.21.r0_ref), channel_id=1, source_target_pairs={{0,3},{1,2},{2,1},{3,0},{4,7},{5,6},{6,5},{7,4},{8,11},{9,10},{10,... | collective-permute-start | bytes 147464 | tf_op jit(solution)/shard_map/ppermute | solution.py:269
  28.7 4.0 %collective-permute-start.2 = (bf16[192,128]{1,0:T(8,128)(2,1)}, bf16[192,128]{1,0:T(8,128)(2,1)S(1)}, u32[]{:S(2)}, u32[]{:S(2)}) collective-permute-start(bf16[192,128]{1,0:T(8,128)(2,1)} %get-tuple-element.21.r0_ref), channel_id=1, source_target_pairs={{0,2},{1,3},{2,0},{3,1},{4,6},{5,7},{6,4},{7,5},{8,10},{9,11},{10,... | collective-permute-start | bytes 147464 | tf_op jit(solution)/shard_map/ppermute | solution.py:269
  32.7 1.9 %collective-permute-start.1 = (bf16[192,128]{1,0:T(8,128)(2,1)}, bf16[192,128]{1,0:T(8,128)(2,1)S(1)}, u32[]{:S(2)}, u32[]{:S(2)}) collective-permute-start(bf16[192,128]{1,0:T(8,128)(2,1)} %get-tuple-element.21.r0_ref), channel_id=1, source_target_pairs={{0,1},{1,0},{2,3},{3,2},{4,5},{5,4},{6,7},{7,6},{8,9},{9,8},{10,11... | collective-permute-start | bytes 147464 | tf_op jit(solution)/shard_map/ppermute | solution.py:269
  34.6 0.0 collective-permute-done.left_ref
  34.6 0.0 collective-permute-done.3.r3_ref
  34.7 0.9 collective-permute-done.2.r2_ref
  35.5 2.5 %collective-permute-done.1.r1_ref = bf16[192,128]{1,0:T(8,128)(2,1)S(1)} collective-permute-done((bf16[192,128]{1,0:T(8,128)(2,1)}, bf16[192,128]{1,0:T(8,128)(2,1)S(1)}, u32[]{:S(2)}, u32[]{:S(2)}) %collective-permute-start.1) | collective-permute-done | bytes 49184 | tf_op jit(solution)/shard_map/ppermute | solution.py:269
  38.0 1.0 all-to-all-done.got_ref
  39.0 0.0 copy-start
  39.0 0.8 copy-done
  39.8 1.0 spread_parts.1
  40.9 7.8 %all-to-all-start.1 = ((bf16[16,192,128]{2,1,0:T(8,128)(2,1)}), bf16[16,192,128]{2,1,0:T(8,128)(2,1)S(1)}, u32[]{:S(2)}, u32[]{:S(2)}) async-start(bf16[16,192,128]{2,1,0:T(8,128)(2,1)} %get-tuple-element.22), calls=%async_computation.1 | async-start | bytes 1572864 | tf_op jit(solution)/shard_map/all_to_all | solution.py:284
  48.6 2.4 %collective-permute-start.4 = (bf16[512,128]{1,0:T(8,128)(2,1)S(1)}, bf16[512,128]{1,0:T(8,128)(2,1)S(1)}, u32[]{:S(2)}, u32[]{:S(2)}) collective-permute-start(bf16[512,128]{1,0:T(8,128)(2,1)S(1)} %get-tuple-element.24), channel_id=1, source_target_pairs={{0,1},{1,0},{2,3},{3,2},{4,5},{5,4},{6,7},{7,6},{8,9},{9,8},{10,11... | collective-permute-start | bytes 393224 | tf_op jit(solution)/shard_map/ppermute | solution.py:285
  51.0 3.5 %collective-permute-start.9 = (bf16[768,128]{1,0:T(8,128)(2,1)S(1)}, bf16[768,128]{1,0:T(8,128)(2,1)S(1)}, u32[]{:S(2)}, u32[]{:S(2)}) collective-permute-start(bf16[768,128]{1,0:T(8,128)(2,1)S(1)} %get-tuple-element.27.r0_ref), channel_id=1, source_target_pairs={{0,72},{8,64},{64,8},{72,0},{1,73},{9,65},{65,9},{73,1},{2,74},{10... | collective-permute-start | bytes 589832 | tf_op jit(solution)/shard_map/ppermute | solution.py:288
  54.5 2.7 %collective-permute-start.8 = (bf16[768,128]{1,0:T(8,128)(2,1)S(1)}, bf16[768,128]{1,0:T(8,128)(2,1)S(1)}, u32[]{:S(2)}, u32[]{:S(2)}) collective-permute-start(bf16[768,128]{1,0:T(8,128)(2,1)S(1)} %get-tuple-element.27.r0_ref), channel_id=1, source_target_pairs={{0,64},{8,72},{64,0},{72,8},{1,65},{9,73},{65,1},{73,9},{2,66},{10... | collective-permute-start | bytes 589832 | tf_op jit(solution)/shard_map/ppermute | solution.py:288
  57.2 2.2 %collective-permute-start.7 = (bf16[768,128]{1,0:T(8,128)(2,1)S(1)}, bf16[768,128]{1,0:T(8,128)(2,1)S(1)}, u32[]{:S(2)}, u32[]{:S(2)}) collective-permute-start(bf16[768,128]{1,0:T(8,128)(2,1)S(1)} %get-tuple-element.27.r0_ref), channel_id=1, source_target_pairs={{0,8},{8,0},{64,72},{72,64},{1,9},{9,1},{65,73},{73,65},{2,10},{10... | collective-permute-start | bytes 589832 | tf_op jit(solution)/shard_map/ppermute | solution.py:288
  59.4 5.0 %collective-permute-start.5 = (bf16[512,128]{1,0:T(8,128)(2,1)S(1)}, bf16[512,128]{1,0:T(8,128)(2,1)S(1)}, u32[]{:S(2)}, u32[]{:S(2)}) collective-permute-start(bf16[512,128]{1,0:T(8,128)(2,1)S(1)} %get-tuple-element.25), channel_id=1, source_target_pairs={{0,2},{1,3},{2,0},{3,1},{4,6},{5,7},{6,4},{7,5},{8,10},{9,11},{10,... | collective-permute-start | bytes 393224 | tf_op jit(solution)/shard_map/ppermute | solution.py:285
  64.4 0.0 collective-permute-done.4.x1_ref
  64.4 2.2 %collective-permute-start.6 = (bf16[512,128]{1,0:T(8,128)(2,1)S(1)}, bf16[512,128]{1,0:T(8,128)(2,1)S(1)}, u32[]{:S(2)}, u32[]{:S(2)}) collective-permute-start(bf16[512,128]{1,0:T(8,128)(2,1)S(1)} %get-tuple-element.26), channel_id=1, source_target_pairs={{0,3},{1,2},{2,1},{3,0},{4,7},{5,6},{6,5},{7,4},{8,11},{9,10},{10,... | collective-permute-start | bytes 393224 | tf_op jit(solution)/shard_map/ppermute | solution.py:285
  66.6 0.4 collective-permute-done.5.x2_ref
  67.0 6.0 %collective-permute-done.6.x3_ref = bf16[512,128]{1,0:T(8,128)(2,1)S(1)} collective-permute-done((bf16[512,128]{1,0:T(8,128)(2,1)S(1)}, bf16[512,128]{1,0:T(8,128)(2,1)S(1)}, u32[]{:S(2)}, u32[]{:S(2)}) %collective-permute-start.6) | collective-permute-done | bytes 131104 | tf_op jit(solution)/shard_map/ppermute | solution.py:285
  73.0 0.4 collective-permute-done.9.r3_ref
  73.5 2.4 %collective-permute-done.8.r2_ref = bf16[768,128]{1,0:T(8,128)(2,1)S(1)} collective-permute-done((bf16[768,128]{1,0:T(8,128)(2,1)S(1)}, bf16[768,128]{1,0:T(8,128)(2,1)S(1)}, u32[]{:S(2)}, u32[]{:S(2)}) %collective-permute-start.8) | collective-permute-done | bytes 196640 | tf_op jit(solution)/shard_map/ppermute | solution.py:288
  75.8 4.3 %collective-permute-done.7.r1_ref = bf16[768,128]{1,0:T(8,128)(2,1)S(1)} collective-permute-done((bf16[768,128]{1,0:T(8,128)(2,1)S(1)}, bf16[768,128]{1,0:T(8,128)(2,1)S(1)}, u32[]{:S(2)}, u32[]{:S(2)}) %collective-permute-start.7) | collective-permute-done | bytes 196640 | tf_op jit(solution)/shard_map/ppermute | solution.py:288
  80.2 0.0 all-to-all-done.1.left_ref
  80.2 0.3 sort_cores.1
  80.5 2.4 %collective-permute-start.10 = (bf16[4,1024,128]{2,1,0:T(8,128)(2,1)S(1)}, bf16[4,1024,128]{2,1,0:T(8,128)(2,1)S(1)}, u32[]{:S(2)}, u32[]{:S(2)}) collective-permute-start(bf16[4,1024,128]{2,1,0:T(8,128)(2,1)S(1)} %get-tuple-element.28), channel_id=1, source_target_pairs={{0,4},{4,0},{1,5},{5,1},{2,6},{6,2},{3,7},{7,3},{8,12},{12,8},{9,1... | collective-permute-start | bytes 3145736 | tf_op jit(solution)/shard_map/ppermute | solution.py:301
  82.9 0.0 copy-done.1
  82.9 0.0 copy-done.2
  82.9 4.7 %sigma_own.1 = (bf16[4,2,2,64,256]{4,3,2,1,0:T(8,128)(2,1)S(1)}, bf16[24,256,256]{2,1,0:T(8,128)(2,1)S(1)}) custom-call(s32[128]{0:T(128)S(1)} %copy-done.1, s32[128]{0:T(128)S(1)} %copy-done.2, bf16[4,1024,128]{2,1,0:T(8,128)(2,1)S(1)} %get-tuple-element.29.refs_2_, bf16[4,768,128]{2,1,0:T(8,128)(2,1)S(1)} %get-tuple-element.30.refs_3_), custom_call_target="tpu_custom_call" | custom-call | tf_op jit(solution)/shard_map/sigma_own/pallas_call | solution.py:319
  87.7 0.0 collective-permute-done.10.got
  87.7 4.3 %sigma_other.1 = bf16[4,2,2,64,256]{4,3,2,1,0:T(8,128)(2,1)S(1)} custom-call(s32[128]{0:T(128)S(1)} %copy-done.1, s32[128]{0:T(128)S(1)} %copy-done.2, bf16[4,1024,128]{2,1,0:T(8,128)(2,1)S(1)} %collective-permute-done.10.got, bf16[24,256,256]{2,1,0:T(8,128)(2,1)S(1)} %get-tuple-element.31.refs_0_, ...), custom_call_target="tpu_custom_call", output_to_operand_aliasing={{}: (4, {})} | custom-call | tf_op jit(solution)/shard_map/sigma_other/pallas_call | solution.py:329
  92.0 10.4 %all_to_all.15.in_ref = bf16[4,2,2,64,256]{4,3,2,1,0:T(8,128)(2,1)S(1)} all-to-all(bf16[4,2,2,64,256]{4,3,2,1,0:T(8,128)(2,1)S(1)} %sigma_other.1), channel_id=1, replica_groups=mesh['yh'=4,'yl'=2,'zh'=4,'zl'=2,'core'=2,'op'=4] {'yl','zl'}, dimensions={0} | all-to-all | bytes 1048576 | tf_op jit(solution)/shard_map/all_to_all | solution.py:341
  102.5 1.1 %merge_sectors.1 = bf16[2,64,2048]{2,1,0:T(8,128)(2,1)} custom-call(bf16[4,2,2,64,256]{4,3,2,1,0:T(8,128)(2,1)S(1)} %all_to_all.15.in_ref), custom_call_target="tpu_custom_call" | custom-call | tf_op jit(solution)/shard_map/merge_sectors/pallas_call | solution.py:342
Async XLA Ops:
  2.7 80.2 %copy-start.1 = (s32[128]{0:T(128)S(1)}, s32[128]{0:T(128)}, u32[]{:S(2)}) copy-start(s32[128]{0:T(128)} %lc.1) | copy-start | bytes 1540
  2.7 80.2 %copy-start.2 = (s32[128]{0:T(128)S(1)}, s32[128]{0:T(128)}, u32[]{:S(2)}) copy-start(s32[128]{0:T(128)} %rc.1) | copy-start | bytes 1540
  2.8 36.3 %all-to-all-start = ((bf16[16,128,128]{2,1,0:T(8,128)(2,1)}), bf16[16,128,128]{2,1,0:T(8,128)(2,1)S(1)}, u32[]{:S(2)}, u32[]{:S(2)}) async-start(bf16[16,128,128]{2,1,0:T(8,128)(2,1)} %get-tuple-element.19), calls=%async_computation | async-start | bytes 1048576 | tf_op jit(solution)/shard_map/all_to_all | solution.py:263
  19.0 15.6 %collective-permute-start = (bf16[192,128]{1,0:T(8,128)(2,1)}, bf16[192,128]{1,0:T(8,128)(2,1)S(1)}, u32[]{:S(2)}, u32[]{:S(2)}) collective-permute-start(bf16[192,128]{1,0:T(8,128)(2,1)} %get-tuple-element.20), channel_id=1, source_target_pairs={{0,0},{1,128},{2,256},{3,384},{128,1},{129,129},{130,257},{131,385... | collective-permute-start | bytes 147464 | tf_op jit(solution)/shard_map/ppermute | solution.py:266
  20.5 14.2 %collective-permute-start.3 = (bf16[192,128]{1,0:T(8,128)(2,1)}, bf16[192,128]{1,0:T(8,128)(2,1)S(1)}, u32[]{:S(2)}, u32[]{:S(2)}) collective-permute-start(bf16[192,128]{1,0:T(8,128)(2,1)} %get-tuple-element.21.r0_ref), channel_id=1, source_target_pairs={{0,3},{1,2},{2,1},{3,0},{4,7},{5,6},{6,5},{7,4},{8,11},{9,10},{10,... | collective-permute-start | bytes 147464 | tf_op jit(solution)/shard_map/ppermute | solution.py:269
  28.7 6.8 %collective-permute-start.2 = (bf16[192,128]{1,0:T(8,128)(2,1)}, bf16[192,128]{1,0:T(8,128)(2,1)S(1)}, u32[]{:S(2)}, u32[]{:S(2)}) collective-permute-start(bf16[192,128]{1,0:T(8,128)(2,1)} %get-tuple-element.21.r0_ref), channel_id=1, source_target_pairs={{0,2},{1,3},{2,0},{3,1},{4,6},{5,7},{6,4},{7,5},{8,10},{9,11},{10,... | collective-permute-start | bytes 147464 | tf_op jit(solution)/shard_map/ppermute | solution.py:269
  32.7 5.3 %collective-permute-start.1 = (bf16[192,128]{1,0:T(8,128)(2,1)}, bf16[192,128]{1,0:T(8,128)(2,1)S(1)}, u32[]{:S(2)}, u32[]{:S(2)}) collective-permute-start(bf16[192,128]{1,0:T(8,128)(2,1)} %get-tuple-element.21.r0_ref), channel_id=1, source_target_pairs={{0,1},{1,0},{2,3},{3,2},{4,5},{5,4},{6,7},{7,6},{8,9},{9,8},{10,11... | collective-permute-start | bytes 147464 | tf_op jit(solution)/shard_map/ppermute | solution.py:269
  39.0 0.8 copy-start
  40.9 39.3 %all-to-all-start.1 = ((bf16[16,192,128]{2,1,0:T(8,128)(2,1)}), bf16[16,192,128]{2,1,0:T(8,128)(2,1)S(1)}, u32[]{:S(2)}, u32[]{:S(2)}) async-start(bf16[16,192,128]{2,1,0:T(8,128)(2,1)} %get-tuple-element.22), calls=%async_computation.1 | async-start | bytes 1572864 | tf_op jit(solution)/shard_map/all_to_all | solution.py:284
  48.6 15.8 %collective-permute-start.4 = (bf16[512,128]{1,0:T(8,128)(2,1)S(1)}, bf16[512,128]{1,0:T(8,128)(2,1)S(1)}, u32[]{:S(2)}, u32[]{:S(2)}) collective-permute-start(bf16[512,128]{1,0:T(8,128)(2,1)S(1)} %get-tuple-element.24), channel_id=1, source_target_pairs={{0,1},{1,0},{2,3},{3,2},{4,5},{5,4},{6,7},{7,6},{8,9},{9,8},{10,11... | collective-permute-start | bytes 393224 | tf_op jit(solution)/shard_map/ppermute | solution.py:285
  51.0 22.5 %collective-permute-start.9 = (bf16[768,128]{1,0:T(8,128)(2,1)S(1)}, bf16[768,128]{1,0:T(8,128)(2,1)S(1)}, u32[]{:S(2)}, u32[]{:S(2)}) collective-permute-start(bf16[768,128]{1,0:T(8,128)(2,1)S(1)} %get-tuple-element.27.r0_ref), channel_id=1, source_target_pairs={{0,72},{8,64},{64,8},{72,0},{1,73},{9,65},{65,9},{73,1},{2,74},{10... | collective-permute-start | bytes 589832 | tf_op jit(solution)/shard_map/ppermute | solution.py:288
  54.5 21.3 %collective-permute-start.8 = (bf16[768,128]{1,0:T(8,128)(2,1)S(1)}, bf16[768,128]{1,0:T(8,128)(2,1)S(1)}, u32[]{:S(2)}, u32[]{:S(2)}) collective-permute-start(bf16[768,128]{1,0:T(8,128)(2,1)S(1)} %get-tuple-element.27.r0_ref), channel_id=1, source_target_pairs={{0,64},{8,72},{64,0},{72,8},{1,65},{9,73},{65,1},{73,9},{2,66},{10... | collective-permute-start | bytes 589832 | tf_op jit(solution)/shard_map/ppermute | solution.py:288
  57.2 23.0 %collective-permute-start.7 = (bf16[768,128]{1,0:T(8,128)(2,1)S(1)}, bf16[768,128]{1,0:T(8,128)(2,1)S(1)}, u32[]{:S(2)}, u32[]{:S(2)}) collective-permute-start(bf16[768,128]{1,0:T(8,128)(2,1)S(1)} %get-tuple-element.27.r0_ref), channel_id=1, source_target_pairs={{0,8},{8,0},{64,72},{72,64},{1,9},{9,1},{65,73},{73,65},{2,10},{10... | collective-permute-start | bytes 589832 | tf_op jit(solution)/shard_map/ppermute | solution.py:288
  59.4 7.6 %collective-permute-start.5 = (bf16[512,128]{1,0:T(8,128)(2,1)S(1)}, bf16[512,128]{1,0:T(8,128)(2,1)S(1)}, u32[]{:S(2)}, u32[]{:S(2)}) collective-permute-start(bf16[512,128]{1,0:T(8,128)(2,1)S(1)} %get-tuple-element.25), channel_id=1, source_target_pairs={{0,2},{1,3},{2,0},{3,1},{4,6},{5,7},{6,4},{7,5},{8,10},{9,11},{10,... | collective-permute-start | bytes 393224 | tf_op jit(solution)/shard_map/ppermute | solution.py:285
  64.4 8.6 %collective-permute-start.6 = (bf16[512,128]{1,0:T(8,128)(2,1)S(1)}, bf16[512,128]{1,0:T(8,128)(2,1)S(1)}, u32[]{:S(2)}, u32[]{:S(2)}) collective-permute-start(bf16[512,128]{1,0:T(8,128)(2,1)S(1)} %get-tuple-element.26), channel_id=1, source_target_pairs={{0,3},{1,2},{2,1},{3,0},{4,7},{5,6},{6,5},{7,4},{8,11},{9,10},{10,... | collective-permute-start | bytes 393224 | tf_op jit(solution)/shard_map/ppermute | solution.py:285
  80.5 7.2 %collective-permute-start.10 = (bf16[4,1024,128]{2,1,0:T(8,128)(2,1)S(1)}, bf16[4,1024,128]{2,1,0:T(8,128)(2,1)S(1)}, u32[]{:S(2)}, u32[]{:S(2)}) collective-permute-start(bf16[4,1024,128]{2,1,0:T(8,128)(2,1)S(1)} %get-tuple-element.28), channel_id=1, source_target_pairs={{0,4},{4,0},{1,5},{5,1},{2,6},{6,2},{3,7},{7,3},{8,12},{12,8},{9,1... | collective-permute-start | bytes 3145736 | tf_op jit(solution)/shard_map/ppermute | solution.py:301

commit v7 on v6

--- a/solution.py
+++ b/solution.py
@@ -1,5 +1,6 @@
 import jax
 import jax.numpy as jnp
+import numpy as np
 from jax import lax
 from jax.experimental import pallas as pl
 from jax.experimental.pallas import tpu as pltpu
@@ -36,8 +37,20 @@
     return jnp.where(keep, moved, jnp.zeros_like(moved))
 
 
+def across(core):
+    return 0, 1 + 2 * core, 2, 3 - 2 * core
+
+
+def around(core):
+    return 0, 1 + core, 2 - core, 3
+
+
 def place():
     return [lax.axis_index(n).astype(jnp.int32) for n in ("op",) + SEC]
+
+
+def turned(core, first, second, size=4):
+    return jnp.where(core == 0, first * size + second, second * size + first)
 
 
 def prepare_kernel(
@@ -45,6 +58,7 @@
     sent_ref, lc_ref, rc_ref, left_ref, right_ref, rows_ref, sems,
 ):
     plane = lax.axis_index("op").astype(jnp.int32)
+    core = lax.axis_index("core").astype(jnp.int32)
     lanes_of = rows_ref.shape[2]
     copies = []
 
@@ -76,8 +90,8 @@
                     sent_ref[yh * ZH + zh, rows, :] = jnp.concatenate(
                         [first[:, lanes], second[:, lanes]], axis=1
                     )
-        places = pl.ds(yh * ZH, ZH)
-        copy(sent_ref.at[places], out_ref.at[places])
+        for zh in range(ZH):
+            copy(sent_ref.at[yh * ZH + zh], out_ref.at[turned(core, yh, zh)])
     for n, (c_ref, in_ref, to_ref) in enumerate(
         ((lc_ref, left_ref, lout_ref), (rc_ref, right_ref, rout_ref))
     ):
@@ -95,51 +109,51 @@
 
 
 def spread_kernel(
-    got_ref, left_ref, r0_ref, r1_ref, r2_ref, r3_ref,
-    x0_ref, x1_ref, x2_ref, x3_ref, sent_ref, right_ref,
+    got_ref, left_ref, r0_ref, ra_ref, rb_ref, rc_ref, p0_ref, pa_ref, pb_ref, pc_ref, sent_ref
 ):
     plane = lax.axis_index("op").astype(jnp.int32)
+    core = lax.axis_index("core").astype(jnp.int32)
     wide = CORE * XROWS
-    for d, ref in enumerate((x0_ref, x1_ref, x2_ref, x3_ref)):
+    for ref, d in zip((p0_ref, pa_ref, pb_ref, pc_ref), across(core)):
         to = jnp.bitwise_xor(plane, d)
         for z in range(ZH):
-            ref[z * wide:(z + 1) * wide, :] = got_ref[to * ZH + z]
+            ref[z * wide:(z + 1) * wide, :] = got_ref[turned(core, to, z)]
+        for right_ref, e in zip((r0_ref, ra_ref, rb_ref, rc_ref), around(core)):
+            rows = pl.ds(pl.multiple_of(ZH * wide + e * RROWS, BLOCK), RROWS)
+            ref[rows, :] = right_ref[...]
     for to in range(YH * ZH):
         sent_ref[to] = left_ref[...]
-    for d, ref in enumerate((r0_ref, r1_ref, r2_ref, r3_ref)):
-        right_ref[d * RROWS:(d + 1) * RROWS, :] = ref[...]
-
-
-def core_kernel(
-    left_ref, x0_ref, x1_ref, x2_ref, x3_ref, r0_ref, r1_ref, r2_ref, r3_ref,
-    own_ref, give_ref, near_ref,
-):
+
+
+def core_kernel(left_ref, p0_ref, pa_ref, pb_ref, pc_ref, own_ref, give_ref, near_ref):
     x_at, _, yl_at, _, zl_at, core = place()
-    for e, ref in enumerate((r0_ref, r1_ref, r2_ref, r3_ref)):
-        near_ref[jnp.bitwise_xor(yl_at * ZL + zl_at, e)] = ref[...]
-    for d, ref in enumerate((x0_ref, x1_ref, x2_ref, x3_ref)):
+    for ref, d in zip((p0_ref, pa_ref, pb_ref, pc_ref), across(core)):
         x = jnp.bitwise_xor(x_at, d)
         for z in range(ZH):
             rows = slice(z * XROWS, (z + 1) * XROWS)
             for to_ref, c in ((own_ref, core), (give_ref, 1 - core)):
                 at = pl.multiple_of((z * CORE + c) * XROWS, XROWS)
                 to_ref[x, rows, :] = ref[pl.ds(at, XROWS), :]
+        rows = pl.ds(pl.multiple_of(x * RROWS, BLOCK), RROWS)
+        for e in range(YL * ZL):
+            at = FROM * XROWS + e * RROWS
+            near_ref[jnp.bitwise_xor(yl_at * ZL + zl_at, e), rows, :] = ref[at:at + RROWS, :]
     for x in range(XDIM):
         for z in range(ZH):
             rows = slice(ZH * XROWS + z * RROWS, ZH * XROWS + (z + 1) * RROWS)
-            left = left_ref[x * ZH + z]
+            left = left_ref[turned(core, x, z)]
             own_ref[x, rows, :] = left
             give_ref[x, rows, :] = left
 
 
-def build_right(x_at, near_ref, right_ref):
+def build_right(near_ref, right_ref):
     zeros = jnp.zeros((BLOCK, WIDE), jnp.bfloat16)
     for b in range(4):
         rows = slice(b * BLOCK, (b + 1) * BLOCK)
         used = slice((b // 2) * WIDE, (b // 2 + 1) * WIDE)
         unused = slice((1 - b // 2) * WIDE, (2 - b // 2) * WIDE)
         for d in range(XDIM):
-            first = jnp.bitwise_xor(x_at, d) * HERE
+            first = d * HERE
             for p in range(PAIRS):
                 at = d * RROWS + p * BLOCK
                 piece = near_ref[b, at:at + BLOCK, :]
@@ -170,7 +184,7 @@
         right_ref, _, out_ref, left_ref, half_ref = refs
     x_at, yh_at, yl_at, zh_at, zl_at, core = place()
     if c == 0:
-        build_right(x_at, near_ref, right_ref)
+        build_right(near_ref, right_ref)
     vectors = half_ref.shape[0] // GROUP
     for v in range(vectors):
         rows = []
@@ -198,7 +212,7 @@
         for v in range(vectors):
             at = v * GROUP + b * BLOCK
             block = out[at:at + BLOCK]
-            out_ref[b, 0, v] = jnp.where(allowed, block, jnp.zeros_like(block)).astype(
+            out_ref[turned(core, b // 2, b % 2, 2), 0, v] = jnp.where(allowed, block, jnp.zeros_like(block)).astype(
                 out_ref.dtype
             )
 
@@ -208,14 +222,36 @@
     for yl in range(YL):
         for zl in range(ZL):
             for m in range(ZH // 2):
-                low = in_ref[yl * ZL + zl, core, 0, :, m * WIDE:(m + 1) * WIDE]
-                high = in_ref[yl * ZL + zl, 1 - core, 0, :, m * WIDE:(m + 1) * WIDE]
+                low = in_ref[turned(core, yl, zl, 2), core, 0, :, m * WIDE:(m + 1) * WIDE]
+                high = in_ref[turned(core, yl, zl, 2), 1 - core, 0, :, m * WIDE:(m + 1) * WIDE]
                 for h in range(2):
                     lanes = slice(h * BLOCK, (h + 1) * BLOCK)
                     at = ((yl * ZH + 2 * m + h) * ZL + zl) * WIDE
                     out_ref[0, :, at:at + WIDE] = jnp.concatenate(
                         [low[:, lanes], high[:, lanes]], axis=1
                     )
+
+
+def exchange(array, ids, axes):
+    ids = np.moveaxis(ids, [SEC.index(a) for a in axes], [-2, -1])
+    at = [a for a in SEC if a not in axes].index("core")
+    groups = []
+    for index in np.ndindex(*ids.shape[:-2]):
+        group = ids[index] if index[at] == 0 else ids[index].T
+        groups.append([int(n) for n in group.reshape(-1)])
+    return lax.all_to_all(array, SEC + ("op",), 0, 0, tiled=True, axis_index_groups=groups)
+
+
+def partners(axis_of_core, steps):
+    pairs = []
+    for core in range(CORE):
+        for n in range(4):
+            to = n ^ steps[core]
+            if axis_of_core == 0:
+                pairs.append((core * 4 + n, core * 4 + to))
+            else:
+                pairs.append((n * CORE + core, to * CORE + core))
+    return pairs
 
 
 def body(
@@ -228,6 +264,7 @@
     right_charge,
 ):
     vectors, _, states = trial_state.shape
+    ids = np.arange(YH * YL * ZH * ZL * CORE * XDIM).reshape(YH, YL, ZH, ZL, CORE, XDIM)
     smem = pl.BlockSpec(memory_space=pltpu.SMEM)
     vmem = pl.BlockSpec(memory_space=pltpu.VMEM)
     anywhere = pl.BlockSpec(memory_space=pl.ANY)
@@ -250,7 +287,7 @@
             pltpu.VMEM(left_operators.shape, jnp.bfloat16),
             pltpu.VMEM(right_operators.shape, jnp.bfloat16),
             pltpu.VMEM((YH, HALF, states // YH), jnp.bfloat16),
-            pltpu.SemaphoreType.DMA((2 * YH + 4,)),
+            pltpu.SemaphoreType.DMA((YH + 4 + YH * ZH,)),
         ],
         name="prepare_parts",
     )(
@@ -260,44 +297,41 @@
         right_operators,
         trial_state,
     )
-    got = lax.all_to_all(sent, FAR, 0, 0, tiled=True)
+    got = exchange(sent, ids, FAR)
 
     swap = [(q * XDIM + x, x * XDIM + q) for q in range(YH) for x in range(XDIM)]
     left = lax.ppermute(left, ("yh", "op"), swap)
 
-    across = [[(n, n ^ d) for n in range(XDIM)] for d in range(XDIM)]
-    rights = [right] + [lax.ppermute(right, "op", across[d]) for d in (1, 2, 3)]
-
-    plane = jax.ShapeDtypeStruct((ZH * wide, WIDE), jnp.bfloat16)
-    *parts, left, right = pl.pallas_call(
+    rights = [right] + [
+        lax.ppermute(right, NEAR + ("core",), partners(1, [around(c)[n] for c in range(CORE)]))
+        for n in (1, 2, 3)
+    ]
+
+    pack = jax.ShapeDtypeStruct((ZH * wide + YL * ZL * RROWS, WIDE), jnp.bfloat16)
+    *packs, left = pl.pallas_call(
         spread_kernel,
         in_specs=[vmem] * 6,
-        out_specs=[vmem] * 6,
-        out_shape=[plane] * XDIM
-        + [
-            jax.ShapeDtypeStruct((YH * ZH, RROWS, WIDE), jnp.bfloat16),
-            jax.ShapeDtypeStruct((XDIM * RROWS, WIDE), jnp.bfloat16),
-        ],
+        out_specs=[vmem] * 5,
+        out_shape=[pack] * XDIM + [jax.ShapeDtypeStruct((YH * ZH, RROWS, WIDE), jnp.bfloat16)],
         compiler_params=small,
         name="spread_parts",
     )(got, left, *rights)
-    left = lax.all_to_all(left, FAR, 0, 0, tiled=True)
-    parts = parts[:1] + [lax.ppermute(parts[d], "op", across[d]) for d in (1, 2, 3)]
-
-    rights = [right] + [
-        lax.ppermute(right, NEAR, [(n, n ^ d) for n in range(YL * ZL)]) for d in (1, 2, 3)
+    left = exchange(left, ids, FAR)
+    packs = packs[:1] + [
+        lax.ppermute(packs[n], ("core", "op"), partners(0, [across(c)[n] for c in range(CORE)]))
+        for n in (1, 2, 3)
     ]
 
     mine = jax.ShapeDtypeStruct((XDIM, ZH * (XROWS + RROWS), WIDE), jnp.bfloat16)
-    near = jax.ShapeDtypeStruct((YL * ZL,) + right.shape, jnp.bfloat16)
+    near = jax.ShapeDtypeStruct((YL * ZL, XDIM * RROWS, WIDE), jnp.bfloat16)
     own, give, right = pl.pallas_call(
         core_kernel,
-        in_specs=[vmem] * 9,
+        in_specs=[vmem] * 5,
         out_specs=[vmem] * 3,
         out_shape=[mine, mine, near],
         compiler_params=small,
         name="sort_cores",
-    )(left, *parts, *rights)
+    )(left, *packs)
     other = lax.ppermute(give, "core", [(0, 1), (1, 0)])
 
     shared = [
@@ -338,7 +372,7 @@
         name="sigma_other",
     )(left_charge, right_charge, other, diagonal, partial)
 
-    partial = lax.all_to_all(partial, NEAR, 0, 0, tiled=True)
+    partial = exchange(partial, ids, NEAR)
     return pl.pallas_call(
         merge_kernel,
         grid=(vectors,),

time: 104 us -> 103 us (level)
  the two profiles are of different devices: /device:TPU:1 before, /device:TPU:60 now
where the time goes in v7:
time: 103 us; the launch traced here: 102 us
  starting transfers between devices  50.6 us (49%)
  blocking collectives  19 us (18%)
  waiting for transfers between devices  17.3 us (17%)
  Pallas kernels  14.3 us (14%)
    all_to_all x2, starting transfers between devices, exchange(): lax.all_to_all(array, SEC + ('op',), 0, 0, tiled=True, axis_index_groups=...  25.4 us
    all_to_all x1, blocking collectives, exchange(): lax.all_to_all(array, SEC + ('op',), 0, 0, tiled=True, axis_index_groups=...  19 us
    ppermute x3, waiting for transfers between devices, body(): lax.ppermute(packs[n], ('core', 'op'), partners(0, [across(c)[n] for c in...  11 us
    ppermute x3, starting transfers between devices, body(): lax.ppermute(right, NEAR + ('core',), partners(1, [around(c)[n] for c in...  9.21 us
    ppermute x3, starting transfers between devices, body(): lax.ppermute(packs[n], ('core', 'op'), partners(0, [across(c)[n] for c in...  9.2 us
    ppermute x1, starting transfers between devices, body(): left = lax.ppermute(left, ('yh', 'op'), swap)  4.89 us
    pallas_call x1, Pallas kernels, body(): pl.pallas_call(lambda *refs: sigma_kernel(0, *refs), grid=(1,), in_specs=...  4.57 us
    pallas_call x1, Pallas kernels, body(): pl.pallas_call(lambda lc, rc, got, *refs: sigma_kernel(1, lc, rc, got, No...  4.33 us
  transfers between devices with their start and end apart: 10, of which 6 were waited for; matrix products, arithmetic and copies ran while one was open for 0% of the time, Pallas kernels for 4%

profile of v7, /device:TPU:60, one launch (start us, length us, event | category | flops | bytes accessed | tf_op | source)
XLA Modules:
  0.0 102.2 jit_solution(1208762075085128764)
XLA Ops:
  0.0 2.8 %prepare_parts.1 = (bf16[16,128,128]{2,1,0:T(8,128)(2,1)}, bf16[192,128]{1,0:T(8,128)(2,1)}, bf16[192,128]{1,0:T(8,128)(2,1)}) custom-call(s32[1,6]{1,0:T(1,128)} %bitcast.2, s32[1,6]{1,0:T(1,128)} %bitcast.3, bf16[6,64,64]{2,1,0:T(8,128)(2,1)} %left_in.1, bf16[6,64,64]{2,1,0:T(8,128)(2,1)} %right_in.1, bf16[2,64,8192]{2,1,0:T(8,128)(2,1)} %x_ref.1), custom_call_target="tpu_custom_call" | custom-call | tf_op jit(solution)/shard_map/prepare_parts/pallas_call | solution.py:278
  2.8 0.0 copy-start.1
  2.9 0.0 copy-start.2
  2.9 15.5 %all-to-all-start = ((bf16[16,128,128]{2,1,0:T(8,128)(2,1)}), bf16[16,128,128]{2,1,0:T(8,128)(2,1)S(1)}, u32[]{:S(2)}, u32[]{:S(2)}) async-start(bf16[16,128,128]{2,1,0:T(8,128)(2,1)} %get-tuple-element.18), calls=%async_computation | async-start | bytes 1048576 | tf_op jit(solution)/shard_map/all_to_all | solution.py:242
  18.3 4.9 %collective-permute-start = (bf16[192,128]{1,0:T(8,128)(2,1)}, bf16[192,128]{1,0:T(8,128)(2,1)S(1)}, u32[]{:S(2)}, u32[]{:S(2)}) collective-permute-start(bf16[192,128]{1,0:T(8,128)(2,1)} %get-tuple-element.19), channel_id=1, source_target_pairs={{0,0},{1,128},{2,256},{3,384},{128,1},{129,129},{130,257},{131,385... | collective-permute-start | bytes 147464 | tf_op jit(solution)/shard_map/ppermute | solution.py:303
  23.2 4.2 %collective-permute-start.3 = (bf16[192,128]{1,0:T(8,128)(2,1)}, bf16[192,128]{1,0:T(8,128)(2,1)S(1)}, u32[]{:S(2)}, u32[]{:S(2)}) collective-permute-start(bf16[192,128]{1,0:T(8,128)(2,1)} %get-tuple-element.20.r0_ref), channel_id=1, source_target_pairs={{0,72},{8,64},{64,8},{72,0},{4,76},{12,68},{68,12},{76,4},{1,73},{... | collective-permute-start | bytes 147464 | tf_op jit(solution)/shard_map/ppermute | solution.py:306
  27.4 2.6 %collective-permute-start.2 = (bf16[192,128]{1,0:T(8,128)(2,1)}, bf16[192,128]{1,0:T(8,128)(2,1)S(1)}, u32[]{:S(2)}, u32[]{:S(2)}) collective-permute-start(bf16[192,128]{1,0:T(8,128)(2,1)} %get-tuple-element.20.r0_ref), channel_id=1, source_target_pairs={{0,64},{8,72},{64,0},{72,8},{4,12},{12,4},{68,76},{76,68},{1,65},{... | collective-permute-start | bytes 147464 | tf_op jit(solution)/shard_map/ppermute | solution.py:306
  30.0 2.5 %collective-permute-start.1 = (bf16[192,128]{1,0:T(8,128)(2,1)}, bf16[192,128]{1,0:T(8,128)(2,1)S(1)}, u32[]{:S(2)}, u32[]{:S(2)}) collective-permute-start(bf16[192,128]{1,0:T(8,128)(2,1)} %get-tuple-element.20.r0_ref), channel_id=1, source_target_pairs={{0,8},{8,0},{64,72},{72,64},{4,68},{12,76},{68,4},{76,12},{1,9},{9... | collective-permute-start | bytes 147464 | tf_op jit(solution)/shard_map/ppermute | solution.py:306
  32.5 3.5 %collective-permute-done.left_ref = bf16[192,128]{1,0:T(8,128)(2,1)S(1)} collective-permute-done((bf16[192,128]{1,0:T(8,128)(2,1)}, bf16[192,128]{1,0:T(8,128)(2,1)S(1)}, u32[]{:S(2)}, u32[]{:S(2)}) %collective-permute-start) | collective-permute-done | bytes 49184 | tf_op jit(solution)/shard_map/ppermute | solution.py:303
  36.0 0.0 collective-permute-done.3.rc_ref
  36.0 0.0 collective-permute-done.2.rb_ref
  36.0 0.2 collective-permute-done.1.ra_ref
  36.2 0.3 all-to-all-done.got_ref
  36.5 0.0 copy-start
  36.5 0.8 copy-done
  37.3 1.1 %spread_parts.1 = (bf16[1280,128]{1,0:T(8,128)(2,1)S(1)}, bf16[1280,128]{1,0:T(8,128)(2,1)S(1)}, bf16[1280,128]{1,0:T(8,128)(2,1)S(1)}, bf16[1280,128]{1,0:T(8,128)(2,1)S(1)}, bf16[16,192,128]{2,1,0:T(8,128)(2,1)}) custom-call(bf16[16,128,128]{2,1,0:T(8,128)(2,1)S(1)} %all-to-all-done.got_ref, bf16[192,128]{1,0:T(8,128)(2,1)S(1)} %collective-permute-done.left_ref, ...), custom_call_target="tpu_custom_call" | custom-call | tf_op jit(solution)/shard_map/spread_parts/pallas_call | solution.py:311
  38.4 9.9 %all-to-all-start.1 = ((bf16[16,192,128]{2,1,0:T(8,128)(2,1)}), bf16[16,192,128]{2,1,0:T(8,128)(2,1)S(1)}, u32[]{:S(2)}, u32[]{:S(2)}) async-start(bf16[16,192,128]{2,1,0:T(8,128)(2,1)} %get-tuple-element.21), calls=%async_computation.1 | async-start | bytes 1572864 | tf_op jit(solution)/shard_map/all_to_all | solution.py:242
  48.4 3.8 %collective-permute-start.4 = (bf16[1280,128]{1,0:T(8,128)(2,1)S(1)}, bf16[1280,128]{1,0:T(8,128)(2,1)S(1)}, u32[]{:S(2)}, u32[]{:S(2)}) collective-permute-start(bf16[1280,128]{1,0:T(8,128)(2,1)S(1)} %get-tuple-element.23), channel_id=1, source_target_pairs={{0,1},{1,0},{2,3},{3,2},{4,7},{5,6},{6,5},{7,4},{8,9},{9,8},{10,11... | collective-permute-start | bytes 983048 | tf_op jit(solution)/shard_map/ppermute | solution.py:321
  52.2 2.9 %collective-permute-start.5 = (bf16[1280,128]{1,0:T(8,128)(2,1)S(1)}, bf16[1280,128]{1,0:T(8,128)(2,1)S(1)}, u32[]{:S(2)}, u32[]{:S(2)}) collective-permute-start(bf16[1280,128]{1,0:T(8,128)(2,1)S(1)} %get-tuple-element.24), channel_id=1, source_target_pairs={{0,2},{1,3},{2,0},{3,1},{4,6},{5,7},{6,4},{7,5},{8,10},{9,11},{10,... | collective-permute-start | bytes 983048 | tf_op jit(solution)/shard_map/ppermute | solution.py:321
  55.1 2.5 %collective-permute-start.6 = (bf16[1280,128]{1,0:T(8,128)(2,1)S(1)}, bf16[1280,128]{1,0:T(8,128)(2,1)S(1)}, u32[]{:S(2)}, u32[]{:S(2)}) collective-permute-start(bf16[1280,128]{1,0:T(8,128)(2,1)S(1)} %get-tuple-element.25), channel_id=1, source_target_pairs={{0,3},{1,2},{2,1},{3,0},{4,5},{5,4},{6,7},{7,6},{8,11},{9,10},{10,... | collective-permute-start | bytes 983048 | tf_op jit(solution)/shard_map/ppermute | solution.py:321
  57.6 3.2 %collective-permute-done.4.pa_ref = bf16[1280,128]{1,0:T(8,128)(2,1)S(1)} collective-permute-done((bf16[1280,128]{1,0:T(8,128)(2,1)S(1)}, bf16[1280,128]{1,0:T(8,128)(2,1)S(1)}, u32[]{:S(2)}, u32[]{:S(2)}) %collective-permute-start.4) | collective-permute-done | bytes 327712 | tf_op jit(solution)/shard_map/ppermute | solution.py:321
  60.8 7.8 %collective-permute-done.5.pb_ref = bf16[1280,128]{1,0:T(8,128)(2,1)S(1)} collective-permute-done((bf16[1280,128]{1,0:T(8,128)(2,1)S(1)}, bf16[1280,128]{1,0:T(8,128)(2,1)S(1)}, u32[]{:S(2)}, u32[]{:S(2)}) %collective-permute-start.5) | collective-permute-done | bytes 327712 | tf_op jit(solution)/shard_map/ppermute | solution.py:321
  68.6 0.0 collective-permute-done.6.pc_ref
  68.6 2.3 %all-to-all-done.1.left_ref = bf16[16,192,128]{2,1,0:T(8,128)(2,1)S(1)} async-done(((bf16[16,192,128]{2,1,0:T(8,128)(2,1)}), bf16[16,192,128]{2,1,0:T(8,128)(2,1)S(1)}, u32[]{:S(2)}, u32[]{:S(2)}) %all-to-all-start.1) | async-done | bytes 786464 | tf_op jit(solution)/shard_map/all_to_all | solution.py:242
  70.9 0.4 sort_cores.1
  71.3 1.9 %collective-permute-start.7 = (bf16[4,1024,128]{2,1,0:T(8,128)(2,1)S(1)}, bf16[4,1024,128]{2,1,0:T(8,128)(2,1)S(1)}, u32[]{:S(2)}, u32[]{:S(2)}) collective-permute-start(bf16[4,1024,128]{2,1,0:T(8,128)(2,1)S(1)} %get-tuple-element.26), channel_id=1, source_target_pairs={{0,4},{4,0},{1,5},{5,1},{2,6},{6,2},{3,7},{7,3},{8,12},{12,8},{9,1... | collective-permute-start | bytes 3145736 | tf_op jit(solution)/shard_map/ppermute | solution.py:335
  73.2 0.0 copy-done.1
  73.2 0.0 copy-done.2
  73.2 4.6 %sigma_own.1 = (bf16[4,2,2,64,256]{4,3,2,1,0:T(8,128)(2,1)S(1)}, bf16[24,256,256]{2,1,0:T(8,128)(2,1)S(1)}) custom-call(s32[128]{0:T(128)S(1)} %copy-done.1, s32[128]{0:T(128)S(1)} %copy-done.2, bf16[4,1024,128]{2,1,0:T(8,128)(2,1)S(1)} %get-tuple-element.27.refs_2_, bf16[4,768,128]{2,1,0:T(8,128)(2,1)S(1)} %get-tuple-element.28.refs_3_), custom_call_target="tpu_custom_call" | custom-call | tf_op jit(solution)/shard_map/sigma_own/pallas_call | solution.py:353
  77.8 0.0 collective-permute-done.7.got
  77.8 4.3 %sigma_other.1 = bf16[4,2,2,64,256]{4,3,2,1,0:T(8,128)(2,1)S(1)} custom-call(s32[128]{0:T(128)S(1)} %copy-done.1, s32[128]{0:T(128)S(1)} %copy-done.2, bf16[4,1024,128]{2,1,0:T(8,128)(2,1)S(1)} %collective-permute-done.7.got, bf16[24,256,256]{2,1,0:T(8,128)(2,1)S(1)} %get-tuple-element.29.refs_0_, ...), custom_call_target="tpu_custom_call", output_to_operand_aliasing={{}: (4, {})} | custom-call | tf_op jit(solution)/shard_map/sigma_other/pallas_call | solution.py:363
  82.1 19.0 %all_to_all.15.in_ref = bf16[4,2,2,64,256]{4,3,2,1,0:T(8,128)(2,1)S(1)} all-to-all(bf16[4,2,2,64,256]{4,3,2,1,0:T(8,128)(2,1)S(1)} %sigma_other.1), channel_id=1, replica_groups={{0,8,64,72},{1,9,65,73},{2,10,66,74},{3,11,67,75},{4,68,12,76},{5,69,13..., dimensions={0} | all-to-all | bytes 1048576 | tf_op jit(solution)/shard_map/all_to_all | solution.py:242
  101.2 1.1 %merge_sectors.1 = bf16[2,64,2048]{2,1,0:T(8,128)(2,1)} custom-call(bf16[4,2,2,64,256]{4,3,2,1,0:T(8,128)(2,1)S(1)} %all_to_all.15.in_ref), custom_call_target="tpu_custom_call" | custom-call | tf_op jit(solution)/shard_map/merge_sectors/pallas_call | solution.py:376
Async XLA Ops:
  2.8 70.3 %copy-start.1 = (s32[128]{0:T(128)S(1)}, s32[128]{0:T(128)}, u32[]{:S(2)}) copy-start(s32[128]{0:T(128)} %lc.1) | copy-start | bytes 1540
  2.9 70.3 %copy-start.2 = (s32[128]{0:T(128)S(1)}, s32[128]{0:T(128)}, u32[]{:S(2)}) copy-start(s32[128]{0:T(128)} %rc.1) | copy-start | bytes 1540
  2.9 33.6 %all-to-all-start = ((bf16[16,128,128]{2,1,0:T(8,128)(2,1)}), bf16[16,128,128]{2,1,0:T(8,128)(2,1)S(1)}, u32[]{:S(2)}, u32[]{:S(2)}) async-start(bf16[16,128,128]{2,1,0:T(8,128)(2,1)} %get-tuple-element.18), calls=%async_computation | async-start | bytes 1048576 | tf_op jit(solution)/shard_map/all_to_all | solution.py:242
  18.3 17.6 %collective-permute-start = (bf16[192,128]{1,0:T(8,128)(2,1)}, bf16[192,128]{1,0:T(8,128)(2,1)S(1)}, u32[]{:S(2)}, u32[]{:S(2)}) collective-permute-start(bf16[192,128]{1,0:T(8,128)(2,1)} %get-tuple-element.19), channel_id=1, source_target_pairs={{0,0},{1,128},{2,256},{3,384},{128,1},{129,129},{130,257},{131,385... | collective-permute-start | bytes 147464 | tf_op jit(solution)/shard_map/ppermute | solution.py:303
  23.2 12.7 %collective-permute-start.3 = (bf16[192,128]{1,0:T(8,128)(2,1)}, bf16[192,128]{1,0:T(8,128)(2,1)S(1)}, u32[]{:S(2)}, u32[]{:S(2)}) collective-permute-start(bf16[192,128]{1,0:T(8,128)(2,1)} %get-tuple-element.20.r0_ref), channel_id=1, source_target_pairs={{0,72},{8,64},{64,8},{72,0},{4,76},{12,68},{68,12},{76,4},{1,73},{... | collective-permute-start | bytes 147464 | tf_op jit(solution)/shard_map/ppermute | solution.py:306
  27.4 8.5 %collective-permute-start.2 = (bf16[192,128]{1,0:T(8,128)(2,1)}, bf16[192,128]{1,0:T(8,128)(2,1)S(1)}, u32[]{:S(2)}, u32[]{:S(2)}) collective-permute-start(bf16[192,128]{1,0:T(8,128)(2,1)} %get-tuple-element.20.r0_ref), channel_id=1, source_target_pairs={{0,64},{8,72},{64,0},{72,8},{4,12},{12,4},{68,76},{76,68},{1,65},{... | collective-permute-start | bytes 147464 | tf_op jit(solution)/shard_map/ppermute | solution.py:306
  30.0 6.2 %collective-permute-start.1 = (bf16[192,128]{1,0:T(8,128)(2,1)}, bf16[192,128]{1,0:T(8,128)(2,1)S(1)}, u32[]{:S(2)}, u32[]{:S(2)}) collective-permute-start(bf16[192,128]{1,0:T(8,128)(2,1)} %get-tuple-element.20.r0_ref), channel_id=1, source_target_pairs={{0,8},{8,0},{64,72},{72,64},{4,68},{12,76},{68,4},{76,12},{1,9},{9... | collective-permute-start | bytes 147464 | tf_op jit(solution)/shard_map/ppermute | solution.py:306
  36.5 0.8 copy-start
  38.4 32.4 %all-to-all-start.1 = ((bf16[16,192,128]{2,1,0:T(8,128)(2,1)}), bf16[16,192,128]{2,1,0:T(8,128)(2,1)S(1)}, u32[]{:S(2)}, u32[]{:S(2)}) async-start(bf16[16,192,128]{2,1,0:T(8,128)(2,1)} %get-tuple-element.21), calls=%async_computation.1 | async-start | bytes 1572864 | tf_op jit(solution)/shard_map/all_to_all | solution.py:242
  48.4 12.4 %collective-permute-start.4 = (bf16[1280,128]{1,0:T(8,128)(2,1)S(1)}, bf16[1280,128]{1,0:T(8,128)(2,1)S(1)}, u32[]{:S(2)}, u32[]{:S(2)}) collective-permute-start(bf16[1280,128]{1,0:T(8,128)(2,1)S(1)} %get-tuple-element.23), channel_id=1, source_target_pairs={{0,1},{1,0},{2,3},{3,2},{4,7},{5,6},{6,5},{7,4},{8,9},{9,8},{10,11... | collective-permute-start | bytes 983048 | tf_op jit(solution)/shard_map/ppermute | solution.py:321
  52.2 16.4 %collective-permute-start.5 = (bf16[1280,128]{1,0:T(8,128)(2,1)S(1)}, bf16[1280,128]{1,0:T(8,128)(2,1)S(1)}, u32[]{:S(2)}, u32[]{:S(2)}) collective-permute-start(bf16[1280,128]{1,0:T(8,128)(2,1)S(1)} %get-tuple-element.24), channel_id=1, source_target_pairs={{0,2},{1,3},{2,0},{3,1},{4,6},{5,7},{6,4},{7,5},{8,10},{9,11},{10,... | collective-permute-start | bytes 983048 | tf_op jit(solution)/shard_map/ppermute | solution.py:321
  55.1 13.5 %collective-permute-start.6 = (bf16[1280,128]{1,0:T(8,128)(2,1)S(1)}, bf16[1280,128]{1,0:T(8,128)(2,1)S(1)}, u32[]{:S(2)}, u32[]{:S(2)}) collective-permute-start(bf16[1280,128]{1,0:T(8,128)(2,1)S(1)} %get-tuple-element.25), channel_id=1, source_target_pairs={{0,3},{1,2},{2,1},{3,0},{4,5},{5,4},{6,7},{7,6},{8,11},{9,10},{10,... | collective-permute-start | bytes 983048 | tf_op jit(solution)/shard_map/ppermute | solution.py:321
  71.3 6.5 %collective-permute-start.7 = (bf16[4,1024,128]{2,1,0:T(8,128)(2,1)S(1)}, bf16[4,1024,128]{2,1,0:T(8,128)(2,1)S(1)}, u32[]{:S(2)}, u32[]{:S(2)}) collective-permute-start(bf16[4,1024,128]{2,1,0:T(8,128)(2,1)S(1)} %get-tuple-element.26), channel_id=1, source_target_pairs={{0,4},{4,0},{1,5},{5,1},{2,6},{6,2},{3,7},{7,3},{8,12},{12,8},{9,1... | collective-permute-start | bytes 3145736 | tf_op jit(solution)/shard_map/ppermute | solution.py:335

commit v8 on v7

--- a/solution.py
+++ b/solution.py
@@ -141,7 +141,8 @@
     for x in range(XDIM):
         for z in range(ZH):
             rows = slice(ZH * XROWS + z * RROWS, ZH * XROWS + (z + 1) * RROWS)
-            left = left_ref[turned(core, x, z)]
+            n = x * ZH + z
+            left = left_ref[jnp.where(core == 0, n, YH * ZH - 1 - n)]
             own_ref[x, rows, :] = left
             give_ref[x, rows, :] = left
 
@@ -232,12 +233,14 @@
                     )
 
 
-def exchange(array, ids, axes):
+def exchange(array, ids, axes, backwards=False):
     ids = np.moveaxis(ids, [SEC.index(a) for a in axes], [-2, -1])
     at = [a for a in SEC if a not in axes].index("core")
     groups = []
     for index in np.ndindex(*ids.shape[:-2]):
-        group = ids[index] if index[at] == 0 else ids[index].T
+        group = ids[index]
+        if index[at] == 1:
+            group = np.flip(group) if backwards else group.T
         groups.append([int(n) for n in group.reshape(-1)])
     return lax.all_to_all(array, SEC + ("op",), 0, 0, tiled=True, axis_index_groups=groups)
 
@@ -316,7 +319,7 @@
         compiler_params=small,
         name="spread_parts",
     )(got, left, *rights)
-    left = exchange(left, ids, FAR)
+    left = exchange(left, ids, FAR, backwards=True)
     packs = packs[:1] + [
         lax.ppermute(packs[n], ("core", "op"), partners(0, [across(c)[n] for c in range(CORE)]))
         for n in (1, 2, 3)

time: 103 us -> 97.8 us (0.950)
  the two profiles are of different devices: /device:TPU:60 before, /device:TPU:1 now
where the time goes in v8:
time: 97.8 us; the launch traced here: 96.3 us
  starting transfers between devices  49.2 us (50%)
  waiting for transfers between devices  21.1 us (22%)
  Pallas kernels  14.4 us (15%)
  blocking collectives  10.6 us (11%)
    all_to_all x2, starting transfers between devices, exchange(): lax.all_to_all(array, SEC + ('op',), 0, 0, tiled=True, axis_index_groups=...  27.5 us
    ppermute x3, waiting for transfers between devices, body(): lax.ppermute(packs[n], ('core', 'op'), partners(0, [across(c)[n] for c in...  11.2 us
    all_to_all x1, blocking collectives, exchange(): lax.all_to_all(array, SEC + ('op',), 0, 0, tiled=True, axis_index_groups=...  10.6 us
    ppermute x3, starting transfers between devices, body(): lax.ppermute(packs[n], ('core', 'op'), partners(0, [across(c)[n] for c in...  9.06 us
    ppermute x3, starting transfers between devices, body(): lax.ppermute(right, NEAR + ('core',), partners(1, [around(c)[n] for c in...  8.36 us
    all_to_all x2, waiting for transfers between devices, exchange(): lax.all_to_all(array, SEC + ('op',), 0, 0, tiled=True, axis_index_groups=...  5.68 us
    pallas_call x1, Pallas kernels, body(): pl.pallas_call(lambda *refs: sigma_kernel(0, *refs), grid=(1,), in_specs=...  4.57 us
    pallas_call x1, Pallas kernels, body(): pl.pallas_call(lambda lc, rc, got, *refs: sigma_kernel(1, lc, rc, got, No...  4.34 us
  transfers between devices with their start and end apart: 10, of which 7 were waited for; matrix products, arithmetic and copies ran while one was open for 0% of the time, Pallas kernels for 5%

profile of v8, /device:TPU:1, one launch (start us, length us, event | category | flops | bytes accessed | tf_op | source)
XLA Modules:
  0.0 96.3 jit_solution(3172077452701507598)
XLA Ops:
  0.0 2.8 %prepare_parts.1 = (bf16[16,128,128]{2,1,0:T(8,128)(2,1)}, bf16[192,128]{1,0:T(8,128)(2,1)}, bf16[192,128]{1,0:T(8,128)(2,1)}) custom-call(s32[1,6]{1,0:T(1,128)} %bitcast.2, s32[1,6]{1,0:T(1,128)} %bitcast.3, bf16[6,64,64]{2,1,0:T(8,128)(2,1)} %left_in.1, bf16[6,64,64]{2,1,0:T(8,128)(2,1)} %right_in.1, bf16[2,64,8192]{2,1,0:T(8,128)(2,1)} %x_ref.1), custom_call_target="tpu_custom_call" | custom-call | tf_op jit(solution)/shard_map/prepare_parts/pallas_call | solution.py:281
  2.8 0.0 copy-start.1
  2.9 0.0 copy-start.2
  2.9 16.2 %all-to-all-start = ((bf16[16,128,128]{2,1,0:T(8,128)(2,1)}), bf16[16,128,128]{2,1,0:T(8,128)(2,1)S(1)}, u32[]{:S(2)}, u32[]{:S(2)}) async-start(bf16[16,128,128]{2,1,0:T(8,128)(2,1)} %get-tuple-element.18), calls=%async_computation | async-start | bytes 1048576 | tf_op jit(solution)/shard_map/all_to_all | solution.py:245
  19.1 1.5 %collective-permute-start = (bf16[192,128]{1,0:T(8,128)(2,1)}, bf16[192,128]{1,0:T(8,128)(2,1)S(1)}, u32[]{:S(2)}, u32[]{:S(2)}) collective-permute-start(bf16[192,128]{1,0:T(8,128)(2,1)} %get-tuple-element.19), channel_id=1, source_target_pairs={{0,0},{1,128},{2,256},{3,384},{128,1},{129,129},{130,257},{131,385... | collective-permute-start | bytes 147464 | tf_op jit(solution)/shard_map/ppermute | solution.py:306
  20.6 3.2 %collective-permute-start.3 = (bf16[192,128]{1,0:T(8,128)(2,1)}, bf16[192,128]{1,0:T(8,128)(2,1)S(1)}, u32[]{:S(2)}, u32[]{:S(2)}) collective-permute-start(bf16[192,128]{1,0:T(8,128)(2,1)} %get-tuple-element.20.r0_ref), channel_id=1, source_target_pairs={{0,72},{8,64},{64,8},{72,0},{4,76},{12,68},{68,12},{76,4},{1,73},{... | collective-permute-start | bytes 147464 | tf_op jit(solution)/shard_map/ppermute | solution.py:309
  23.8 2.2 %collective-permute-start.2 = (bf16[192,128]{1,0:T(8,128)(2,1)}, bf16[192,128]{1,0:T(8,128)(2,1)S(1)}, u32[]{:S(2)}, u32[]{:S(2)}) collective-permute-start(bf16[192,128]{1,0:T(8,128)(2,1)} %get-tuple-element.20.r0_ref), channel_id=1, source_target_pairs={{0,64},{8,72},{64,0},{72,8},{4,12},{12,4},{68,76},{76,68},{1,65},{... | collective-permute-start | bytes 147464 | tf_op jit(solution)/shard_map/ppermute | solution.py:309
  26.0 3.0 %collective-permute-start.1 = (bf16[192,128]{1,0:T(8,128)(2,1)}, bf16[192,128]{1,0:T(8,128)(2,1)S(1)}, u32[]{:S(2)}, u32[]{:S(2)}) collective-permute-start(bf16[192,128]{1,0:T(8,128)(2,1)} %get-tuple-element.20.r0_ref), channel_id=1, source_target_pairs={{0,8},{8,0},{64,72},{72,64},{4,68},{12,76},{68,4},{76,12},{1,9},{9... | collective-permute-start | bytes 147464 | tf_op jit(solution)/shard_map/ppermute | solution.py:309
  28.9 0.0 collective-permute-done.left_ref
  29.0 1.2 %collective-permute-done.3.rc_ref = bf16[192,128]{1,0:T(8,128)(2,1)S(1)} collective-permute-done((bf16[192,128]{1,0:T(8,128)(2,1)}, bf16[192,128]{1,0:T(8,128)(2,1)S(1)}, u32[]{:S(2)}, u32[]{:S(2)}) %collective-permute-start.3) | collective-permute-done | bytes 49184 | tf_op jit(solution)/shard_map/ppermute | solution.py:309
  30.2 3.0 %collective-permute-done.2.rb_ref = bf16[192,128]{1,0:T(8,128)(2,1)S(1)} collective-permute-done((bf16[192,128]{1,0:T(8,128)(2,1)}, bf16[192,128]{1,0:T(8,128)(2,1)S(1)}, u32[]{:S(2)}, u32[]{:S(2)}) %collective-permute-start.2) | collective-permute-done | bytes 49184 | tf_op jit(solution)/shard_map/ppermute | solution.py:309
  33.2 0.0 collective-permute-done.1.ra_ref
  33.2 4.4 %all-to-all-done.got_ref = bf16[16,128,128]{2,1,0:T(8,128)(2,1)S(1)} async-done(((bf16[16,128,128]{2,1,0:T(8,128)(2,1)}), bf16[16,128,128]{2,1,0:T(8,128)(2,1)S(1)}, u32[]{:S(2)}, u32[]{:S(2)}) %all-to-all-start) | async-done | bytes 524320 | tf_op jit(solution)/shard_map/all_to_all | solution.py:245
  37.5 0.0 copy-start
  37.5 0.8 copy-done
  38.3 1.1 %spread_parts.1 = (bf16[1280,128]{1,0:T(8,128)(2,1)S(1)}, bf16[1280,128]{1,0:T(8,128)(2,1)S(1)}, bf16[1280,128]{1,0:T(8,128)(2,1)S(1)}, bf16[1280,128]{1,0:T(8,128)(2,1)S(1)}, bf16[16,192,128]{2,1,0:T(8,128)(2,1)}) custom-call(bf16[16,128,128]{2,1,0:T(8,128)(2,1)S(1)} %all-to-all-done.got_ref, bf16[192,128]{1,0:T(8,128)(2,1)S(1)} %collective-permute-done.left_ref, ...), custom_call_target="tpu_custom_call" | custom-call | tf_op jit(solution)/shard_map/spread_parts/pallas_call | solution.py:314
  39.5 11.3 %all-to-all-start.1 = ((bf16[16,192,128]{2,1,0:T(8,128)(2,1)}), bf16[16,192,128]{2,1,0:T(8,128)(2,1)S(1)}, u32[]{:S(2)}, u32[]{:S(2)}) async-start(bf16[16,192,128]{2,1,0:T(8,128)(2,1)} %get-tuple-element.21), calls=%async_computation.1 | async-start | bytes 1572864 | tf_op jit(solution)/shard_map/all_to_all | solution.py:245
  50.8 4.2 %collective-permute-start.4 = (bf16[1280,128]{1,0:T(8,128)(2,1)S(1)}, bf16[1280,128]{1,0:T(8,128)(2,1)S(1)}, u32[]{:S(2)}, u32[]{:S(2)}) collective-permute-start(bf16[1280,128]{1,0:T(8,128)(2,1)S(1)} %get-tuple-element.23), channel_id=1, source_target_pairs={{0,1},{1,0},{2,3},{3,2},{4,7},{5,6},{6,5},{7,4},{8,9},{9,8},{10,11... | collective-permute-start | bytes 983048 | tf_op jit(solution)/shard_map/ppermute | solution.py:324
  55.0 2.9 %collective-permute-start.5 = (bf16[1280,128]{1,0:T(8,128)(2,1)S(1)}, bf16[1280,128]{1,0:T(8,128)(2,1)S(1)}, u32[]{:S(2)}, u32[]{:S(2)}) collective-permute-start(bf16[1280,128]{1,0:T(8,128)(2,1)S(1)} %get-tuple-element.24), channel_id=1, source_target_pairs={{0,2},{1,3},{2,0},{3,1},{4,6},{5,7},{6,4},{7,5},{8,10},{9,11},{10,... | collective-permute-start | bytes 983048 | tf_op jit(solution)/shard_map/ppermute | solution.py:324
  57.9 1.9 %collective-permute-start.6 = (bf16[1280,128]{1,0:T(8,128)(2,1)S(1)}, bf16[1280,128]{1,0:T(8,128)(2,1)S(1)}, u32[]{:S(2)}, u32[]{:S(2)}) collective-permute-start(bf16[1280,128]{1,0:T(8,128)(2,1)S(1)} %get-tuple-element.25), channel_id=1, source_target_pairs={{0,3},{1,2},{2,1},{3,0},{4,5},{5,4},{6,7},{7,6},{8,11},{9,10},{10,... | collective-permute-start | bytes 983048 | tf_op jit(solution)/shard_map/ppermute | solution.py:324
  59.8 0.2 collective-permute-done.4.pa_ref
  60.1 8.1 %collective-permute-done.5.pb_ref = bf16[1280,128]{1,0:T(8,128)(2,1)S(1)} collective-permute-done((bf16[1280,128]{1,0:T(8,128)(2,1)S(1)}, bf16[1280,128]{1,0:T(8,128)(2,1)S(1)}, u32[]{:S(2)}, u32[]{:S(2)}) %collective-permute-start.5) | collective-permute-done | bytes 327712 | tf_op jit(solution)/shard_map/ppermute | solution.py:324
  68.1 2.9 %collective-permute-done.6.pc_ref = bf16[1280,128]{1,0:T(8,128)(2,1)S(1)} collective-permute-done((bf16[1280,128]{1,0:T(8,128)(2,1)S(1)}, bf16[1280,128]{1,0:T(8,128)(2,1)S(1)}, u32[]{:S(2)}, u32[]{:S(2)}) %collective-permute-start.6) | collective-permute-done | bytes 327712 | tf_op jit(solution)/shard_map/ppermute | solution.py:324
  71.1 1.3 %all-to-all-done.1.left_ref = bf16[16,192,128]{2,1,0:T(8,128)(2,1)S(1)} async-done(((bf16[16,192,128]{2,1,0:T(8,128)(2,1)}), bf16[16,192,128]{2,1,0:T(8,128)(2,1)S(1)}, u32[]{:S(2)}, u32[]{:S(2)}) %all-to-all-start.1) | async-done | bytes 786464 | tf_op jit(solution)/shard_map/all_to_all | solution.py:245
  72.4 0.4 sort_cores.1
  72.8 2.9 %collective-permute-start.7 = (bf16[4,1024,128]{2,1,0:T(8,128)(2,1)S(1)}, bf16[4,1024,128]{2,1,0:T(8,128)(2,1)S(1)}, u32[]{:S(2)}, u32[]{:S(2)}) collective-permute-start(bf16[4,1024,128]{2,1,0:T(8,128)(2,1)S(1)} %get-tuple-element.26), channel_id=1, source_target_pairs={{0,4},{4,0},{1,5},{5,1},{2,6},{6,2},{3,7},{7,3},{8,12},{12,8},{9,1... | collective-permute-start | bytes 3145736 | tf_op jit(solution)/shard_map/ppermute | solution.py:338
  75.7 0.0 copy-done.1
  75.7 0.0 copy-done.2
  75.7 4.6 %sigma_own.1 = (bf16[4,2,2,64,256]{4,3,2,1,0:T(8,128)(2,1)S(1)}, bf16[24,256,256]{2,1,0:T(8,128)(2,1)S(1)}) custom-call(s32[128]{0:T(128)S(1)} %copy-done.1, s32[128]{0:T(128)S(1)} %copy-done.2, bf16[4,1024,128]{2,1,0:T(8,128)(2,1)S(1)} %get-tuple-element.27.refs_2_, bf16[4,768,128]{2,1,0:T(8,128)(2,1)S(1)} %get-tuple-element.28.refs_3_), custom_call_target="tpu_custom_call" | custom-call | tf_op jit(solution)/shard_map/sigma_own/pallas_call | solution.py:356
  80.3 0.0 collective-permute-done.7.got
  80.3 4.3 %sigma_other.1 = bf16[4,2,2,64,256]{4,3,2,1,0:T(8,128)(2,1)S(1)} custom-call(s32[128]{0:T(128)S(1)} %copy-done.1, s32[128]{0:T(128)S(1)} %copy-done.2, bf16[4,1024,128]{2,1,0:T(8,128)(2,1)S(1)} %collective-permute-done.7.got, bf16[24,256,256]{2,1,0:T(8,128)(2,1)S(1)} %get-tuple-element.29.refs_0_, ...), custom_call_target="tpu_custom_call", output_to_operand_aliasing={{}: (4, {})} | custom-call | tf_op jit(solution)/shard_map/sigma_other/pallas_call | solution.py:366
  84.6 10.6 %all_to_all.15.in_ref = bf16[4,2,2,64,256]{4,3,2,1,0:T(8,128)(2,1)S(1)} all-to-all(bf16[4,2,2,64,256]{4,3,2,1,0:T(8,128)(2,1)S(1)} %sigma_other.1), channel_id=1, replica_groups={{0,8,64,72},{1,9,65,73},{2,10,66,74},{3,11,67,75},{4,68,12,76},{5,69,13..., dimensions={0} | all-to-all | bytes 1048576 | tf_op jit(solution)/shard_map/all_to_all | solution.py:245
  95.3 1.1 %merge_sectors.1 = bf16[2,64,2048]{2,1,0:T(8,128)(2,1)} custom-call(bf16[4,2,2,64,256]{4,3,2,1,0:T(8,128)(2,1)S(1)} %all_to_all.15.in_ref), custom_call_target="tpu_custom_call" | custom-call | tf_op jit(solution)/shard_map/merge_sectors/pallas_call | solution.py:379
Async XLA Ops:
  2.8 72.8 %copy-start.1 = (s32[128]{0:T(128)S(1)}, s32[128]{0:T(128)}, u32[]{:S(2)}) copy-start(s32[128]{0:T(128)} %lc.1) | copy-start | bytes 1540
  2.9 72.8 %copy-start.2 = (s32[128]{0:T(128)S(1)}, s32[128]{0:T(128)}, u32[]{:S(2)}) copy-start(s32[128]{0:T(128)} %rc.1) | copy-start | bytes 1540
  2.9 34.7 %all-to-all-start = ((bf16[16,128,128]{2,1,0:T(8,128)(2,1)}), bf16[16,128,128]{2,1,0:T(8,128)(2,1)S(1)}, u32[]{:S(2)}, u32[]{:S(2)}) async-start(bf16[16,128,128]{2,1,0:T(8,128)(2,1)} %get-tuple-element.18), calls=%async_computation | async-start | bytes 1048576 | tf_op jit(solution)/shard_map/all_to_all | solution.py:245
  19.1 9.8 %collective-permute-start = (bf16[192,128]{1,0:T(8,128)(2,1)}, bf16[192,128]{1,0:T(8,128)(2,1)S(1)}, u32[]{:S(2)}, u32[]{:S(2)}) collective-permute-start(bf16[192,128]{1,0:T(8,128)(2,1)} %get-tuple-element.19), channel_id=1, source_target_pairs={{0,0},{1,128},{2,256},{3,384},{128,1},{129,129},{130,257},{131,385... | collective-permute-start | bytes 147464 | tf_op jit(solution)/shard_map/ppermute | solution.py:306
  20.6 9.6 %collective-permute-start.3 = (bf16[192,128]{1,0:T(8,128)(2,1)}, bf16[192,128]{1,0:T(8,128)(2,1)S(1)}, u32[]{:S(2)}, u32[]{:S(2)}) collective-permute-start(bf16[192,128]{1,0:T(8,128)(2,1)} %get-tuple-element.20.r0_ref), channel_id=1, source_target_pairs={{0,72},{8,64},{64,8},{72,0},{4,76},{12,68},{68,12},{76,4},{1,73},{... | collective-permute-start | bytes 147464 | tf_op jit(solution)/shard_map/ppermute | solution.py:309
  23.8 9.4 %collective-permute-start.2 = (bf16[192,128]{1,0:T(8,128)(2,1)}, bf16[192,128]{1,0:T(8,128)(2,1)S(1)}, u32[]{:S(2)}, u32[]{:S(2)}) collective-permute-start(bf16[192,128]{1,0:T(8,128)(2,1)} %get-tuple-element.20.r0_ref), channel_id=1, source_target_pairs={{0,64},{8,72},{64,0},{72,8},{4,12},{12,4},{68,76},{76,68},{1,65},{... | collective-permute-start | bytes 147464 | tf_op jit(solution)/shard_map/ppermute | solution.py:309
  26.0 7.2 %collective-permute-start.1 = (bf16[192,128]{1,0:T(8,128)(2,1)}, bf16[192,128]{1,0:T(8,128)(2,1)S(1)}, u32[]{:S(2)}, u32[]{:S(2)}) collective-permute-start(bf16[192,128]{1,0:T(8,128)(2,1)} %get-tuple-element.20.r0_ref), channel_id=1, source_target_pairs={{0,8},{8,0},{64,72},{72,64},{4,68},{12,76},{68,4},{76,12},{1,9},{9... | collective-permute-start | bytes 147464 | tf_op jit(solution)/shard_map/ppermute | solution.py:309
  37.5 0.8 copy-start
  39.5 32.9 %all-to-all-start.1 = ((bf16[16,192,128]{2,1,0:T(8,128)(2,1)}), bf16[16,192,128]{2,1,0:T(8,128)(2,1)S(1)}, u32[]{:S(2)}, u32[]{:S(2)}) async-start(bf16[16,192,128]{2,1,0:T(8,128)(2,1)} %get-tuple-element.21), calls=%async_computation.1 | async-start | bytes 1572864 | tf_op jit(solution)/shard_map/all_to_all | solution.py:245
  50.8 9.3 %collective-permute-start.4 = (bf16[1280,128]{1,0:T(8,128)(2,1)S(1)}, bf16[1280,128]{1,0:T(8,128)(2,1)S(1)}, u32[]{:S(2)}, u32[]{:S(2)}) collective-permute-start(bf16[1280,128]{1,0:T(8,128)(2,1)S(1)} %get-tuple-element.23), channel_id=1, source_target_pairs={{0,1},{1,0},{2,3},{3,2},{4,7},{5,6},{6,5},{7,4},{8,9},{9,8},{10,11... | collective-permute-start | bytes 983048 | tf_op jit(solution)/shard_map/ppermute | solution.py:324
  55.0 13.2 %collective-permute-start.5 = (bf16[1280,128]{1,0:T(8,128)(2,1)S(1)}, bf16[1280,128]{1,0:T(8,128)(2,1)S(1)}, u32[]{:S(2)}, u32[]{:S(2)}) collective-permute-start(bf16[1280,128]{1,0:T(8,128)(2,1)S(1)} %get-tuple-element.24), channel_id=1, source_target_pairs={{0,2},{1,3},{2,0},{3,1},{4,6},{5,7},{6,4},{7,5},{8,10},{9,11},{10,... | collective-permute-start | bytes 983048 | tf_op jit(solution)/shard_map/ppermute | solution.py:324
  57.9 13.2 %collective-permute-start.6 = (bf16[1280,128]{1,0:T(8,128)(2,1)S(1)}, bf16[1280,128]{1,0:T(8,128)(2,1)S(1)}, u32[]{:S(2)}, u32[]{:S(2)}) collective-permute-start(bf16[1280,128]{1,0:T(8,128)(2,1)S(1)} %get-tuple-element.25), channel_id=1, source_target_pairs={{0,3},{1,2},{2,1},{3,0},{4,5},{5,4},{6,7},{7,6},{8,11},{9,10},{10,... | collective-permute-start | bytes 983048 | tf_op jit(solution)/shard_map/ppermute | solution.py:324
  72.8 7.5 %collective-permute-start.7 = (bf16[4,1024,128]{2,1,0:T(8,128)(2,1)S(1)}, bf16[4,1024,128]{2,1,0:T(8,128)(2,1)S(1)}, u32[]{:S(2)}, u32[]{:S(2)}) collective-permute-start(bf16[4,1024,128]{2,1,0:T(8,128)(2,1)S(1)} %get-tuple-element.26), channel_id=1, source_target_pairs={{0,4},{4,0},{1,5},{5,1},{2,6},{6,2},{3,7},{7,3},{8,12},{12,8},{9,1... | collective-permute-start | bytes 3145736 | tf_op jit(solution)/shard_map/ppermute | solution.py:338

commit v9 on v8

--- a/solution.py
+++ b/solution.py
@@ -11,6 +11,7 @@
 SEC = ("yh", "yl", "zh", "zl", "core")
 FAR = ("yh", "zh")
 NEAR = ("yl", "zl")
+X_ORDER, L_ORDER, OUT_ORDER = "backwards", "both", "backwards"
 NT = (((1,), (1,)), ((), ()))
 BLOCK = 64
 WIDE = 2 * BLOCK
@@ -49,8 +50,10 @@
     return [lax.axis_index(n).astype(jnp.int32) for n in ("op",) + SEC]
 
 
-def turned(core, first, second, size=4):
-    return jnp.where(core == 0, first * size + second, second * size + first)
+def turned(core, first, second, size, order):
+    n, turn = first * size + second, second * size + first
+    last = size * size - 1
+    return jnp.where(core == 0, n, {"columns": turn, "backwards": last - n, "both": last - turn}[order])
 
 
 def prepare_kernel(
@@ -91,7 +94,7 @@
                         [first[:, lanes], second[:, lanes]], axis=1
                     )
         for zh in range(ZH):
-            copy(sent_ref.at[yh * ZH + zh], out_ref.at[turned(core, yh, zh)])
+            copy(sent_ref.at[yh * ZH + zh], out_ref.at[turned(core, yh, zh, ZH, X_ORDER)])
     for n, (c_ref, in_ref, to_ref) in enumerate(
         ((lc_ref, left_ref, lout_ref), (rc_ref, right_ref, rout_ref))
     ):
@@ -117,7 +120,7 @@
     for ref, d in zip((p0_ref, pa_ref, pb_ref, pc_ref), across(core)):
         to = jnp.bitwise_xor(plane, d)
         for z in range(ZH):
-            ref[z * wide:(z + 1) * wide, :] = got_ref[turned(core, to, z)]
+            ref[z * wide:(z + 1) * wide, :] = got_ref[turned(core, to, z, ZH, X_ORDER)]
         for right_ref, e in zip((r0_ref, ra_ref, rb_ref, rc_ref), around(core)):
             rows = pl.ds(pl.multiple_of(ZH * wide + e * RROWS, BLOCK), RROWS)
             ref[rows, :] = right_ref[...]
@@ -141,8 +144,7 @@
     for x in range(XDIM):
         for z in range(ZH):
             rows = slice(ZH * XROWS + z * RROWS, ZH * XROWS + (z + 1) * RROWS)
-            n = x * ZH + z
-            left = left_ref[jnp.where(core == 0, n, YH * ZH - 1 - n)]
+            left = left_ref[turned(core, x ^ 2, z, ZH, L_ORDER)]
             own_ref[x, rows, :] = left
             give_ref[x, rows, :] = left
 
@@ -213,7 +215,7 @@
         for v in range(vectors):
             at = v * GROUP + b * BLOCK
             block = out[at:at + BLOCK]
-            out_ref[turned(core, b // 2, b % 2, 2), 0, v] = jnp.where(allowed, block, jnp.zeros_like(block)).astype(
+            out_ref[turned(core, b // 2, b % 2, ZL, OUT_ORDER), 0, v] = jnp.where(allowed, block, jnp.zeros_like(block)).astype(
                 out_ref.dtype
             )
 
@@ -223,8 +225,8 @@
     for yl in range(YL):
         for zl in range(ZL):
             for m in range(ZH // 2):
-                low = in_ref[turned(core, yl, zl, 2), core, 0, :, m * WIDE:(m + 1) * WIDE]
-                high = in_ref[turned(core, yl, zl, 2), 1 - core, 0, :, m * WIDE:(m + 1) * WIDE]
+                low = in_ref[turned(core, yl, zl, ZL, OUT_ORDER), core, 0, :, m * WIDE:(m + 1) * WIDE]
+                high = in_ref[turned(core, yl, zl, ZL, OUT_ORDER), 1 - core, 0, :, m * WIDE:(m + 1) * WIDE]
                 for h in range(2):
                     lanes = slice(h * BLOCK, (h + 1) * BLOCK)
                     at = ((yl * ZH + 2 * m + h) * ZL + zl) * WIDE
@@ -233,14 +235,15 @@
                     )
 
 
-def exchange(array, ids, axes, backwards=False):
+def exchange(array, ids, axes, order):
     ids = np.moveaxis(ids, [SEC.index(a) for a in axes], [-2, -1])
     at = [a for a in SEC if a not in axes].index("core")
     groups = []
     for index in np.ndindex(*ids.shape[:-2]):
         group = ids[index]
         if index[at] == 1:
-            group = np.flip(group) if backwards else group.T
+            group = group if order == "backwards" else group.T
+            group = group if order == "columns" else np.flip(group)
         groups.append([int(n) for n in group.reshape(-1)])
     return lax.all_to_all(array, SEC + ("op",), 0, 0, tiled=True, axis_index_groups=groups)
 
@@ -300,9 +303,9 @@
         right_operators,
         trial_state,
     )
-    got = exchange(sent, ids, FAR)
-
-    swap = [(q * XDIM + x, x * XDIM + q) for q in range(YH) for x in range(XDIM)]
+    got = exchange(sent, ids, FAR, X_ORDER)
+
+    swap = [(q * XDIM + x, (x ^ 2) * XDIM + q) for q in range(YH) for x in range(XDIM)]
     left = lax.ppermute(left, ("yh", "op"), swap)
 
     rights = [right] + [
@@ -319,7 +322,7 @@
         compiler_params=small,
         name="spread_parts",
     )(got, left, *rights)
-    left = exchange(left, ids, FAR, backwards=True)
+    left = exchange(left, ids, FAR, L_ORDER)
     packs = packs[:1] + [
         lax.ppermute(packs[n], ("core", "op"), partners(0, [across(c)[n] for c in range(CORE)]))
         for n in (1, 2, 3)
@@ -375,7 +378,7 @@
         name="sigma_other",
     )(left_charge, right_charge, other, diagonal, partial)
 
-    partial = exchange(partial, ids, NEAR)
+    partial = exchange(partial, ids, NEAR, OUT_ORDER)
     return pl.pallas_call(
         merge_kernel,
         grid=(vectors,),

time: 97.8 us -> 97.5 us (level)
  waiting for transfers between devices: 21.1 us -> 16.9 us
  starting transfers between devices: 49.2 us -> 52.1 us
  blocking collectives: 10.6 us -> 12.6 us
    all_to_all x2, waiting for transfers between devices: 5.68 us -> 0.01 us  [exchange(): lax.all_to_all(array, SEC + ('op',), 0, 0, tiled=True, axis_index_groups=...]
    ppermute x1, starting transfers between devices: 1.46 us -> 3.92 us  [body(): left = lax.ppermute(left, ('yh', 'op'), swap)]
    all_to_all x1, blocking collectives: 10.6 us -> 12.6 us  [exchange(): lax.all_to_all(array, SEC + ('op',), 0, 0, tiled=True, axis_index_groups=...]
    ppermute x3, waiting for transfers between devices: 11.2 us -> 12.9 us  [body(): lax.ppermute(packs[n], ('core', 'op'), partners(0, [across(c)[n] for c in...]
  transfers between devices with their start and end apart: 10 -> 10, of which waited for: 7 -> 5; matrix products, arithmetic and copies ran while one was open for 0% -> 0% of each run, Pallas kernels for 5% -> 5%
where the time goes in v9:
time: 97.5 us; the launch traced here: 96.9 us
  starting transfers between devices  52.1 us (53%)
  waiting for transfers between devices  16.9 us (17%)
  Pallas kernels  14.4 us (15%)
  blocking collectives  12.6 us (13%)
    all_to_all x2, starting transfers between devices, exchange(): lax.all_to_all(array, SEC + ('op',), 0, 0, tiled=True, axis_index_groups=...  27.9 us
    ppermute x3, waiting for transfers between devices, body(): lax.ppermute(packs[n], ('core', 'op'), partners(0, [across(c)[n] for c in...  12.9 us
    all_to_all x1, blocking collectives, exchange(): lax.all_to_all(array, SEC + ('op',), 0, 0, tiled=True, axis_index_groups=...  12.6 us
    ppermute x3, starting transfers between devices, body(): lax.ppermute(packs[n], ('core', 'op'), partners(0, [across(c)[n] for c in...  9.07 us
    ppermute x3, starting transfers between devices, body(): lax.ppermute(right, NEAR + ('core',), partners(1, [around(c)[n] for c in...  8.37 us
    pallas_call x1, Pallas kernels, body(): pl.pallas_call(lambda *refs: sigma_kernel(0, *refs), grid=(1,), in_specs=...  4.61 us
    pallas_call x1, Pallas kernels, body(): pl.pallas_call(lambda lc, rc, got, *refs: sigma_kernel(1, lc, rc, got, No...  4.37 us
    ppermute x1, starting transfers between devices, body(): left = lax.ppermute(left, ('yh', 'op'), swap)  3.92 us
  transfers between devices with their start and end apart: 10, of which 5 were waited for; matrix products, arithmetic and copies ran while one was open for 0% of the time, Pallas kernels for 5%

profile of v9, /device:TPU:1, one launch (start us, length us, event | category | flops | bytes accessed | tf_op | source)
XLA Modules:
  0.0 96.9 jit_solution(3186005460957771190)
XLA Ops:
  0.0 2.8 %prepare_parts.1 = (bf16[16,128,128]{2,1,0:T(8,128)(2,1)}, bf16[192,128]{1,0:T(8,128)(2,1)}, bf16[192,128]{1,0:T(8,128)(2,1)}) custom-call(s32[1,6]{1,0:T(1,128)} %bitcast.2, s32[1,6]{1,0:T(1,128)} %bitcast.3, bf16[6,64,64]{2,1,0:T(8,128)(2,1)} %left_in.1, bf16[6,64,64]{2,1,0:T(8,128)(2,1)} %right_in.1, bf16[2,64,8192]{2,1,0:T(8,128)(2,1)} %x_ref.1), custom_call_target="tpu_custom_call" | custom-call | tf_op jit(solution)/shard_map/prepare_parts/pallas_call | solution.py:284
  2.8 0.0 copy-start.1
  2.9 0.0 copy-start.2
  2.9 16.7 %all-to-all-start = ((bf16[16,128,128]{2,1,0:T(8,128)(2,1)}), bf16[16,128,128]{2,1,0:T(8,128)(2,1)S(1)}, u32[]{:S(2)}, u32[]{:S(2)}) async-start(bf16[16,128,128]{2,1,0:T(8,128)(2,1)} %get-tuple-element.18), calls=%async_computation | async-start | bytes 1048576 | tf_op jit(solution)/shard_map/all_to_all | solution.py:248
  19.6 3.9 %collective-permute-start = (bf16[192,128]{1,0:T(8,128)(2,1)}, bf16[192,128]{1,0:T(8,128)(2,1)S(1)}, u32[]{:S(2)}, u32[]{:S(2)}) collective-permute-start(bf16[192,128]{1,0:T(8,128)(2,1)} %get-tuple-element.19), channel_id=1, source_target_pairs={{0,256},{1,384},{2,0},{3,128},{128,257},{129,385},{130,1},{131,129... | collective-permute-start | bytes 147464 | tf_op jit(solution)/shard_map/ppermute | solution.py:309
  23.5 3.6 %collective-permute-start.3 = (bf16[192,128]{1,0:T(8,128)(2,1)}, bf16[192,128]{1,0:T(8,128)(2,1)S(1)}, u32[]{:S(2)}, u32[]{:S(2)}) collective-permute-start(bf16[192,128]{1,0:T(8,128)(2,1)} %get-tuple-element.20.r0_ref), channel_id=1, source_target_pairs={{0,72},{8,64},{64,8},{72,0},{4,76},{12,68},{68,12},{76,4},{1,73},{... | collective-permute-start | bytes 147464 | tf_op jit(solution)/shard_map/ppermute | solution.py:312
  27.2 2.2 %collective-permute-start.2 = (bf16[192,128]{1,0:T(8,128)(2,1)}, bf16[192,128]{1,0:T(8,128)(2,1)S(1)}, u32[]{:S(2)}, u32[]{:S(2)}) collective-permute-start(bf16[192,128]{1,0:T(8,128)(2,1)} %get-tuple-element.20.r0_ref), channel_id=1, source_target_pairs={{0,64},{8,72},{64,0},{72,8},{4,12},{12,4},{68,76},{76,68},{1,65},{... | collective-permute-start | bytes 147464 | tf_op jit(solution)/shard_map/ppermute | solution.py:312
  29.4 2.6 %collective-permute-start.1 = (bf16[192,128]{1,0:T(8,128)(2,1)}, bf16[192,128]{1,0:T(8,128)(2,1)S(1)}, u32[]{:S(2)}, u32[]{:S(2)}) collective-permute-start(bf16[192,128]{1,0:T(8,128)(2,1)} %get-tuple-element.20.r0_ref), channel_id=1, source_target_pairs={{0,8},{8,0},{64,72},{72,64},{4,68},{12,76},{68,4},{76,12},{1,9},{9... | collective-permute-start | bytes 147464 | tf_op jit(solution)/shard_map/ppermute | solution.py:312
  31.9 0.3 collective-permute-done.left_ref
  32.3 3.7 %collective-permute-done.3.rc_ref = bf16[192,128]{1,0:T(8,128)(2,1)S(1)} collective-permute-done((bf16[192,128]{1,0:T(8,128)(2,1)}, bf16[192,128]{1,0:T(8,128)(2,1)S(1)}, u32[]{:S(2)}, u32[]{:S(2)}) %collective-permute-start.3) | collective-permute-done | bytes 49184 | tf_op jit(solution)/shard_map/ppermute | solution.py:312
  35.9 0.0 collective-permute-done.2.rb_ref
  35.9 0.0 collective-permute-done.1.ra_ref
  35.9 0.0 all-to-all-done.got_ref
  35.9 0.0 copy-start
  35.9 0.8 copy-done
  36.7 1.1 %spread_parts.1 = (bf16[1280,128]{1,0:T(8,128)(2,1)S(1)}, bf16[1280,128]{1,0:T(8,128)(2,1)S(1)}, bf16[1280,128]{1,0:T(8,128)(2,1)S(1)}, bf16[1280,128]{1,0:T(8,128)(2,1)S(1)}, bf16[16,192,128]{2,1,0:T(8,128)(2,1)}) custom-call(bf16[16,128,128]{2,1,0:T(8,128)(2,1)S(1)} %all-to-all-done.got_ref, bf16[192,128]{1,0:T(8,128)(2,1)S(1)} %collective-permute-done.left_ref, ...), custom_call_target="tpu_custom_call" | custom-call | tf_op jit(solution)/shard_map/spread_parts/pallas_call | solution.py:317
  37.9 11.1 %all-to-all-start.1 = ((bf16[16,192,128]{2,1,0:T(8,128)(2,1)}), bf16[16,192,128]{2,1,0:T(8,128)(2,1)S(1)}, u32[]{:S(2)}, u32[]{:S(2)}) async-start(bf16[16,192,128]{2,1,0:T(8,128)(2,1)} %get-tuple-element.21), calls=%async_computation.1 | async-start | bytes 1572864 | tf_op jit(solution)/shard_map/all_to_all | solution.py:248
  49.0 3.6 %collective-permute-start.4 = (bf16[1280,128]{1,0:T(8,128)(2,1)S(1)}, bf16[1280,128]{1,0:T(8,128)(2,1)S(1)}, u32[]{:S(2)}, u32[]{:S(2)}) collective-permute-start(bf16[1280,128]{1,0:T(8,128)(2,1)S(1)} %get-tuple-element.23), channel_id=1, source_target_pairs={{0,1},{1,0},{2,3},{3,2},{4,7},{5,6},{6,5},{7,4},{8,9},{9,8},{10,11... | collective-permute-start | bytes 983048 | tf_op jit(solution)/shard_map/ppermute | solution.py:327
  52.6 3.6 %collective-permute-start.5 = (bf16[1280,128]{1,0:T(8,128)(2,1)S(1)}, bf16[1280,128]{1,0:T(8,128)(2,1)S(1)}, u32[]{:S(2)}, u32[]{:S(2)}) collective-permute-start(bf16[1280,128]{1,0:T(8,128)(2,1)S(1)} %get-tuple-element.24), channel_id=1, source_target_pairs={{0,2},{1,3},{2,0},{3,1},{4,6},{5,7},{6,4},{7,5},{8,10},{9,11},{10,... | collective-permute-start | bytes 983048 | tf_op jit(solution)/shard_map/ppermute | solution.py:327
  56.1 1.9 %collective-permute-start.6 = (bf16[1280,128]{1,0:T(8,128)(2,1)S(1)}, bf16[1280,128]{1,0:T(8,128)(2,1)S(1)}, u32[]{:S(2)}, u32[]{:S(2)}) collective-permute-start(bf16[1280,128]{1,0:T(8,128)(2,1)S(1)} %get-tuple-element.25), channel_id=1, source_target_pairs={{0,3},{1,2},{2,1},{3,0},{4,5},{5,4},{6,7},{7,6},{8,11},{9,10},{10,... | collective-permute-start | bytes 983048 | tf_op jit(solution)/shard_map/ppermute | solution.py:327
  58.1 0.1 collective-permute-done.4.pa_ref
  58.1 7.7 %collective-permute-done.5.pb_ref = bf16[1280,128]{1,0:T(8,128)(2,1)S(1)} collective-permute-done((bf16[1280,128]{1,0:T(8,128)(2,1)S(1)}, bf16[1280,128]{1,0:T(8,128)(2,1)S(1)}, u32[]{:S(2)}, u32[]{:S(2)}) %collective-permute-start.5) | collective-permute-done | bytes 327712 | tf_op jit(solution)/shard_map/ppermute | solution.py:327
  65.8 5.2 %collective-permute-done.6.pc_ref = bf16[1280,128]{1,0:T(8,128)(2,1)S(1)} collective-permute-done((bf16[1280,128]{1,0:T(8,128)(2,1)S(1)}, bf16[1280,128]{1,0:T(8,128)(2,1)S(1)}, u32[]{:S(2)}, u32[]{:S(2)}) %collective-permute-start.6) | collective-permute-done | bytes 327712 | tf_op jit(solution)/shard_map/ppermute | solution.py:327
  71.0 0.0 all-to-all-done.1.left_ref
  71.0 0.4 sort_cores.1
  71.4 2.8 %collective-permute-start.7 = (bf16[4,1024,128]{2,1,0:T(8,128)(2,1)S(1)}, bf16[4,1024,128]{2,1,0:T(8,128)(2,1)S(1)}, u32[]{:S(2)}, u32[]{:S(2)}) collective-permute-start(bf16[4,1024,128]{2,1,0:T(8,128)(2,1)S(1)} %get-tuple-element.26), channel_id=1, source_target_pairs={{0,4},{4,0},{1,5},{5,1},{2,6},{6,2},{3,7},{7,3},{8,12},{12,8},{9,1... | collective-permute-start | bytes 3145736 | tf_op jit(solution)/shard_map/ppermute | solution.py:341
  74.3 0.0 copy-done.1
  74.3 0.0 copy-done.2
  74.3 4.6 %sigma_own.1 = (bf16[4,2,2,64,256]{4,3,2,1,0:T(8,128)(2,1)S(1)}, bf16[24,256,256]{2,1,0:T(8,128)(2,1)S(1)}) custom-call(s32[128]{0:T(128)S(1)} %copy-done.1, s32[128]{0:T(128)S(1)} %copy-done.2, bf16[4,1024,128]{2,1,0:T(8,128)(2,1)S(1)} %get-tuple-element.27.refs_2_, bf16[4,768,128]{2,1,0:T(8,128)(2,1)S(1)} %get-tuple-element.28.refs_3_), custom_call_target="tpu_custom_call" | custom-call | tf_op jit(solution)/shard_map/sigma_own/pallas_call | solution.py:359
  78.9 0.0 collective-permute-done.7.got
  78.9 4.4 %sigma_other.1 = bf16[4,2,2,64,256]{4,3,2,1,0:T(8,128)(2,1)S(1)} custom-call(s32[128]{0:T(128)S(1)} %copy-done.1, s32[128]{0:T(128)S(1)} %copy-done.2, bf16[4,1024,128]{2,1,0:T(8,128)(2,1)S(1)} %collective-permute-done.7.got, bf16[24,256,256]{2,1,0:T(8,128)(2,1)S(1)} %get-tuple-element.29.refs_0_, ...), custom_call_target="tpu_custom_call", output_to_operand_aliasing={{}: (4, {})} | custom-call | tf_op jit(solution)/shard_map/sigma_other/pallas_call | solution.py:369
  83.3 12.6 %all_to_all.15.in_ref = bf16[4,2,2,64,256]{4,3,2,1,0:T(8,128)(2,1)S(1)} all-to-all(bf16[4,2,2,64,256]{4,3,2,1,0:T(8,128)(2,1)S(1)} %sigma_other.1), channel_id=1, replica_groups={{0,8,64,72},{1,9,65,73},{2,10,66,74},{3,11,67,75},{76,68,12,4},{77,69,1..., dimensions={0} | all-to-all | bytes 1048576 | tf_op jit(solution)/shard_map/all_to_all | solution.py:248
  95.9 1.1 %merge_sectors.1 = bf16[2,64,2048]{2,1,0:T(8,128)(2,1)} custom-call(bf16[4,2,2,64,256]{4,3,2,1,0:T(8,128)(2,1)S(1)} %all_to_all.15.in_ref), custom_call_target="tpu_custom_call" | custom-call | tf_op jit(solution)/shard_map/merge_sectors/pallas_call | solution.py:382
Async XLA Ops:
  2.8 71.4 %copy-start.1 = (s32[128]{0:T(128)S(1)}, s32[128]{0:T(128)}, u32[]{:S(2)}) copy-start(s32[128]{0:T(128)} %lc.1) | copy-start | bytes 1540
  2.9 71.4 %copy-start.2 = (s32[128]{0:T(128)S(1)}, s32[128]{0:T(128)}, u32[]{:S(2)}) copy-start(s32[128]{0:T(128)} %rc.1) | copy-start | bytes 1540
  2.9 33.1 %all-to-all-start = ((bf16[16,128,128]{2,1,0:T(8,128)(2,1)}), bf16[16,128,128]{2,1,0:T(8,128)(2,1)S(1)}, u32[]{:S(2)}, u32[]{:S(2)}) async-start(bf16[16,128,128]{2,1,0:T(8,128)(2,1)} %get-tuple-element.18), calls=%async_computation | async-start | bytes 1048576 | tf_op jit(solution)/shard_map/all_to_all | solution.py:248
  19.6 12.7 %collective-permute-start = (bf16[192,128]{1,0:T(8,128)(2,1)}, bf16[192,128]{1,0:T(8,128)(2,1)S(1)}, u32[]{:S(2)}, u32[]{:S(2)}) collective-permute-start(bf16[192,128]{1,0:T(8,128)(2,1)} %get-tuple-element.19), channel_id=1, source_target_pairs={{0,256},{1,384},{2,0},{3,128},{128,257},{129,385},{130,1},{131,129... | collective-permute-start | bytes 147464 | tf_op jit(solution)/shard_map/ppermute | solution.py:309
  23.5 12.4 %collective-permute-start.3 = (bf16[192,128]{1,0:T(8,128)(2,1)}, bf16[192,128]{1,0:T(8,128)(2,1)S(1)}, u32[]{:S(2)}, u32[]{:S(2)}) collective-permute-start(bf16[192,128]{1,0:T(8,128)(2,1)} %get-tuple-element.20.r0_ref), channel_id=1, source_target_pairs={{0,72},{8,64},{64,8},{72,0},{4,76},{12,68},{68,12},{76,4},{1,73},{... | collective-permute-start | bytes 147464 | tf_op jit(solution)/shard_map/ppermute | solution.py:312
  27.2 8.8 %collective-permute-start.2 = (bf16[192,128]{1,0:T(8,128)(2,1)}, bf16[192,128]{1,0:T(8,128)(2,1)S(1)}, u32[]{:S(2)}, u32[]{:S(2)}) collective-permute-start(bf16[192,128]{1,0:T(8,128)(2,1)} %get-tuple-element.20.r0_ref), channel_id=1, source_target_pairs={{0,64},{8,72},{64,0},{72,8},{4,12},{12,4},{68,76},{76,68},{1,65},{... | collective-permute-start | bytes 147464 | tf_op jit(solution)/shard_map/ppermute | solution.py:312
  29.4 6.6 %collective-permute-start.1 = (bf16[192,128]{1,0:T(8,128)(2,1)}, bf16[192,128]{1,0:T(8,128)(2,1)S(1)}, u32[]{:S(2)}, u32[]{:S(2)}) collective-permute-start(bf16[192,128]{1,0:T(8,128)(2,1)} %get-tuple-element.20.r0_ref), channel_id=1, source_target_pairs={{0,8},{8,0},{64,72},{72,64},{4,68},{12,76},{68,4},{76,12},{1,9},{9... | collective-permute-start | bytes 147464 | tf_op jit(solution)/shard_map/ppermute | solution.py:312
  35.9 0.8 copy-start
  37.9 33.2 %all-to-all-start.1 = ((bf16[16,192,128]{2,1,0:T(8,128)(2,1)}), bf16[16,192,128]{2,1,0:T(8,128)(2,1)S(1)}, u32[]{:S(2)}, u32[]{:S(2)}) async-start(bf16[16,192,128]{2,1,0:T(8,128)(2,1)} %get-tuple-element.21), calls=%async_computation.1 | async-start | bytes 1572864 | tf_op jit(solution)/shard_map/all_to_all | solution.py:248
  49.0 9.2 %collective-permute-start.4 = (bf16[1280,128]{1,0:T(8,128)(2,1)S(1)}, bf16[1280,128]{1,0:T(8,128)(2,1)S(1)}, u32[]{:S(2)}, u32[]{:S(2)}) collective-permute-start(bf16[1280,128]{1,0:T(8,128)(2,1)S(1)} %get-tuple-element.23), channel_id=1, source_target_pairs={{0,1},{1,0},{2,3},{3,2},{4,7},{5,6},{6,5},{7,4},{8,9},{9,8},{10,11... | collective-permute-start | bytes 983048 | tf_op jit(solution)/shard_map/ppermute | solution.py:327
  52.6 13.2 %collective-permute-start.5 = (bf16[1280,128]{1,0:T(8,128)(2,1)S(1)}, bf16[1280,128]{1,0:T(8,128)(2,1)S(1)}, u32[]{:S(2)}, u32[]{:S(2)}) collective-permute-start(bf16[1280,128]{1,0:T(8,128)(2,1)S(1)} %get-tuple-element.24), channel_id=1, source_target_pairs={{0,2},{1,3},{2,0},{3,1},{4,6},{5,7},{6,4},{7,5},{8,10},{9,11},{10,... | collective-permute-start | bytes 983048 | tf_op jit(solution)/shard_map/ppermute | solution.py:327
  56.1 14.9 %collective-permute-start.6 = (bf16[1280,128]{1,0:T(8,128)(2,1)S(1)}, bf16[1280,128]{1,0:T(8,128)(2,1)S(1)}, u32[]{:S(2)}, u32[]{:S(2)}) collective-permute-start(bf16[1280,128]{1,0:T(8,128)(2,1)S(1)} %get-tuple-element.25), channel_id=1, source_target_pairs={{0,3},{1,2},{2,1},{3,0},{4,5},{5,4},{6,7},{7,6},{8,11},{9,10},{10,... | collective-permute-start | bytes 983048 | tf_op jit(solution)/shard_map/ppermute | solution.py:327
  71.4 7.5 %collective-permute-start.7 = (bf16[4,1024,128]{2,1,0:T(8,128)(2,1)S(1)}, bf16[4,1024,128]{2,1,0:T(8,128)(2,1)S(1)}, u32[]{:S(2)}, u32[]{:S(2)}) collective-permute-start(bf16[4,1024,128]{2,1,0:T(8,128)(2,1)S(1)} %get-tuple-element.26), channel_id=1, source_target_pairs={{0,4},{4,0},{1,5},{5,1},{2,6},{6,2},{3,7},{7,3},{8,12},{12,8},{9,1... | collective-permute-start | bytes 3145736 | tf_op jit(solution)/shard_map/ppermute | solution.py:341

commit v10 on v9

--- a/solution.py
+++ b/solution.py
@@ -111,6 +111,12 @@
         done.wait()
 
 
+def stage_kernel(left_ref, right_ref, sent_ref, own_ref):
+    for to in range(YH * ZH):
+        sent_ref[to] = left_ref[...]
+    own_ref[...] = right_ref[...]
+
+
 def spread_kernel(
     got_ref, left_ref, r0_ref, ra_ref, rb_ref, rc_ref, p0_ref, pa_ref, pb_ref, pc_ref, sent_ref
 ):
@@ -124,8 +130,6 @@
         for right_ref, e in zip((r0_ref, ra_ref, rb_ref, rc_ref), around(core)):
             rows = pl.ds(pl.multiple_of(ZH * wide + e * RROWS, BLOCK), RROWS)
             ref[rows, :] = right_ref[...]
-    for to in range(YH * ZH):
-        sent_ref[to] = left_ref[...]
 
 
 def core_kernel(left_ref, p0_ref, pa_ref, pb_ref, pc_ref, own_ref, give_ref, near_ref):
@@ -313,12 +317,23 @@
         for n in (1, 2, 3)
     ]
 
+    copies = jax.ShapeDtypeStruct((YH * ZH, RROWS, WIDE), jnp.bfloat16)
+    left, rights[0] = pl.pallas_call(
+        stage_kernel,
+        in_specs=[vmem] * 2,
+        out_specs=[vmem] * 2,
+        out_shape=[copies, operator],
+        compiler_params=small,
+        name="stage_parts",
+    )(left, right)
+
     pack = jax.ShapeDtypeStruct((ZH * wide + YL * ZL * RROWS, WIDE), jnp.bfloat16)
     *packs, left = pl.pallas_call(
         spread_kernel,
-        in_specs=[vmem] * 6,
-        out_specs=[vmem] * 5,
-        out_shape=[pack] * XDIM + [jax.ShapeDtypeStruct((YH * ZH, RROWS, WIDE), jnp.bfloat16)],
+        in_specs=[vmem, anywhere] + [vmem] * 4,
+        out_specs=[vmem] * 4 + [anywhere],
+        out_shape=[pack] * XDIM + [copies],
+        input_output_aliases={1: XDIM},
         compiler_params=small,
         name="spread_parts",
     )(got, left, *rights)

time: 97.5 us -> 98.4 us (level)
  waiting for transfers between devices: 16.9 us -> 13.5 us
  starting transfers between devices: 52.1 us -> 55.1 us
  blocking collectives: 12.6 us -> 13.8 us
    all_to_all x2, starting transfers between devices: 27.9 us -> 29.7 us  [exchange(): lax.all_to_all(array, SEC + ('op',), 0, 0, tiled=True, axis_index_groups=...]
    ppermute x3, waiting for transfers between devices: 3.66 us -> 1.87 us  [body(): lax.ppermute(right, NEAR + ('core',), partners(1, [around(c)[n] for c in...]
    ppermute x3, waiting for transfers between devices: 12.9 us -> 11.3 us  [body(): lax.ppermute(packs[n], ('core', 'op'), partners(0, [across(c)[n] for c in...]
    ppermute x1, starting transfers between devices: 2.83 us -> 4.2 us  [body(): other = lax.ppermute(give, 'core', [(0, 1), (1, 0)])]
    all_to_all x1, blocking collectives: 12.6 us -> 13.8 us  [exchange(): lax.all_to_all(array, SEC + ('op',), 0, 0, tiled=True, axis_index_groups=...]
  transfers between devices with their start and end apart: 10 -> 10, of which waited for: 5 -> 5; matrix products, arithmetic and copies ran while one was open for 0% -> 0% of each run, Pallas kernels for 5% -> 6%
where the time goes in v10:
time: 98.4 us; the launch traced here: 97.8 us
  starting transfers between devices  55.1 us (56%)
  Pallas kernels  14.4 us (15%)
  blocking collectives  13.8 us (14%)
  waiting for transfers between devices  13.5 us (14%)
    all_to_all x2, starting transfers between devices, exchange(): lax.all_to_all(array, SEC + ('op',), 0, 0, tiled=True, axis_index_groups=...  29.7 us
    all_to_all x1, blocking collectives, exchange(): lax.all_to_all(array, SEC + ('op',), 0, 0, tiled=True, axis_index_groups=...  13.8 us
    ppermute x3, waiting for transfers between devices, body(): lax.ppermute(packs[n], ('core', 'op'), partners(0, [across(c)[n] for c in...  11.3 us
    ppermute x3, starting transfers between devices, body(): lax.ppermute(packs[n], ('core', 'op'), partners(0, [across(c)[n] for c in...  8.97 us
    ppermute x3, starting transfers between devices, body(): lax.ppermute(right, NEAR + ('core',), partners(1, [around(c)[n] for c in...  8.37 us
    pallas_call x1, Pallas kernels, body(): pl.pallas_call(lambda *refs: sigma_kernel(0, *refs), grid=(1,), in_specs=...  4.6 us
    pallas_call x1, Pallas kernels, body(): pl.pallas_call(lambda lc, rc, got, *refs: sigma_kernel(1, lc, rc, got, No...  4.37 us
    ppermute x1, starting transfers between devices, body(): other = lax.ppermute(give, 'core', [(0, 1), (1, 0)])  4.2 us
  transfers between devices with their start and end apart: 10, of which 5 were waited for; matrix products, arithmetic and copies ran while one was open for 0% of the time, Pallas kernels for 6%

profile of v10, /device:TPU:1, one launch (start us, length us, event | category | flops | bytes accessed | tf_op | source)
XLA Modules:
  0.0 97.8 jit_solution(2366912951763714781)
XLA Ops:
  0.0 2.8 %prepare_parts.1 = (bf16[16,128,128]{2,1,0:T(8,128)(2,1)}, bf16[192,128]{1,0:T(8,128)(2,1)}, bf16[192,128]{1,0:T(8,128)(2,1)}) custom-call(s32[1,6]{1,0:T(1,128)} %bitcast.2, s32[1,6]{1,0:T(1,128)} %bitcast.3, bf16[6,64,64]{2,1,0:T(8,128)(2,1)} %left_in.1, bf16[6,64,64]{2,1,0:T(8,128)(2,1)} %right_in.1, bf16[2,64,8192]{2,1,0:T(8,128)(2,1)} %x_ref.1), custom_call_target="tpu_custom_call" | custom-call | tf_op jit(solution)/shard_map/prepare_parts/pallas_call | solution.py:288
  2.8 0.0 copy-start.1
  2.9 0.0 copy-start.2
  2.9 16.7 %all-to-all-start = ((bf16[16,128,128]{2,1,0:T(8,128)(2,1)}), bf16[16,128,128]{2,1,0:T(8,128)(2,1)S(1)}, u32[]{:S(2)}, u32[]{:S(2)}) async-start(bf16[16,128,128]{2,1,0:T(8,128)(2,1)} %get-tuple-element.20), calls=%async_computation | async-start | bytes 1048576 | tf_op jit(solution)/shard_map/all_to_all | solution.py:252
  19.6 3.9 %collective-permute-start = (bf16[192,128]{1,0:T(8,128)(2,1)}, bf16[192,128]{1,0:T(8,128)(2,1)S(1)}, u32[]{:S(2)}, u32[]{:S(2)}) collective-permute-start(bf16[192,128]{1,0:T(8,128)(2,1)} %get-tuple-element.21), channel_id=1, source_target_pairs={{0,256},{1,384},{2,0},{3,128},{128,257},{129,385},{130,1},{131,129... | collective-permute-start | bytes 147464 | tf_op jit(solution)/shard_map/ppermute | solution.py:313
  23.5 3.6 %collective-permute-start.3 = (bf16[192,128]{1,0:T(8,128)(2,1)}, bf16[192,128]{1,0:T(8,128)(2,1)S(1)}, u32[]{:S(2)}, u32[]{:S(2)}) collective-permute-start(bf16[192,128]{1,0:T(8,128)(2,1)} %get-tuple-element.22.right_ref), channel_id=1, source_target_pairs={{0,72},{8,64},{64,8},{72,0},{4,76},{12,68},{68,12},{76,4},{1,73},{... | collective-permute-start | bytes 147464 | tf_op jit(solution)/shard_map/ppermute | solution.py:316
  27.2 2.2 %collective-permute-start.2 = (bf16[192,128]{1,0:T(8,128)(2,1)}, bf16[192,128]{1,0:T(8,128)(2,1)S(1)}, u32[]{:S(2)}, u32[]{:S(2)}) collective-permute-start(bf16[192,128]{1,0:T(8,128)(2,1)} %get-tuple-element.22.right_ref), channel_id=1, source_target_pairs={{0,64},{8,72},{64,0},{72,8},{4,12},{12,4},{68,76},{76,68},{1,65},{... | collective-permute-start | bytes 147464 | tf_op jit(solution)/shard_map/ppermute | solution.py:316
  29.4 2.6 %collective-permute-start.1 = (bf16[192,128]{1,0:T(8,128)(2,1)}, bf16[192,128]{1,0:T(8,128)(2,1)S(1)}, u32[]{:S(2)}, u32[]{:S(2)}) collective-permute-start(bf16[192,128]{1,0:T(8,128)(2,1)} %get-tuple-element.22.right_ref), channel_id=1, source_target_pairs={{0,8},{8,0},{64,72},{72,64},{4,68},{12,76},{68,4},{76,12},{1,9},{9... | collective-permute-start | bytes 147464 | tf_op jit(solution)/shard_map/ppermute | solution.py:316
  31.9 0.3 collective-permute-done.left_ref
  32.3 0.0 copy-start
  32.3 0.8 copy-done
  33.1 1.0 %stage_parts.1 = (bf16[16,192,128]{2,1,0:T(8,128)(2,1)}, bf16[192,128]{1,0:T(8,128)(2,1)S(1)}) custom-call(bf16[192,128]{1,0:T(8,128)(2,1)S(1)} %collective-permute-done.left_ref, bf16[192,128]{1,0:T(8,128)(2,1)S(1)} %copy-done), custom_call_target="tpu_custom_call" | custom-call | tf_op jit(solution)/shard_map/stage_parts/pallas_call | solution.py:321
  34.1 1.9 %collective-permute-done.3.rc_ref = bf16[192,128]{1,0:T(8,128)(2,1)S(1)} collective-permute-done((bf16[192,128]{1,0:T(8,128)(2,1)}, bf16[192,128]{1,0:T(8,128)(2,1)S(1)}, u32[]{:S(2)}, u32[]{:S(2)}) %collective-permute-start.3) | collective-permute-done | bytes 49184 | tf_op jit(solution)/shard_map/ppermute | solution.py:316
  35.9 0.0 collective-permute-done.2.rb_ref
  35.9 0.0 collective-permute-done.1.ra_ref
  35.9 0.0 all-to-all-done.got_ref
  35.9 0.1 spread_parts.1
  36.1 12.9 %all-to-all-start.1 = ((bf16[16,192,128]{2,1,0:T(8,128)(2,1)}), bf16[16,192,128]{2,1,0:T(8,128)(2,1)S(1)}, u32[]{:S(2)}, u32[]{:S(2)}) async-start(bf16[16,192,128]{2,1,0:T(8,128)(2,1)} %get-tuple-element.25), calls=%async_computation.1 | async-start | bytes 1572864 | tf_op jit(solution)/shard_map/all_to_all | solution.py:252
  49.0 1.9 %collective-permute-start.4 = (bf16[1280,128]{1,0:T(8,128)(2,1)S(1)}, bf16[1280,128]{1,0:T(8,128)(2,1)S(1)}, u32[]{:S(2)}, u32[]{:S(2)}) collective-permute-start(bf16[1280,128]{1,0:T(8,128)(2,1)S(1)} %get-tuple-element.27), channel_id=1, source_target_pairs={{0,1},{1,0},{2,3},{3,2},{4,7},{5,6},{6,5},{7,4},{8,9},{9,8},{10,11... | collective-permute-start | bytes 983048 | tf_op jit(solution)/shard_map/ppermute | solution.py:342
  50.9 4.9 %collective-permute-start.5 = (bf16[1280,128]{1,0:T(8,128)(2,1)S(1)}, bf16[1280,128]{1,0:T(8,128)(2,1)S(1)}, u32[]{:S(2)}, u32[]{:S(2)}) collective-permute-start(bf16[1280,128]{1,0:T(8,128)(2,1)S(1)} %get-tuple-element.28), channel_id=1, source_target_pairs={{0,2},{1,3},{2,0},{3,1},{4,6},{5,7},{6,4},{7,5},{8,10},{9,11},{10,... | collective-permute-start | bytes 983048 | tf_op jit(solution)/shard_map/ppermute | solution.py:342
  55.8 2.2 %collective-permute-start.6 = (bf16[1280,128]{1,0:T(8,128)(2,1)S(1)}, bf16[1280,128]{1,0:T(8,128)(2,1)S(1)}, u32[]{:S(2)}, u32[]{:S(2)}) collective-permute-start(bf16[1280,128]{1,0:T(8,128)(2,1)S(1)} %get-tuple-element.29), channel_id=1, source_target_pairs={{0,3},{1,2},{2,1},{3,0},{4,5},{5,4},{6,7},{7,6},{8,11},{9,10},{10,... | collective-permute-start | bytes 983048 | tf_op jit(solution)/shard_map/ppermute | solution.py:342
  58.0 1.5 %collective-permute-done.4.pa_ref = bf16[1280,128]{1,0:T(8,128)(2,1)S(1)} collective-permute-done((bf16[1280,128]{1,0:T(8,128)(2,1)S(1)}, bf16[1280,128]{1,0:T(8,128)(2,1)S(1)}, u32[]{:S(2)}, u32[]{:S(2)}) %collective-permute-start.4) | collective-permute-done | bytes 327712 | tf_op jit(solution)/shard_map/ppermute | solution.py:342
  59.6 4.6 %collective-permute-done.5.pb_ref = bf16[1280,128]{1,0:T(8,128)(2,1)S(1)} collective-permute-done((bf16[1280,128]{1,0:T(8,128)(2,1)S(1)}, bf16[1280,128]{1,0:T(8,128)(2,1)S(1)}, u32[]{:S(2)}, u32[]{:S(2)}) %collective-permute-start.5) | collective-permute-done | bytes 327712 | tf_op jit(solution)/shard_map/ppermute | solution.py:342
  64.2 5.1 %collective-permute-done.6.pc_ref = bf16[1280,128]{1,0:T(8,128)(2,1)S(1)} collective-permute-done((bf16[1280,128]{1,0:T(8,128)(2,1)S(1)}, bf16[1280,128]{1,0:T(8,128)(2,1)S(1)}, u32[]{:S(2)}, u32[]{:S(2)}) %collective-permute-start.6) | collective-permute-done | bytes 327712 | tf_op jit(solution)/shard_map/ppermute | solution.py:342
  69.3 0.0 all-to-all-done.1.left_ref
  69.3 0.4 sort_cores.1
  69.7 4.2 %collective-permute-start.7 = (bf16[4,1024,128]{2,1,0:T(8,128)(2,1)S(1)}, bf16[4,1024,128]{2,1,0:T(8,128)(2,1)S(1)}, u32[]{:S(2)}, u32[]{:S(2)}) collective-permute-start(bf16[4,1024,128]{2,1,0:T(8,128)(2,1)S(1)} %get-tuple-element.30), channel_id=1, source_target_pairs={{0,4},{4,0},{1,5},{5,1},{2,6},{6,2},{3,7},{7,3},{8,12},{12,8},{9,1... | collective-permute-start | bytes 3145736 | tf_op jit(solution)/shard_map/ppermute | solution.py:356
  73.9 0.0 copy-done.1
  73.9 0.0 copy-done.2
  73.9 4.6 %sigma_own.1 = (bf16[4,2,2,64,256]{4,3,2,1,0:T(8,128)(2,1)S(1)}, bf16[24,256,256]{2,1,0:T(8,128)(2,1)S(1)}) custom-call(s32[128]{0:T(128)S(1)} %copy-done.1, s32[128]{0:T(128)S(1)} %copy-done.2, bf16[4,1024,128]{2,1,0:T(8,128)(2,1)S(1)} %get-tuple-element.31.refs_2_, bf16[4,768,128]{2,1,0:T(8,128)(2,1)S(1)} %get-tuple-element.32.refs_3_), custom_call_target="tpu_custom_call" | custom-call | tf_op jit(solution)/shard_map/sigma_own/pallas_call | solution.py:374
  78.5 0.0 collective-permute-done.7.got
  78.5 4.4 %sigma_other.1 = bf16[4,2,2,64,256]{4,3,2,1,0:T(8,128)(2,1)S(1)} custom-call(s32[128]{0:T(128)S(1)} %copy-done.1, s32[128]{0:T(128)S(1)} %copy-done.2, bf16[4,1024,128]{2,1,0:T(8,128)(2,1)S(1)} %collective-permute-done.7.got, bf16[24,256,256]{2,1,0:T(8,128)(2,1)S(1)} %get-tuple-element.33.refs_0_, ...), custom_call_target="tpu_custom_call", output_to_operand_aliasing={{}: (4, {})} | custom-call | tf_op jit(solution)/shard_map/sigma_other/pallas_call | solution.py:384
  82.9 13.8 %all_to_all.15.in_ref = bf16[4,2,2,64,256]{4,3,2,1,0:T(8,128)(2,1)S(1)} all-to-all(bf16[4,2,2,64,256]{4,3,2,1,0:T(8,128)(2,1)S(1)} %sigma_other.1), channel_id=1, replica_groups={{0,8,64,72},{1,9,65,73},{2,10,66,74},{3,11,67,75},{76,68,12,4},{77,69,1..., dimensions={0} | all-to-all | bytes 1048576 | tf_op jit(solution)/shard_map/all_to_all | solution.py:252
  96.7 1.1 %merge_sectors.1 = bf16[2,64,2048]{2,1,0:T(8,128)(2,1)} custom-call(bf16[4,2,2,64,256]{4,3,2,1,0:T(8,128)(2,1)S(1)} %all_to_all.15.in_ref), custom_call_target="tpu_custom_call" | custom-call | tf_op jit(solution)/shard_map/merge_sectors/pallas_call | solution.py:397
Async XLA Ops:
  2.8 71.1 %copy-start.1 = (s32[128]{0:T(128)S(1)}, s32[128]{0:T(128)}, u32[]{:S(2)}) copy-start(s32[128]{0:T(128)} %lc.1) | copy-start | bytes 1540
  2.9 71.1 %copy-start.2 = (s32[128]{0:T(128)S(1)}, s32[128]{0:T(128)}, u32[]{:S(2)}) copy-start(s32[128]{0:T(128)} %rc.1) | copy-start | bytes 1540
  2.9 33.1 %all-to-all-start = ((bf16[16,128,128]{2,1,0:T(8,128)(2,1)}), bf16[16,128,128]{2,1,0:T(8,128)(2,1)S(1)}, u32[]{:S(2)}, u32[]{:S(2)}) async-start(bf16[16,128,128]{2,1,0:T(8,128)(2,1)} %get-tuple-element.20), calls=%async_computation | async-start | bytes 1048576 | tf_op jit(solution)/shard_map/all_to_all | solution.py:252
  19.6 12.7 %collective-permute-start = (bf16[192,128]{1,0:T(8,128)(2,1)}, bf16[192,128]{1,0:T(8,128)(2,1)S(1)}, u32[]{:S(2)}, u32[]{:S(2)}) collective-permute-start(bf16[192,128]{1,0:T(8,128)(2,1)} %get-tuple-element.21), channel_id=1, source_target_pairs={{0,256},{1,384},{2,0},{3,128},{128,257},{129,385},{130,1},{131,129... | collective-permute-start | bytes 147464 | tf_op jit(solution)/shard_map/ppermute | solution.py:313
  23.5 12.4 %collective-permute-start.3 = (bf16[192,128]{1,0:T(8,128)(2,1)}, bf16[192,128]{1,0:T(8,128)(2,1)S(1)}, u32[]{:S(2)}, u32[]{:S(2)}) collective-permute-start(bf16[192,128]{1,0:T(8,128)(2,1)} %get-tuple-element.22.right_ref), channel_id=1, source_target_pairs={{0,72},{8,64},{64,8},{72,0},{4,76},{12,68},{68,12},{76,4},{1,73},{... | collective-permute-start | bytes 147464 | tf_op jit(solution)/shard_map/ppermute | solution.py:316
  27.2 8.8 %collective-permute-start.2 = (bf16[192,128]{1,0:T(8,128)(2,1)}, bf16[192,128]{1,0:T(8,128)(2,1)S(1)}, u32[]{:S(2)}, u32[]{:S(2)}) collective-permute-start(bf16[192,128]{1,0:T(8,128)(2,1)} %get-tuple-element.22.right_ref), channel_id=1, source_target_pairs={{0,64},{8,72},{64,0},{72,8},{4,12},{12,4},{68,76},{76,68},{1,65},{... | collective-permute-start | bytes 147464 | tf_op jit(solution)/shard_map/ppermute | solution.py:316
  29.4 6.6 %collective-permute-start.1 = (bf16[192,128]{1,0:T(8,128)(2,1)}, bf16[192,128]{1,0:T(8,128)(2,1)S(1)}, u32[]{:S(2)}, u32[]{:S(2)}) collective-permute-start(bf16[192,128]{1,0:T(8,128)(2,1)} %get-tuple-element.22.right_ref), channel_id=1, source_target_pairs={{0,8},{8,0},{64,72},{72,64},{4,68},{12,76},{68,4},{76,12},{1,9},{9... | collective-permute-start | bytes 147464 | tf_op jit(solution)/shard_map/ppermute | solution.py:316
  32.3 0.8 copy-start
  36.1 33.2 %all-to-all-start.1 = ((bf16[16,192,128]{2,1,0:T(8,128)(2,1)}), bf16[16,192,128]{2,1,0:T(8,128)(2,1)S(1)}, u32[]{:S(2)}, u32[]{:S(2)}) async-start(bf16[16,192,128]{2,1,0:T(8,128)(2,1)} %get-tuple-element.25), calls=%async_computation.1 | async-start | bytes 1572864 | tf_op jit(solution)/shard_map/all_to_all | solution.py:252
  49.0 10.5 %collective-permute-start.4 = (bf16[1280,128]{1,0:T(8,128)(2,1)S(1)}, bf16[1280,128]{1,0:T(8,128)(2,1)S(1)}, u32[]{:S(2)}, u32[]{:S(2)}) collective-permute-start(bf16[1280,128]{1,0:T(8,128)(2,1)S(1)} %get-tuple-element.27), channel_id=1, source_target_pairs={{0,1},{1,0},{2,3},{3,2},{4,7},{5,6},{6,5},{7,4},{8,9},{9,8},{10,11... | collective-permute-start | bytes 983048 | tf_op jit(solution)/shard_map/ppermute | solution.py:342
  50.9 13.2 %collective-permute-start.5 = (bf16[1280,128]{1,0:T(8,128)(2,1)S(1)}, bf16[1280,128]{1,0:T(8,128)(2,1)S(1)}, u32[]{:S(2)}, u32[]{:S(2)}) collective-permute-start(bf16[1280,128]{1,0:T(8,128)(2,1)S(1)} %get-tuple-element.28), channel_id=1, source_target_pairs={{0,2},{1,3},{2,0},{3,1},{4,6},{5,7},{6,4},{7,5},{8,10},{9,11},{10,... | collective-permute-start | bytes 983048 | tf_op jit(solution)/shard_map/ppermute | solution.py:342
  55.8 13.5 %collective-permute-start.6 = (bf16[1280,128]{1,0:T(8,128)(2,1)S(1)}, bf16[1280,128]{1,0:T(8,128)(2,1)S(1)}, u32[]{:S(2)}, u32[]{:S(2)}) collective-permute-start(bf16[1280,128]{1,0:T(8,128)(2,1)S(1)} %get-tuple-element.29), channel_id=1, source_target_pairs={{0,3},{1,2},{2,1},{3,0},{4,5},{5,4},{6,7},{7,6},{8,11},{9,10},{10,... | collective-permute-start | bytes 983048 | tf_op jit(solution)/shard_map/ppermute | solution.py:342
  69.7 8.8 %collective-permute-start.7 = (bf16[4,1024,128]{2,1,0:T(8,128)(2,1)S(1)}, bf16[4,1024,128]{2,1,0:T(8,128)(2,1)S(1)}, u32[]{:S(2)}, u32[]{:S(2)}) collective-permute-start(bf16[4,1024,128]{2,1,0:T(8,128)(2,1)S(1)} %get-tuple-element.30), channel_id=1, source_target_pairs={{0,4},{4,0},{1,5},{5,1},{2,6},{6,2},{3,7},{7,3},{8,12},{12,8},{9,1... | collective-permute-start | bytes 3145736 | tf_op jit(solution)/shard_map/ppermute | solution.py:356

commit v11 on v9

--- a/solution.py
+++ b/solution.py
@@ -39,7 +39,7 @@
 
 
 def across(core):
-    return 0, 1 + 2 * core, 2, 3 - 2 * core
+    return 0, 1 + core, 2 + core, 3 - 2 * core
 
 
 def around(core):

time: 97.5 us -> 97.6 us (level)
  waiting for transfers between devices: 16.9 us -> 14.2 us
  starting transfers between devices: 52.1 us -> 54.8 us
    ppermute x3, waiting for transfers between devices: 12.9 us -> 10.2 us  [body(): lax.ppermute(packs[n], ('core', 'op'), partners(0, [across(c)[n] for c in...]
    ppermute x1, starting transfers between devices: 2.83 us -> 5.3 us  [body(): other = lax.ppermute(give, 'core', [(0, 1), (1, 0)])]
where the time goes in v11:
time: 97.6 us; the launch traced here: 97 us
  starting transfers between devices  54.8 us (56%)
  Pallas kernels  14.4 us (15%)
  waiting for transfers between devices  14.2 us (15%)
  blocking collectives  12.6 us (13%)
    all_to_all x2, starting transfers between devices, exchange(): lax.all_to_all(array, SEC + ('op',), 0, 0, tiled=True, axis_index_groups=...  27.9 us
    all_to_all x1, blocking collectives, exchange(): lax.all_to_all(array, SEC + ('op',), 0, 0, tiled=True, axis_index_groups=...  12.6 us
    ppermute x3, waiting for transfers between devices, body(): lax.ppermute(packs[n], ('core', 'op'), partners(0, [across(c)[n] for c in...  10.2 us
    ppermute x3, starting transfers between devices, body(): lax.ppermute(packs[n], ('core', 'op'), partners(0, [across(c)[n] for c in...  9.29 us
    ppermute x3, starting transfers between devices, body(): lax.ppermute(right, NEAR + ('core',), partners(1, [around(c)[n] for c in...  8.37 us
    ppermute x1, starting transfers between devices, body(): other = lax.ppermute(give, 'core', [(0, 1), (1, 0)])  5.3 us
    pallas_call x1, Pallas kernels, body(): pl.pallas_call(lambda *refs: sigma_kernel(0, *refs), grid=(1,), in_specs=...  4.6 us
    pallas_call x1, Pallas kernels, body(): pl.pallas_call(lambda lc, rc, got, *refs: sigma_kernel(1, lc, rc, got, No...  4.37 us
  transfers between devices with their start and end apart: 10, of which 5 were waited for; matrix products, arithmetic and copies ran while one was open for 0% of the time, Pallas kernels for 5%

profile of v11, /device:TPU:1, one launch (start us, length us, event | category | flops | bytes accessed | tf_op | source)
XLA Modules:
  0.0 97.0 jit_solution(18342593743902146870)
XLA Ops:
  0.0 2.8 %prepare_parts.1 = (bf16[16,128,128]{2,1,0:T(8,128)(2,1)}, bf16[192,128]{1,0:T(8,128)(2,1)}, bf16[192,128]{1,0:T(8,128)(2,1)}) custom-call(s32[1,6]{1,0:T(1,128)} %bitcast.2, s32[1,6]{1,0:T(1,128)} %bitcast.3, bf16[6,64,64]{2,1,0:T(8,128)(2,1)} %left_in.1, bf16[6,64,64]{2,1,0:T(8,128)(2,1)} %right_in.1, bf16[2,64,8192]{2,1,0:T(8,128)(2,1)} %x_ref.1), custom_call_target="tpu_custom_call" | custom-call | tf_op jit(solution)/shard_map/prepare_parts/pallas_call | solution.py:284
  2.8 0.0 copy-start.1
  2.9 0.0 copy-start.2
  2.9 16.7 %all-to-all-start = ((bf16[16,128,128]{2,1,0:T(8,128)(2,1)}), bf16[16,128,128]{2,1,0:T(8,128)(2,1)S(1)}, u32[]{:S(2)}, u32[]{:S(2)}) async-start(bf16[16,128,128]{2,1,0:T(8,128)(2,1)} %get-tuple-element.18), calls=%async_computation | async-start | bytes 1048576 | tf_op jit(solution)/shard_map/all_to_all | solution.py:248
  19.6 3.9 %collective-permute-start = (bf16[192,128]{1,0:T(8,128)(2,1)}, bf16[192,128]{1,0:T(8,128)(2,1)S(1)}, u32[]{:S(2)}, u32[]{:S(2)}) collective-permute-start(bf16[192,128]{1,0:T(8,128)(2,1)} %get-tuple-element.19), channel_id=1, source_target_pairs={{0,256},{1,384},{2,0},{3,128},{128,257},{129,385},{130,1},{131,129... | collective-permute-start | bytes 147464 | tf_op jit(solution)/shard_map/ppermute | solution.py:309
  23.5 3.6 %collective-permute-start.3 = (bf16[192,128]{1,0:T(8,128)(2,1)}, bf16[192,128]{1,0:T(8,128)(2,1)S(1)}, u32[]{:S(2)}, u32[]{:S(2)}) collective-permute-start(bf16[192,128]{1,0:T(8,128)(2,1)} %get-tuple-element.20.r0_ref), channel_id=1, source_target_pairs={{0,72},{8,64},{64,8},{72,0},{4,76},{12,68},{68,12},{76,4},{1,73},{... | collective-permute-start | bytes 147464 | tf_op jit(solution)/shard_map/ppermute | solution.py:312
  27.2 2.2 %collective-permute-start.2 = (bf16[192,128]{1,0:T(8,128)(2,1)}, bf16[192,128]{1,0:T(8,128)(2,1)S(1)}, u32[]{:S(2)}, u32[]{:S(2)}) collective-permute-start(bf16[192,128]{1,0:T(8,128)(2,1)} %get-tuple-element.20.r0_ref), channel_id=1, source_target_pairs={{0,64},{8,72},{64,0},{72,8},{4,12},{12,4},{68,76},{76,68},{1,65},{... | collective-permute-start | bytes 147464 | tf_op jit(solution)/shard_map/ppermute | solution.py:312
  29.4 2.6 %collective-permute-start.1 = (bf16[192,128]{1,0:T(8,128)(2,1)}, bf16[192,128]{1,0:T(8,128)(2,1)S(1)}, u32[]{:S(2)}, u32[]{:S(2)}) collective-permute-start(bf16[192,128]{1,0:T(8,128)(2,1)} %get-tuple-element.20.r0_ref), channel_id=1, source_target_pairs={{0,8},{8,0},{64,72},{72,64},{4,68},{12,76},{68,4},{76,12},{1,9},{9... | collective-permute-start | bytes 147464 | tf_op jit(solution)/shard_map/ppermute | solution.py:312
  31.9 0.3 collective-permute-done.left_ref
  32.3 3.7 %collective-permute-done.3.rc_ref = bf16[192,128]{1,0:T(8,128)(2,1)S(1)} collective-permute-done((bf16[192,128]{1,0:T(8,128)(2,1)}, bf16[192,128]{1,0:T(8,128)(2,1)S(1)}, u32[]{:S(2)}, u32[]{:S(2)}) %collective-permute-start.3) | collective-permute-done | bytes 49184 | tf_op jit(solution)/shard_map/ppermute | solution.py:312
  35.9 0.0 collective-permute-done.2.rb_ref
  35.9 0.0 collective-permute-done.1.ra_ref
  35.9 0.0 all-to-all-done.got_ref
  35.9 0.0 copy-start
  35.9 0.8 copy-done
  36.7 1.1 %spread_parts.1 = (bf16[1280,128]{1,0:T(8,128)(2,1)S(1)}, bf16[1280,128]{1,0:T(8,128)(2,1)S(1)}, bf16[1280,128]{1,0:T(8,128)(2,1)S(1)}, bf16[1280,128]{1,0:T(8,128)(2,1)S(1)}, bf16[16,192,128]{2,1,0:T(8,128)(2,1)}) custom-call(bf16[16,128,128]{2,1,0:T(8,128)(2,1)S(1)} %all-to-all-done.got_ref, bf16[192,128]{1,0:T(8,128)(2,1)S(1)} %collective-permute-done.left_ref, ...), custom_call_target="tpu_custom_call" | custom-call | tf_op jit(solution)/shard_map/spread_parts/pallas_call | solution.py:317
  37.9 11.1 %all-to-all-start.1 = ((bf16[16,192,128]{2,1,0:T(8,128)(2,1)}), bf16[16,192,128]{2,1,0:T(8,128)(2,1)S(1)}, u32[]{:S(2)}, u32[]{:S(2)}) async-start(bf16[16,192,128]{2,1,0:T(8,128)(2,1)} %get-tuple-element.21), calls=%async_computation.1 | async-start | bytes 1572864 | tf_op jit(solution)/shard_map/all_to_all | solution.py:248
  49.0 5.2 %collective-permute-start.4 = (bf16[1280,128]{1,0:T(8,128)(2,1)S(1)}, bf16[1280,128]{1,0:T(8,128)(2,1)S(1)}, u32[]{:S(2)}, u32[]{:S(2)}) collective-permute-start(bf16[1280,128]{1,0:T(8,128)(2,1)S(1)} %get-tuple-element.23), channel_id=1, source_target_pairs={{0,1},{1,0},{2,3},{3,2},{4,6},{5,7},{6,4},{7,5},{8,9},{9,8},{10,11... | collective-permute-start | bytes 983048 | tf_op jit(solution)/shard_map/ppermute | solution.py:327
  54.2 2.1 %collective-permute-start.5 = (bf16[1280,128]{1,0:T(8,128)(2,1)S(1)}, bf16[1280,128]{1,0:T(8,128)(2,1)S(1)}, u32[]{:S(2)}, u32[]{:S(2)}) collective-permute-start(bf16[1280,128]{1,0:T(8,128)(2,1)S(1)} %get-tuple-element.24), channel_id=1, source_target_pairs={{0,2},{1,3},{2,0},{3,1},{4,7},{5,6},{6,5},{7,4},{8,10},{9,11},{10,... | collective-permute-start | bytes 983048 | tf_op jit(solution)/shard_map/ppermute | solution.py:327
  56.4 1.9 %collective-permute-start.6 = (bf16[1280,128]{1,0:T(8,128)(2,1)S(1)}, bf16[1280,128]{1,0:T(8,128)(2,1)S(1)}, u32[]{:S(2)}, u32[]{:S(2)}) collective-permute-start(bf16[1280,128]{1,0:T(8,128)(2,1)S(1)} %get-tuple-element.25), channel_id=1, source_target_pairs={{0,3},{1,2},{2,1},{3,0},{4,5},{5,4},{6,7},{7,6},{8,11},{9,10},{10,... | collective-permute-start | bytes 983048 | tf_op jit(solution)/shard_map/ppermute | solution.py:327
  58.3 3.4 %collective-permute-done.4.pa_ref = bf16[1280,128]{1,0:T(8,128)(2,1)S(1)} collective-permute-done((bf16[1280,128]{1,0:T(8,128)(2,1)S(1)}, bf16[1280,128]{1,0:T(8,128)(2,1)S(1)}, u32[]{:S(2)}, u32[]{:S(2)}) %collective-permute-start.4) | collective-permute-done | bytes 327712 | tf_op jit(solution)/shard_map/ppermute | solution.py:327
  61.7 6.5 %collective-permute-done.5.pb_ref = bf16[1280,128]{1,0:T(8,128)(2,1)S(1)} collective-permute-done((bf16[1280,128]{1,0:T(8,128)(2,1)S(1)}, bf16[1280,128]{1,0:T(8,128)(2,1)S(1)}, u32[]{:S(2)}, u32[]{:S(2)}) %collective-permute-start.5) | collective-permute-done | bytes 327712 | tf_op jit(solution)/shard_map/ppermute | solution.py:327
  68.2 0.4 collective-permute-done.6.pc_ref
  68.6 0.0 all-to-all-done.1.left_ref
  68.6 0.4 sort_cores.1
  69.0 5.3 %collective-permute-start.7 = (bf16[4,1024,128]{2,1,0:T(8,128)(2,1)S(1)}, bf16[4,1024,128]{2,1,0:T(8,128)(2,1)S(1)}, u32[]{:S(2)}, u32[]{:S(2)}) collective-permute-start(bf16[4,1024,128]{2,1,0:T(8,128)(2,1)S(1)} %get-tuple-element.26), channel_id=1, source_target_pairs={{0,4},{4,0},{1,5},{5,1},{2,6},{6,2},{3,7},{7,3},{8,12},{12,8},{9,1... | collective-permute-start | bytes 3145736 | tf_op jit(solution)/shard_map/ppermute | solution.py:341
  74.3 0.0 copy-done.1
  74.3 0.0 copy-done.2
  74.3 4.6 %sigma_own.1 = (bf16[4,2,2,64,256]{4,3,2,1,0:T(8,128)(2,1)S(1)}, bf16[24,256,256]{2,1,0:T(8,128)(2,1)S(1)}) custom-call(s32[128]{0:T(128)S(1)} %copy-done.1, s32[128]{0:T(128)S(1)} %copy-done.2, bf16[4,1024,128]{2,1,0:T(8,128)(2,1)S(1)} %get-tuple-element.27.refs_2_, bf16[4,768,128]{2,1,0:T(8,128)(2,1)S(1)} %get-tuple-element.28.refs_3_), custom_call_target="tpu_custom_call" | custom-call | tf_op jit(solution)/shard_map/sigma_own/pallas_call | solution.py:359
  78.9 0.0 collective-permute-done.7.got
  78.9 4.4 %sigma_other.1 = bf16[4,2,2,64,256]{4,3,2,1,0:T(8,128)(2,1)S(1)} custom-call(s32[128]{0:T(128)S(1)} %copy-done.1, s32[128]{0:T(128)S(1)} %copy-done.2, bf16[4,1024,128]{2,1,0:T(8,128)(2,1)S(1)} %collective-permute-done.7.got, bf16[24,256,256]{2,1,0:T(8,128)(2,1)S(1)} %get-tuple-element.29.refs_0_, ...), custom_call_target="tpu_custom_call", output_to_operand_aliasing={{}: (4, {})} | custom-call | tf_op jit(solution)/shard_map/sigma_other/pallas_call | solution.py:369
  83.3 12.6 %all_to_all.15.in_ref = bf16[4,2,2,64,256]{4,3,2,1,0:T(8,128)(2,1)S(1)} all-to-all(bf16[4,2,2,64,256]{4,3,2,1,0:T(8,128)(2,1)S(1)} %sigma_other.1), channel_id=1, replica_groups={{0,8,64,72},{1,9,65,73},{2,10,66,74},{3,11,67,75},{76,68,12,4},{77,69,1..., dimensions={0} | all-to-all | bytes 1048576 | tf_op jit(solution)/shard_map/all_to_all | solution.py:248
  95.9 1.1 %merge_sectors.1 = bf16[2,64,2048]{2,1,0:T(8,128)(2,1)} custom-call(bf16[4,2,2,64,256]{4,3,2,1,0:T(8,128)(2,1)S(1)} %all_to_all.15.in_ref), custom_call_target="tpu_custom_call" | custom-call | tf_op jit(solution)/shard_map/merge_sectors/pallas_call | solution.py:382
Async XLA Ops:
  2.8 71.4 %copy-start.1 = (s32[128]{0:T(128)S(1)}, s32[128]{0:T(128)}, u32[]{:S(2)}) copy-start(s32[128]{0:T(128)} %lc.1) | copy-start | bytes 1540
  2.9 71.4 %copy-start.2 = (s32[128]{0:T(128)S(1)}, s32[128]{0:T(128)}, u32[]{:S(2)}) copy-start(s32[128]{0:T(128)} %rc.1) | copy-start | bytes 1540
  2.9 33.1 %all-to-all-start = ((bf16[16,128,128]{2,1,0:T(8,128)(2,1)}), bf16[16,128,128]{2,1,0:T(8,128)(2,1)S(1)}, u32[]{:S(2)}, u32[]{:S(2)}) async-start(bf16[16,128,128]{2,1,0:T(8,128)(2,1)} %get-tuple-element.18), calls=%async_computation | async-start | bytes 1048576 | tf_op jit(solution)/shard_map/all_to_all | solution.py:248
  19.6 12.7 %collective-permute-start = (bf16[192,128]{1,0:T(8,128)(2,1)}, bf16[192,128]{1,0:T(8,128)(2,1)S(1)}, u32[]{:S(2)}, u32[]{:S(2)}) collective-permute-start(bf16[192,128]{1,0:T(8,128)(2,1)} %get-tuple-element.19), channel_id=1, source_target_pairs={{0,256},{1,384},{2,0},{3,128},{128,257},{129,385},{130,1},{131,129... | collective-permute-start | bytes 147464 | tf_op jit(solution)/shard_map/ppermute | solution.py:309
  23.5 12.4 %collective-permute-start.3 = (bf16[192,128]{1,0:T(8,128)(2,1)}, bf16[192,128]{1,0:T(8,128)(2,1)S(1)}, u32[]{:S(2)}, u32[]{:S(2)}) collective-permute-start(bf16[192,128]{1,0:T(8,128)(2,1)} %get-tuple-element.20.r0_ref), channel_id=1, source_target_pairs={{0,72},{8,64},{64,8},{72,0},{4,76},{12,68},{68,12},{76,4},{1,73},{... | collective-permute-start | bytes 147464 | tf_op jit(solution)/shard_map/ppermute | solution.py:312
  27.2 8.8 %collective-permute-start.2 = (bf16[192,128]{1,0:T(8,128)(2,1)}, bf16[192,128]{1,0:T(8,128)(2,1)S(1)}, u32[]{:S(2)}, u32[]{:S(2)}) collective-permute-start(bf16[192,128]{1,0:T(8,128)(2,1)} %get-tuple-element.20.r0_ref), channel_id=1, source_target_pairs={{0,64},{8,72},{64,0},{72,8},{4,12},{12,4},{68,76},{76,68},{1,65},{... | collective-permute-start | bytes 147464 | tf_op jit(solution)/shard_map/ppermute | solution.py:312
  29.4 6.6 %collective-permute-start.1 = (bf16[192,128]{1,0:T(8,128)(2,1)}, bf16[192,128]{1,0:T(8,128)(2,1)S(1)}, u32[]{:S(2)}, u32[]{:S(2)}) collective-permute-start(bf16[192,128]{1,0:T(8,128)(2,1)} %get-tuple-element.20.r0_ref), channel_id=1, source_target_pairs={{0,8},{8,0},{64,72},{72,64},{4,68},{12,76},{68,4},{76,12},{1,9},{9... | collective-permute-start | bytes 147464 | tf_op jit(solution)/shard_map/ppermute | solution.py:312
  35.9 0.8 copy-start
  37.9 30.7 %all-to-all-start.1 = ((bf16[16,192,128]{2,1,0:T(8,128)(2,1)}), bf16[16,192,128]{2,1,0:T(8,128)(2,1)S(1)}, u32[]{:S(2)}, u32[]{:S(2)}) async-start(bf16[16,192,128]{2,1,0:T(8,128)(2,1)} %get-tuple-element.21), calls=%async_computation.1 | async-start | bytes 1572864 | tf_op jit(solution)/shard_map/all_to_all | solution.py:248
  49.0 12.7 %collective-permute-start.4 = (bf16[1280,128]{1,0:T(8,128)(2,1)S(1)}, bf16[1280,128]{1,0:T(8,128)(2,1)S(1)}, u32[]{:S(2)}, u32[]{:S(2)}) collective-permute-start(bf16[1280,128]{1,0:T(8,128)(2,1)S(1)} %get-tuple-element.23), channel_id=1, source_target_pairs={{0,1},{1,0},{2,3},{3,2},{4,6},{5,7},{6,4},{7,5},{8,9},{9,8},{10,11... | collective-permute-start | bytes 983048 | tf_op jit(solution)/shard_map/ppermute | solution.py:327
  54.2 14.0 %collective-permute-start.5 = (bf16[1280,128]{1,0:T(8,128)(2,1)S(1)}, bf16[1280,128]{1,0:T(8,128)(2,1)S(1)}, u32[]{:S(2)}, u32[]{:S(2)}) collective-permute-start(bf16[1280,128]{1,0:T(8,128)(2,1)S(1)} %get-tuple-element.24), channel_id=1, source_target_pairs={{0,2},{1,3},{2,0},{3,1},{4,7},{5,6},{6,5},{7,4},{8,10},{9,11},{10,... | collective-permute-start | bytes 983048 | tf_op jit(solution)/shard_map/ppermute | solution.py:327
  56.4 12.2 %collective-permute-start.6 = (bf16[1280,128]{1,0:T(8,128)(2,1)S(1)}, bf16[1280,128]{1,0:T(8,128)(2,1)S(1)}, u32[]{:S(2)}, u32[]{:S(2)}) collective-permute-start(bf16[1280,128]{1,0:T(8,128)(2,1)S(1)} %get-tuple-element.25), channel_id=1, source_target_pairs={{0,3},{1,2},{2,1},{3,0},{4,5},{5,4},{6,7},{7,6},{8,11},{9,10},{10,... | collective-permute-start | bytes 983048 | tf_op jit(solution)/shard_map/ppermute | solution.py:327
  69.0 9.9 %collective-permute-start.7 = (bf16[4,1024,128]{2,1,0:T(8,128)(2,1)S(1)}, bf16[4,1024,128]{2,1,0:T(8,128)(2,1)S(1)}, u32[]{:S(2)}, u32[]{:S(2)}) collective-permute-start(bf16[4,1024,128]{2,1,0:T(8,128)(2,1)S(1)} %get-tuple-element.26), channel_id=1, source_target_pairs={{0,4},{4,0},{1,5},{5,1},{2,6},{6,2},{3,7},{7,3},{8,12},{12,8},{9,1... | collective-permute-start | bytes 3145736 | tf_op jit(solution)/shard_map/ppermute | solution.py:341
